TPU v7x, 32 devices: a whole 2x2x4 slice. The times are simulated.
32 devices in a mesh: parts: 2 (over y), az: 16 (over z, x, core).
Axes of the slice: x: 2, y: 2, z: 4, core: 2. Of those that a mesh axis runs over, the one named last changes fastest.
Arguments:
- fields: bfloat16 [256, 64, 128], P(('parts', 'az')), parts along dimension 0, may hold values from -6 to 6
- cotangent: bfloat16 [256, 64, 128], P(('parts', 'az')), parts along dimension 0, may hold values from -21 to 21
- azimuth_filter: float32 [9, 64], replicated, may hold values from -2 to 2
- radial_filter: float32 [7, 64], replicated, may hold values from -2 to 2
- mixing: bfloat16 [64, 64], replicated, may hold values from -0.75 to 0.75
- tap_offsets: int32 [9], replicated, may hold values from -48 to 48, as said below
Outputs:
- output_field: bfloat16 [256, 64, 128], P(('parts', 'az')), parts along dimension 0
- input_grad: bfloat16 [256, 64, 128], P(('parts', 'az')), parts along dimension 0
- azimuth_grad: float32 [18, 64], P('parts'), parts along dimension 0
- radial_grad: float32 [14, 64], P('parts'), parts along dimension 0
- mixing_grad: float32 [128, 64], P('parts'), parts along dimension 0
There are 2 independent parts, one for each index of `parts`. A program takes and returns all parts, laid end to end along the dimension named above; an argument that names none is the same for every part. Nothing has to cross between parts.
Inputs may be any that keep to these rules, and one draw needn't show every extreme that they name: `tap_offsets`: offsets are distinct and rise with the tap; the first is the most negative and the last the most positive.
All inputs are finite; a program needn't handle non-finite values.
Results may differ from a plain program's by a relative error of at most 0.008.
Values may be sent and summed in bfloat16 or wider, within the bound.
No kernel may reach another device: no remote copies, remote signals or barrier semaphores. Data moves between devices by JAX's collectives and lax.ppermute only.
A program may use at most 64 MiB of HBM per device.

v0:
```python
import math

import jax
import jax.numpy as jnp
from jax import lax
from jax.sharding import PartitionSpec as P


def extended(x, sides, width):
    for axis, dim in sides:
        peers, length = (lax.axis_size(axis), x.shape[dim])
        up = [(i, (i + 1) % peers) for i in range(peers - 1)]
        down = [(j, i) for i, j in up]
        last = lax.slice_in_dim(x, length - width, length, axis=dim)
        leading = lax.slice_in_dim(x, 0, width, axis=dim)
        before = lax.ppermute(last, axis, up)
        after = lax.ppermute(leading, axis, down)
        x = jnp.concatenate([before, x, after], axis=dim)
    return x


def apply_mix(values, matrix):
    flat = values.reshape(-1, values.shape[2])
    return jnp.dot(flat, matrix, preferred_element_type=jnp.float32).reshape(values.shape)


def mix_product(hidden, grads):
    width = hidden.shape[2]
    return lax.dot_general(
        hidden.reshape(-1, width),
        grads.reshape(-1, width),
        (((0,), (0,)), ((), ())),
        preferred_element_type=jnp.float32,
    )


def azim_taps(values, azim_wide, tap_offsets):
    total = jnp.zeros(values.shape, jnp.float32)
    for tap in range(tap_offsets.shape[0]):
        total = total + azim_wide[tap] * jnp.roll(values, -tap_offsets[tap], axis=0)
    return total


def local(fields, cotangent, azimuth_filter, radial_filter, mixing, tap_offsets):
    taps = tap_offsets.shape[0]
    rtaps = radial_filter.shape[0]
    channels = mixing.shape[0]
    feat = fields.shape[2]
    axial = feat // channels
    wide_mix = jnp.kron(jnp.eye(axial, dtype=jnp.bfloat16), mixing)
    wide_back = jnp.kron(jnp.eye(axial, dtype=jnp.bfloat16), mixing.T)
    azim_wide = jnp.tile(azimuth_filter, (1, axial))
    radial_wide = jnp.tile(radial_filter, (1, axial))
    moved_field, moved_cot = (
        lax.all_to_all(fields, "az", split_axis=1, concat_axis=0, tiled=True),
        lax.all_to_all(cotangent, "az", split_axis=1, concat_axis=0, tiled=True),
    )
    radii = moved_field.shape[1]
    field_float = moved_field.astype(jnp.float32)
    azim_sum = azim_taps(field_float, azim_wide, tap_offsets)
    azim_padded = extended(azim_sum, (("az", 1),), 3)
    radial_sum = jnp.zeros(moved_field.shape, jnp.float32)
    for tap in range(rtaps):
        radial_sum = radial_sum + radial_wide[tap] * azim_padded[:, tap : tap + radii]
    hidden = radial_sum.astype(jnp.bfloat16)
    output_moved = (field_float + apply_mix(hidden, wide_mix)).astype(jnp.bfloat16)
    grad_hidden = apply_mix(moved_cot, wide_back).astype(jnp.bfloat16)
    mix_full = mix_product(hidden, moved_cot)
    grad_padded = extended(grad_hidden, (("az", 1),), 3)
    grad_float = grad_hidden.astype(jnp.float32)
    grad_azim = jnp.zeros(moved_field.shape, jnp.float32)
    radial_terms = []
    for tap in range(rtaps):
        grad_azim = grad_azim + radial_wide[tap] * grad_padded[:, 6 - tap : 6 - tap + radii].astype(
            jnp.float32
        )
        radial_terms.append(jnp.sum(azim_padded[:, tap : tap + radii] * grad_float, axis=(0, 1)))
    branch = jnp.zeros(moved_field.shape, jnp.float32)
    azim_terms = []
    for tap in range(taps):
        shifted = jnp.roll(field_float, -tap_offsets[tap], axis=0)
        azim_terms.append(jnp.sum(shifted * grad_azim, axis=(0, 1)))
        branch = branch + azim_wide[tap] * jnp.roll(grad_azim, tap_offsets[tap], axis=0)
    branch_grad = branch.astype(jnp.bfloat16)
    input_moved = (moved_cot.astype(jnp.float32) + branch_grad.astype(jnp.float32)).astype(
        jnp.bfloat16
    )
    output_field, input_grad = (
        lax.all_to_all(output_moved, "az", split_axis=0, concat_axis=1, tiled=True),
        lax.all_to_all(input_moved, "az", split_axis=0, concat_axis=1, tiled=True),
    )
    azim_fold = jnp.sum(jnp.stack(azim_terms).reshape(taps, axial, channels), axis=1)
    radial_fold = jnp.sum(jnp.stack(radial_terms).reshape(rtaps, axial, channels), axis=1)
    mix_fold = jnp.einsum("zczd->cd", mix_full.reshape(axial, channels, axial, channels))
    cells = moved_field.shape[0] * radii * lax.axis_size("az") * axial
    scale = 1.0 / math.sqrt(cells)
    azimuth_grad, radial_grad, mixing_grad = lax.psum(
        (scale * azim_fold, scale * radial_fold, scale * mix_fold), "az"
    )
    return (output_field, input_grad, azimuth_grad, radial_grad, mixing_grad)


def solution(mesh):
    in_specs = (P(("parts", "az"), None, None), P(("parts", "az"), None, None), P(), P(), P(), P())
    out_specs = (
        P(("parts", "az"), None, None),
        P(("parts", "az"), None, None),
        P("parts", None),
        P("parts", None),
        P("parts", None),
    )
    return jax.shard_map(local, mesh=mesh, in_specs=in_specs, out_specs=out_specs, check_vma=False)
```

profile of v0, /device:TPU:0, one launch (start us, length us, event | category | flops | bytes accessed | tf_op | source)
XLA Modules:
  0.0 140.7 jit_solution(2120247580672372273)
XLA Ops:
  0.6 1.6 %copy.87 = bf16[8,64,128]{2,0,1:T(8,128)(2,1)} copy(bf16[8,64,128]{2,1,0:T(8,128)(2,1)} %param.9) | data formatting | bytes 262144 | tf_op args[1]
  2.3 7.5 %all-to-all-start.2 = ((bf16[8,64,128]{2,0,1:T(8,128)(2,1)}), bf16[8,64,128]{2,0,1:T(8,128)(2,1)S(1)}, u32[]{:S(2)}, u32[]{:S(2)}) async-start(bf16[8,64,128]{2,0,1:T(8,128)(2,1)} %copy.87), calls=%async_computation.2 | async-start | bytes 262144 | tf_op jit(solution)/shard_map/all_to_all | solution.py:56
  9.9 0.7 fusion.58
  15.6 0.1 copy.89
  15.7 0.7 copy.83
  16.5 0.2 broadcast_multiply_fusion
  16.7 1.1 all-to-all-done.2
  17.7 5.0 %all-to-all-start = ((bf16[8,64,128]{2,0,1:T(8,128)(2,1)}), bf16[8,64,128]{2,0,1:T(8,128)(2,1)S(1)}, u32[]{:S(2)}, u32[]{:S(2)}) async-start(bf16[8,64,128]{2,0,1:T(8,128)(2,1)} %copy.83), calls=%async_computation | async-start | bytes 262144 | tf_op jit(solution)/shard_map/all_to_all | solution.py:55
  40.7 0.1 tile.75
  40.8 0.1 tile.101
  40.9 0.1 tile.99
  41.0 0.1 tile.97
  41.0 0.1 tile.95
  41.1 0.1 tile.105
  41.2 0.1 tile.103
  41.3 0.1 tile.77
  41.4 0.1 tile.89
  41.5 0.1 tile.87
  41.6 0.1 tile.85
  41.6 0.1 tile.83
  41.7 0.1 tile.81
  41.8 0.1 tile.79
  41.9 0.1 tile.93
  42.0 0.1 tile.91
  42.1 0.1 mul.377
  42.2 0.1 reshape.189
  42.5 0.2 fusion.1
  42.7 0.1 copy.91
  42.8 0.1 copy.101
  43.0 0.1 fusion.57
  43.2 2.3 %collective-permute-start.3 = (bf16[128,3,128]{2,0,1:T(8,128)(2,1)S(1)}, bf16[128,3,128]{2,0,1:T(8,128)(2,1)S(1)}, u32[]{:S(2)}, u32[]{:S(2)}) collective-permute-start(bf16[128,3,128]{2,0,1:T(8,128)(2,1)S(1)} %copy.117), channel_id=1, source_target_pairs={{0,1},{1,2},{2,3},{3,4},{4,5},{5,6},{6,7},{7,8},{8,9},{9,10},{10,1... | collective-permute-start | bytes 294920 | tf_op jit(solution)/shard_map/ppermute | solution.py:16
  45.5 1.3 collective-permute-start.2
  46.8 1.3 multiply_add_fusion
  48.1 1.3 collective-permute-start.1
  49.4 4.8 %collective-permute-start = (f32[128,3,128]{2,0,1:T(8,128)S(1)}, f32[128,3,128]{2,0,1:T(8,128)S(1)}, u32[]{:S(2)}, u32[]{:S(2)}) collective-permute-start(f32[128,3,128]{2,0,1:T(8,128)S(1)} %get-tuple-element.30), channel_id=1, source_target_pairs={{0,1},{1,2},{2,3},{3,4},{4,5},{5,6},{6,7},{7,8},{8,9},{9,10},{10,1... | collective-permute-start | bytes 589832 | tf_op jit(solution)/shard_map/ppermute | solution.py:16
  54.3 0.4 multiply_reduce_fusion.1
  54.8 0.6 multiply_reduce_fusion
  55.4 1.3 fusion.54
  56.7 0.8 copy.97
  57.4 0.1 stack.61
  57.5 0.1 stack.62
  57.6 0.1 stack.59
  57.8 0.1 stack.54
  57.8 0.1 stack.55
  57.9 0.1 stack.56
  58.0 0.1 stack.57
  58.1 0.1 stack.58
  58.2 6.9 %all-to-all-start.3 = ((bf16[128,4,128]{2,1,0:T(4,128)(2,1)}), bf16[128,4,128]{2,1,0:T(4,128)(2,1)S(1)}, u32[]{:S(2)}, u32[]{:S(2)}) async-start(bf16[128,4,128]{2,1,0:T(4,128)(2,1)} %copy.97), calls=%async_computation.3 | async-start | bytes 262144 | tf_op jit(solution)/shard_map/all_to_all | solution.py:90
  65.2 0.1 fusion.17
  65.4 0.1 stack.70
  65.5 0.1 stack.68
  65.5 0.1 stack.69
  65.6 0.1 stack.65
  65.9 0.1 add_convert_fusion
  66.1 0.2 fusion
  66.3 0.1 copy.99
  66.4 0.1 copy.100
  66.6 0.8 copy.85
  67.3 5.6 %all-to-all-done.3 = bf16[128,4,128]{2,1,0:T(4,128)(2,1)S(1)} async-done(((bf16[128,4,128]{2,1,0:T(4,128)(2,1)}), bf16[128,4,128]{2,1,0:T(4,128)(2,1)S(1)}, u32[]{:S(2)}, u32[]{:S(2)}) %all-to-all-start.3) | async-done | bytes 131104 | tf_op jit(solution)/shard_map/all_to_all | solution.py:90
  73.0 3.5 %all-to-all-start.1 = ((bf16[128,4,128]{2,1,0:T(4,128)(2,1)}), bf16[128,4,128]{2,1,0:T(4,128)(2,1)S(1)}, u32[]{:S(2)}, u32[]{:S(2)}) async-start(bf16[128,4,128]{2,1,0:T(4,128)(2,1)} %copy.85), calls=%async_computation.1 | async-start | bytes 262144 | tf_op jit(solution)/shard_map/all_to_all | solution.py:89
  76.5 0.2 fusion.2
  76.7 62.6 %all-reduce = (f32[9,64]{1,0:T(8,128)}, f32[7,64]{1,0:T(8,128)}, f32[64,64]{1,0:T(8,128)}) all-reduce(f32[9,64]{1,0:T(8,128)S(1)} %broadcast_multiply_fusion.3, f32[7,64]{1,0:T(8,128)S(1)} %broadcast_multiply_fusion.4, f32[64,64]{1,0:T(8,128)S(1)} %broadcast_multiply_fusion.2), channel_id=1, replica_groups=mesh['parts'=2,'az'=16] {'az'}, use_global_device_ids=true, to_apply=%region_10.12 | all-reduce | flops 5120 | bytes 40960 | tf_op jit(solution)/shard_map/psum | solution.py:97
  139.3 0.7 copy.98
  140.0 0.7 copy.86
  (69 shorter events, 0.8 us)
Async XLA Ops:
  2.3 7.5 %copy-start.3 = (f32[7,64]{1,0:T(8,128)S(1)}, f32[7,64]{1,0:T(8,128)}, u32[]{:S(2)}) copy-start(f32[7,64]{1,0:T(8,128)} %param.11) | copy-start | bytes 5380
  2.3 7.6 %copy-start.4 = (f32[9,64]{1,0:T(8,128)S(1)}, f32[9,64]{1,0:T(8,128)}, u32[]{:S(2)}) copy-start(f32[9,64]{1,0:T(8,128)} %param.10) | copy-start | bytes 6916
  2.3 7.6 %copy-start.2 = (s32[9]{0:T(128)S(1)}, s32[9]{0:T(128)}, u32[]{:S(2)}) copy-start(s32[9]{0:T(128)} %param.13) | copy-start | bytes 112
  2.3 13.3 %copy-start.1 = (bf16[64,64]{1,0:T(8,128)(2,1)S(1)}, bf16[64,64]{1,0:T(8,128)(2,1)}, u32[]{:S(2)}) copy-start(bf16[64,64]{1,0:T(8,128)(2,1)} %param.12) | copy-start | bytes 24580
  2.3 15.4 %all-to-all-start.2 = ((bf16[8,64,128]{2,0,1:T(8,128)(2,1)}), bf16[8,64,128]{2,0,1:T(8,128)(2,1)S(1)}, u32[]{:S(2)}, u32[]{:S(2)}) async-start(bf16[8,64,128]{2,0,1:T(8,128)(2,1)} %copy.87), calls=%async_computation.2 | async-start | bytes 262144 | tf_op jit(solution)/shard_map/all_to_all | solution.py:56
  9.8 5.9 %copy-start = (bf16[8,64,128]{2,1,0:T(8,128)(2,1)S(1)}, bf16[8,64,128]{2,1,0:T(8,128)(2,1)}, u32[]{:S(2)}) copy-start(bf16[8,64,128]{2,1,0:T(8,128)(2,1)} %param.8) | copy-start | bytes 393220
  17.7 25.2 %all-to-all-start = ((bf16[8,64,128]{2,0,1:T(8,128)(2,1)}), bf16[8,64,128]{2,0,1:T(8,128)(2,1)S(1)}, u32[]{:S(2)}, u32[]{:S(2)}) async-start(bf16[8,64,128]{2,0,1:T(8,128)(2,1)} %copy.83), calls=%async_computation | async-start | bytes 262144 | tf_op jit(solution)/shard_map/all_to_all | solution.py:55
  43.2 11.0 %collective-permute-start.3 = (bf16[128,3,128]{2,0,1:T(8,128)(2,1)S(1)}, bf16[128,3,128]{2,0,1:T(8,128)(2,1)S(1)}, u32[]{:S(2)}, u32[]{:S(2)}) collective-permute-start(bf16[128,3,128]{2,0,1:T(8,128)(2,1)S(1)} %copy.117), channel_id=1, source_target_pairs={{0,1},{1,2},{2,3},{3,4},{4,5},{5,6},{6,7},{7,8},{8,9},{9,10},{10,1... | collective-permute-start | bytes 294920 | tf_op jit(solution)/shard_map/ppermute | solution.py:16
  45.5 8.8 %collective-permute-start.2 = (bf16[128,3,128]{2,0,1:T(8,128)(2,1)S(1)}, bf16[128,3,128]{2,0,1:T(8,128)(2,1)S(1)}, u32[]{:S(2)}, u32[]{:S(2)}) collective-permute-start(bf16[128,3,128]{2,0,1:T(8,128)(2,1)S(1)} %copy.118), channel_id=1, source_target_pairs={{1,0},{2,1},{3,2},{4,3},{5,4},{6,5},{7,6},{8,7},{9,8},{10,9},{11,1... | collective-permute-start | bytes 294920 | tf_op jit(solution)/shard_map/ppermute | solution.py:17
  48.1 17.1 %collective-permute-start.1 = (f32[128,3,128]{2,0,1:T(8,128)S(1)}, f32[128,3,128]{2,0,1:T(8,128)S(1)}, u32[]{:S(2)}, u32[]{:S(2)}) collective-permute-start(f32[128,3,128]{2,0,1:T(8,128)S(1)} %get-tuple-element.29), channel_id=1, source_target_pairs={{1,0},{2,1},{3,2},{4,3},{5,4},{6,5},{7,6},{8,7},{9,8},{10,9},{11,1... | collective-permute-start | bytes 589832 | tf_op jit(solution)/shard_map/ppermute | solution.py:17
  49.4 15.8 %collective-permute-start = (f32[128,3,128]{2,0,1:T(8,128)S(1)}, f32[128,3,128]{2,0,1:T(8,128)S(1)}, u32[]{:S(2)}, u32[]{:S(2)}) collective-permute-start(f32[128,3,128]{2,0,1:T(8,128)S(1)} %get-tuple-element.30), channel_id=1, source_target_pairs={{0,1},{1,2},{2,3},{3,4},{4,5},{5,6},{6,7},{7,8},{8,9},{9,10},{10,1... | collective-permute-start | bytes 589832 | tf_op jit(solution)/shard_map/ppermute | solution.py:16
  58.2 14.8 %all-to-all-start.3 = ((bf16[128,4,128]{2,1,0:T(4,128)(2,1)}), bf16[128,4,128]{2,1,0:T(4,128)(2,1)S(1)}, u32[]{:S(2)}, u32[]{:S(2)}) async-start(bf16[128,4,128]{2,1,0:T(4,128)(2,1)} %copy.97), calls=%async_computation.3 | async-start | bytes 262144 | tf_op jit(solution)/shard_map/all_to_all | solution.py:90
  73.0 67.0 %all-to-all-start.1 = ((bf16[128,4,128]{2,1,0:T(4,128)(2,1)}), bf16[128,4,128]{2,1,0:T(4,128)(2,1)S(1)}, u32[]{:S(2)}, u32[]{:S(2)}) async-start(bf16[128,4,128]{2,1,0:T(4,128)(2,1)} %copy.85), calls=%async_computation.1 | async-start | bytes 262144 | tf_op jit(solution)/shard_map/all_to_all | solution.py:89
where the time goes:
time: 142 us; the launch traced here: 141 us
  blocking collectives  62.6 us (44%)
  starting transfers between devices  32.5 us (23%)
  between operations  24.3 us (17%)
  local copies, waits for them, and re-layouts  9.88 us (7%)
  waiting for transfers between devices  6.74 us (5%)
  other arithmetic  4.16 us (3%)
    psum x1, blocking collectives, local(): lax.psum((scale * azim_fold, scale * radial_fold, scale * mix_fold), 'az')  62.6 us
    all_to_all x1, starting transfers between devices, local(): lax.all_to_all(cotangent, 'az', split_axis=1, concat_axis=0, tiled=True)  7.5 us
    ppermute x2, starting transfers between devices, extended(): before = lax.ppermute(last, axis, up)  7.12 us
    all_to_all x1, starting transfers between devices, local(): lax.all_to_all(input_moved, 'az', split_axis=0, concat_axis=1, tiled=True)  6.88 us
    all_to_all x1, waiting for transfers between devices, local(): lax.all_to_all(input_moved, 'az', split_axis=0, concat_axis=1, tiled=True)  5.65 us
    all_to_all x1, starting transfers between devices, local(): lax.all_to_all(fields, 'az', split_axis=1, concat_axis=0, tiled=True)  4.95 us
    all_to_all x1, starting transfers between devices, local(): lax.all_to_all(output_moved, 'az', split_axis=0, concat_axis=1, tiled=True)  3.51 us
  transfers between devices with their start and end apart: 8, of which 2 were waited for; matrix products, arithmetic and copies ran while one was open for 9% of the time, Pallas kernels for 0%

commit v1 on v0

v1 whole, which is shorter than its diff:
```python
import functools
import math

import jax
import jax.numpy as jnp
from jax import lax
from jax.experimental import pallas as pl
from jax.experimental.pallas import tpu as pltpu
from jax.sharding import PartitionSpec as P

F32, BF16 = jnp.float32, jnp.bfloat16
VMEM = pl.BlockSpec(memory_space=pltpu.VMEM)
SMEM = pl.BlockSpec(memory_space=pltpu.SMEM)
ROWS = 8
HALO = 3
SLAB = 8
PARAMS = pltpu.CompilerParams(vmem_limit_bytes=56 * 1024 * 1024)


def place():
    at = lax.axis_index("az")
    return at // 2, at % 2


def widen(azimuth_ref, radial_ref, mixing_ref, filters_ref, mix_ref):
    taps, channels = azimuth_ref.shape
    rtaps = radial_ref.shape[0]
    feat = mix_ref.shape[0]
    filters_ref[...] = jnp.zeros(filters_ref.shape, F32)
    mix_ref[...] = jnp.zeros(mix_ref.shape, BF16)
    for low in range(0, feat, channels):
        cell = slice(low, low + channels)
        filters_ref[0:taps, cell] = azimuth_ref[...]
        filters_ref[taps : taps + rtaps, cell] = radial_ref[...]
        mix_ref[cell, cell] = mixing_ref[...]


def visit(refs, stage, step, fill=False):
    if stage is None:
        for i, ref in enumerate(refs):
            step(i, ref)
        return
    if not fill:
        for i, ref in enumerate(refs):
            stage[i] = ref[...]

    def body(i, carry):
        step(i, stage.at[i])
        return carry

    lax.fori_loop(0, len(refs), body, 0)
    if fill:
        for i, ref in enumerate(refs):
            ref[...] = stage[i]


def partner(rounds, i, side):
    return 2 * (rounds - 1 - i) + side


def pack(rounds, own_f, own_g, other_f, other_g, *refs):
    outs, (fields, cots, *stage) = refs[:rounds], refs[rounds:]
    chip, core = place()
    near, rad, feat = own_f.shape
    step = rad + 2 * ROWS
    wide = fields.reshape(2 * near, step, feat)
    edge = jnp.zeros((2 * near, ROWS, feat), F32)
    wide[:, 0:ROWS, :] = edge
    wide[:, ROWS + rad : step, :] = edge
    for side, f, g in ((core, own_f, own_g), (1 - core, other_f, other_g)):
        wide[pl.ds(side * near, near), ROWS : ROWS + rad, :] = f[...].astype(F32)
        cots[pl.ds(side * near, near)] = g[...].astype(F32)
    body = 2 * near * ROWS

    def step_(i, out):
        to = chip ^ partner(rounds, i, core)
        first = pl.multiple_of(to * ROWS, ROWS)
        center = wide[:, pl.ds(pl.multiple_of(first + ROWS, ROWS), ROWS), :]
        out[0:body, :] = center.reshape(body, feat).astype(BF16)
        for h in range(2 * HALO):
            row = first + ROWS + (h - HALO if h < HALO else ROWS + h - HALO)
            at = body + h * 2 * near
            out[at : at + 2 * near, :] = fields[pl.ds(row, 2 * near, stride=step), :].astype(BF16)
        at = body + 2 * HALO * 2 * near
        out[at : at + body, :] = cots[:, pl.ds(first, ROWS), :].reshape(body, feat).astype(BF16)

    visit(outs, stage[0] if stage else None, step_, fill=True)


def convolve(rounds, taps, rtaps, channels, offsets, filters, mix, *refs):
    blocks, outs = refs[: 2 * rounds], refs[2 * rounds : 3 * rounds]
    fields, radial, grads, cots, hidden, spread, *stage = refs[3 * rounds :]
    chip, core = place()
    azim = radial.shape[0] // 2
    feat = mix.shape[0]
    step = 2 * ROWS
    wide = fields.reshape(azim, step, feat)
    near = azim // (2 * rounds)
    body = near * ROWS
    weight = [jnp.broadcast_to(filters[k : k + 1, :], (ROWS, feat)) for k in range(taps + rtaps)]
    def take(side, i, block):
        source = chip ^ partner(rounds, i, side)
        first = source * near
        wide[pl.ds(first, near), HALO : HALO + ROWS, :] = (
            block[0:body, :].astype(F32).reshape(near, ROWS, feat)
        )
        for h in range(2 * HALO):
            row = h if h < HALO else ROWS + h
            at = body + h * near
            fields[pl.ds(first * step + row, near, stride=step), :] = block[
                at : at + near, :
            ].astype(F32)
        at = body + 2 * HALO * near
        cot = block[at : at + body, :]
        cots[pl.ds(pl.multiple_of(first * ROWS, body), body), :] = cot
        back = lax.dot_general(cot, mix[...], (((1,), (1,)), ((), ())), preferred_element_type=F32)
        back = back.astype(BF16).astype(F32).reshape(near, ROWS, feat)
        grads[pl.ds(first, near)] = back
        grads[pl.ds(azim + first, near)] = back
        total = weight[taps] * wide[pl.ds(first, near), 0:ROWS, :]
        for j in range(1, rtaps):
            total = total + weight[taps + j] * wide[pl.ds(first, near), j : j + ROWS, :]
        radial[pl.ds(first, near)] = total
        radial[pl.ds(azim + first, near)] = total
    for side, group in ((core, blocks[:rounds]), (1 - core, blocks[rounds:])):
        visit(group, stage[0] if stage else None, functools.partial(take, side))
    ahead = [lax.rem(offsets[k] + azim, azim) for k in range(taps)]
    behind = [lax.rem(azim - offsets[k], azim) for k in range(taps)]

    def slab(n, sums):
        sums = list(sums)
        a = n * SLAB
        grad = grads[pl.ds(a, SLAB)]
        value = jnp.zeros((SLAB, ROWS, feat), F32)
        back = jnp.zeros((SLAB, ROWS, feat), F32)
        for k in range(taps):
            x = radial[pl.ds(a + ahead[k], SLAB)]
            value = value + weight[k] * x
            sums[k] = sums[k] + jnp.sum(x * grad, axis=0)
            back = back + weight[k] * grads[pl.ds(a + behind[k], SLAB)]
        rows = pl.ds(pl.multiple_of(a * ROWS, SLAB * ROWS), SLAB * ROWS)
        hidden[rows, :] = value.reshape(SLAB * ROWS, feat).astype(BF16)
        spread[rows, :] = back.reshape(SLAB * ROWS, feat).astype(BF16)
        for j in range(rtaps):
            sums[taps + j] = sums[taps + j] + jnp.sum(
                wide[pl.ds(a, SLAB), j : j + ROWS, :] * back, axis=0
            )
        return tuple(sums)

    zero = jnp.zeros((ROWS, feat), F32)
    sums = lax.fori_loop(0, azim // SLAB, slab, (zero,) * (taps + rtaps))
    product = lax.dot_general(
        hidden[...], cots[...], (((0,), (0,)), ((), ())), preferred_element_type=F32
    )
    lane = lax.broadcasted_iota(jnp.int32, (channels, feat), 1)
    mixed = jnp.where(lane < channels, product[0:channels], product[channels:feat])
    part = jnp.concatenate([jnp.sum(s, axis=0, keepdims=True) for s in sums] + [mixed], axis=0)
    part = part + pltpu.roll(part, channels, 1)
    few, half = (taps + rtaps) // 2, channels // 2
    low = jnp.concatenate([part[0:few], part[2 * few : 2 * few + half]], axis=0)
    high = jnp.concatenate([part[few : 2 * few], part[2 * few + half : 2 * few + channels]], axis=0)
    lane = lax.broadcasted_iota(jnp.int32, low.shape, 1)
    part = jnp.where(lane < channels, low, high)
    part = jnp.concatenate([part, jnp.zeros((8, feat), F32)], axis=0).astype(BF16)
    for i, out in enumerate(outs):
        to = chip ^ partner(rounds, i, core)
        rows = pl.ds(pl.multiple_of(to * body, body), body)
        out[0:body, :] = hidden[rows, :]
        out[body : 2 * body, :] = spread[rows, :]
        out[2 * body : 2 * body + part.shape[0], :] = part


def finish(rounds, taps, rtaps, scale, field, cot, filters, mix, *refs):
    blocks = refs[: 2 * rounds]
    out, grad, azimuth_out, radial_out, mixing_out, hidden, spread, summed, *stage = refs[2 * rounds :]
    chip, core = place()
    near, rad, feat = field.shape
    channels = azimuth_out.shape[1]
    body = near * ROWS
    spread[:, 0:ROWS, :] = jnp.zeros((near, ROWS, feat), F32)
    spread[:, ROWS + rad :, :] = jnp.zeros((near, ROWS, feat), F32)
    few, half = (taps + rtaps) // 2, channels // 2
    mine = pl.multiple_of(core * body, body)
    summed[...] = jnp.zeros(summed.shape, F32)

    def take(side, i, block):
        first = pl.multiple_of((chip ^ partner(rounds, i, side)) * ROWS, ROWS)
        hidden[:, pl.ds(first, ROWS), :] = (
            block[pl.ds(mine, body), :].astype(F32).reshape(near, ROWS, feat)
        )
        spread[:, pl.ds(pl.multiple_of(first + ROWS, ROWS), ROWS), :] = (
            block[pl.ds(2 * body + mine, body), :].astype(F32).reshape(near, ROWS, feat)
        )
        summed[...] += block[4 * body : 4 * body + summed.shape[0], :].astype(F32)

    for side, group in ((core, blocks[:rounds]), (1 - core, blocks[rounds:])):
        visit(group, stage[0] if stage else None, functools.partial(take, side))
    part = summed[0 : few + half, :] * scale
    azimuth_out[0:few, :] = part[0:few, 0:channels]
    azimuth_out[few:taps, :] = part[0 : taps - few, channels:feat]
    radial_out[...] = part[taps - few : few, channels:feat]
    mixing_out[0:half, :] = part[few : few + half, 0:channels]
    mixing_out[half:channels, :] = part[few : few + half, channels:feat]
    flat = hidden[...].reshape(near * rad, feat).astype(BF16)
    mixed = jnp.dot(flat, mix[...], preferred_element_type=F32).reshape(near, rad, feat)
    out[...] = (field[...].astype(F32) + mixed).astype(BF16)
    total = jnp.zeros((near, rad, feat), F32)
    for j in range(rtaps):
        weight = jnp.broadcast_to(filters[taps + j : taps + j + 1, :], (rad, feat))
        first = ROWS + HALO - j
        total = total + weight * spread[:, first : first + rad, :]
    branch = total.astype(BF16).astype(F32)
    grad[...] = (cot[...].astype(F32) + branch).astype(BF16)


def call(kernel, ins, outs, scratch, keep=False, name=None):
    ins = [pltpu.with_memory_space_constraint(x, pltpu.VMEM) if x.ndim > 1 else x for x in ins]
    return pl.pallas_call(
        kernel,
        in_specs=[VMEM if x.ndim > 1 else SMEM for x in ins],
        out_specs=[VMEM] * len(outs),
        out_shape=[(pltpu.VMEM if keep else jax.ShapeDtypeStruct)(*out) for out in outs],
        scratch_shapes=[pltpu.VMEM(*out) for out in scratch],
        compiler_params=PARAMS,
        name=name,
    )(*ins)


def swap(x):
    size = lax.axis_size("az")
    return lax.ppermute(x, "az", [(i, i ^ 1) for i in range(size)])


def exchange(messages):
    chips = lax.axis_size("az") // 2
    got = []
    for i, message in enumerate(messages):
        pairs = [
            (2 * c + k, 2 * (c ^ partner(len(messages), i, k)) + k) for c in range(chips) for k in range(2)
        ]
        got.append(lax.ppermute(message, "az", pairs))
    return got + [swap(x) for x in got]


def local(fields, cotangent, azimuth_filter, radial_filter, mixing, tap_offsets):
    size = lax.axis_size("az")
    rounds = size // 4
    near, rad, feat = fields.shape
    azim = near * size
    taps, rtaps, channels = tap_offsets.shape[0], radial_filter.shape[0], mixing.shape[0]
    many = rounds > 8
    other_f, other_g = swap(fields), swap(cotangent)
    filters, mix = call(
        widen,
        (azimuth_filter, radial_filter, mixing),
        [((taps + rtaps, feat), F32), ((feat, feat), BF16)],
        [],
        keep=True,
        name="widen",
    )
    other_f, other_g, filters, mix = lax.optimization_barrier((other_f, other_g, filters, mix))
    body = 2 * near * ROWS
    length = 2 * body + 2 * HALO * 2 * near
    message = ((length, feat), BF16)
    messages = call(
        functools.partial(pack, rounds),
        (fields, cotangent, other_f, other_g),
        [message] * rounds,
        [((2 * near * (rad + 2 * ROWS), feat), F32), ((2 * near, rad, feat), F32)]
        + [((rounds, length, feat), BF16)] * many,
        keep=True,
        name="pack",
    )
    blocks = exchange(messages)
    sums = (taps + rtaps + channels) // 2 + 8
    flat = ((azim * ROWS, feat), BF16)
    messages = call(
        functools.partial(convolve, rounds, taps, rtaps, channels),
        (tap_offsets, filters, mix, *blocks),
        [((2 * body + sums, feat), BF16)] * rounds,
        [((azim * 2 * ROWS, feat), F32)]
        + [((2 * azim, ROWS, feat), F32)] * 2
        + [flat] * 3
        + [((rounds, length, feat), BF16)] * many,
        keep=True,
        name="convolve",
    )
    blocks = exchange(messages)
    scale = 1.0 / math.sqrt(azim * rad * (feat // channels))
    return call(
        functools.partial(finish, rounds, taps, rtaps, scale),
        (fields, cotangent, filters, mix, *blocks),
        [
            (fields.shape, BF16),
            (fields.shape, BF16),
            ((taps, channels), F32),
            ((rtaps, channels), F32),
            ((channels, channels), F32),
        ],
        [((near, rad, feat), F32), ((near, rad + 2 * ROWS, feat), F32), ((sums, feat), F32)]
        + [((rounds, 2 * body + sums, feat), BF16)] * many,
        name="finish",
    )


def solution(mesh):
    cells = P(("parts", "az"), None, None)
    parts = P("parts", None)
    return jax.shard_map(
        lambda *args: tuple(local(*args)),
        mesh=mesh,
        in_specs=(cells, cells, P(), P(), P(), P()),
        out_specs=(cells, cells, parts, parts, parts),
        check_vma=False,
    )
```

time: 142 us -> 37.6 us (0.26)
  blocking collectives: 62.6 us -> 0 us
  between operations: 24.3 us -> 0.7 us
  starting transfers between devices: 32.5 us -> 15.2 us
  waiting for transfers between devices: 6.74 us -> 12.9 us
  local copies, waits for them, and re-layouts: 9.88 us -> 3.91 us
  Pallas kernels: 0 us -> 4.45 us
  other arithmetic: 4.16 us -> 0 us
    psum x1 -> x0, blocking collectives: 62.6 us -> none  [local(): lax.psum((scale * azim_fold, scale * radial_fold, scale * mix_fold), 'az')]
    all_to_all x4 -> x0, starting transfers between devices: 22.8 us -> none  [the longest x1 7.5 us: local(): lax.all_to_all(cotangent, 'az', split_axis=1, concat_axis=0, tiled=True)]
    ppermute x4 -> x18, waiting for transfers between devices: 0.01 us -> 12.9 us  [the longest x8 10.5 us: exchange(): got.append(lax.ppermute(message, 'az', pairs))]
    all_to_all x4 -> x0, waiting for transfers between devices: 6.73 us -> none  [the longest x1 5.65 us: local(): lax.all_to_all(input_moved, 'az', split_axis=0, concat_axis=1, tiled=True)]
    ppermute x4 -> x18, starting transfers between devices: 9.7 us -> 15.2 us  [the longest x8 11.6 us: exchange(): got.append(lax.ppermute(message, 'az', pairs))]
    pallas_call x0 -> x4, Pallas kernels: none -> 4.45 us  [call(): pl.pallas_call(kernel, in_specs=[VMEM if x.ndim > 1 else SMEM for x in in...]
    another operation x50 -> x0, local copies, waits for them, and re-layouts: 2.69 us -> none  [the longest x18 0.77 us: local(): azim_wide = jnp.tile(azimuth_filter, (1, axial))]
    convert_element_type x4 -> x0, local copies, waits for them, and re-layouts: 1.74 us -> none  [the longest x1 0.76 us: local(): (field_float + apply_mix(hidden, wide_mix)).astype(jnp.bfloat16)]
  transfers between devices with their start and end apart: 8 -> 18, of which waited for: 2 -> 10; matrix products, arithmetic and copies ran while one was open for 9% -> 0% of each run, Pallas kernels for 0% -> 0%
where the time goes in v1:
time: 37.6 us; the launch traced here: 37.2 us
  starting transfers between devices  15.2 us (40%)
  waiting for transfers between devices  12.9 us (34%)
  Pallas kernels  4.45 us (12%)
  local copies, waits for them, and re-layouts  3.91 us (10%)
  between operations  0.7 us (2%)
    ppermute x8, starting transfers between devices, exchange(): got.append(lax.ppermute(message, 'az', pairs))  11.6 us
    ppermute x8, waiting for transfers between devices, exchange(): got.append(lax.ppermute(message, 'az', pairs))  10.5 us
    pallas_call x4, Pallas kernels, call(): pl.pallas_call(kernel, in_specs=[VMEM if x.ndim > 1 else SMEM for x in in...  4.45 us
    unnamed x14, local copies, waits for them, and re-layouts  3.91 us
    ppermute x10, starting transfers between devices, swap(): return lax.ppermute(x, 'az', [(i, i ^ 1) for i in range(size)])  3.59 us
    ppermute x10, waiting for transfers between devices, swap(): return lax.ppermute(x, 'az', [(i, i ^ 1) for i in range(size)])  2.38 us
  transfers between devices with their start and end apart: 18, of which 10 were waited for; matrix products, arithmetic and copies ran while one was open for 0% of the time, Pallas kernels for 0%

profile of v1, /device:TPU:0, one launch (start us, length us, event | category | flops | bytes accessed | tf_op | source)
XLA Modules:
  0.0 37.2 jit_solution(5951628367344400529)
XLA Ops:
  0.6 0.5 %collective-permute-start = (bf16[8,64,128]{2,1,0:T(8,128)(2,1)}, bf16[8,64,128]{2,1,0:T(8,128)(2,1)S(1)}, u32[]{:S(2)}, u32[]{:S(2)}) collective-permute-start(bf16[8,64,128]{2,1,0:T(8,128)(2,1)} %field.1), channel_id=1, source_target_pairs={{0,1},{1,0},{2,3},{3,2},{4,5},{5,4},{6,7},{7,6},{8,9},{9,8},{10,11... | collective-permute-start | bytes 393224 | tf_op jit(solution)/shard_map/ppermute | solution.py:231
  1.1 0.1 collective-permute-start.1
  1.2 0.0 copy-start.4
  1.2 0.7 %copy-done.4 = bf16[64,64]{1,0:T(8,128)(2,1)S(1)} copy-done((bf16[64,64]{1,0:T(8,128)(2,1)S(1)}, bf16[64,64]{1,0:T(8,128)(2,1)}, u32[]{:S(2)}) %copy-start.4) | copy-done | bytes 8216
  1.9 0.0 copy-start.5
  2.0 0.7 %copy-done.5 = f32[9,64]{1,0:T(8,128)S(1)} copy-done((f32[9,64]{1,0:T(8,128)S(1)}, f32[9,64]{1,0:T(8,128)}, u32[]{:S(2)}) %copy-start.5) | copy-done | bytes 2328
  2.6 0.0 copy-start.6
  2.6 0.7 %copy-done.6 = f32[7,64]{1,0:T(8,128)S(1)} copy-done((f32[7,64]{1,0:T(8,128)S(1)}, f32[7,64]{1,0:T(8,128)}, u32[]{:S(2)}) %copy-start.6) | copy-done | bytes 1816
  3.3 0.1 widen.1
  3.4 0.0 collective-permute-done.other_f
  3.4 0.0 collective-permute-done.1.other_g
  3.4 0.0 copy-start
  3.4 0.9 %copy-done = bf16[8,64,128]{2,1,0:T(8,128)(2,1)S(1)} copy-done((bf16[8,64,128]{2,1,0:T(8,128)(2,1)S(1)}, bf16[8,64,128]{2,1,0:T(8,128)(2,1)}, u32[]{:S(2)}) %copy-start) | copy-done | bytes 131096
  4.3 0.0 copy-start.2
  4.3 0.9 %copy-done.2 = bf16[8,64,128]{2,1,0:T(8,128)(2,1)S(1)} copy-done((bf16[8,64,128]{2,1,0:T(8,128)(2,1)S(1)}, bf16[8,64,128]{2,1,0:T(8,128)(2,1)}, u32[]{:S(2)}) %copy-start.2) | copy-done | bytes 131096
  5.2 0.2 pack.1
  5.4 5.1 %collective-permute-start.2 = (bf16[352,128]{1,0:T(8,128)(2,1)S(1)}, bf16[352,128]{1,0:T(8,128)(2,1)S(1)}, u32[]{:S(2)}, u32[]{:S(2)}) collective-permute-start(bf16[352,128]{1,0:T(8,128)(2,1)S(1)} %get-tuple-element.25), channel_id=1, source_target_pairs={{0,12},{1,15},{2,14},{3,13},{4,8},{5,11},{6,10},{7,9},{8,4},{9,7},... | collective-permute-start | bytes 270344 | tf_op jit(solution)/shard_map/ppermute | solution.py:241
  10.5 0.0 collective-permute-start.3
  10.5 0.6 %collective-permute-start.4 = (bf16[352,128]{1,0:T(8,128)(2,1)S(1)}, bf16[352,128]{1,0:T(8,128)(2,1)S(1)}, u32[]{:S(2)}, u32[]{:S(2)}) collective-permute-start(bf16[352,128]{1,0:T(8,128)(2,1)S(1)} %get-tuple-element.27), channel_id=1, source_target_pairs={{0,4},{1,7},{2,6},{3,5},{4,0},{5,3},{6,2},{7,1},{8,12},{9,15},{10,... | collective-permute-start | bytes 270344 | tf_op jit(solution)/shard_map/ppermute | solution.py:241
  11.1 0.0 copy-start.1
  11.2 0.0 copy-start.3
  11.2 0.8 %collective-permute-start.5 = (bf16[352,128]{1,0:T(8,128)(2,1)S(1)}, bf16[352,128]{1,0:T(8,128)(2,1)S(1)}, u32[]{:S(2)}, u32[]{:S(2)}) collective-permute-start(bf16[352,128]{1,0:T(8,128)(2,1)S(1)} %get-tuple-element.28), channel_id=1, source_target_pairs={{0,0},{1,3},{2,2},{3,1},{4,4},{5,7},{6,6},{7,5},{8,8},{9,11},{10,1... | collective-permute-start | bytes 270344 | tf_op jit(solution)/shard_map/ppermute | solution.py:241
  11.9 1.9 %collective-permute-done.2.refs_0_ = bf16[352,128]{1,0:T(8,128)(2,1)S(1)} collective-permute-done((bf16[352,128]{1,0:T(8,128)(2,1)S(1)}, bf16[352,128]{1,0:T(8,128)(2,1)S(1)}, u32[]{:S(2)}, u32[]{:S(2)}) %collective-permute-start.2) | collective-permute-done | bytes 90144 | tf_op jit(solution)/shard_map/ppermute | solution.py:241
  13.8 1.1 %collective-permute-start.6 = (bf16[352,128]{1,0:T(8,128)(2,1)S(1)}, bf16[352,128]{1,0:T(8,128)(2,1)S(1)}, u32[]{:S(2)}, u32[]{:S(2)}) collective-permute-start(bf16[352,128]{1,0:T(8,128)(2,1)S(1)} %collective-permute-done.2.refs_0_), channel_id=1, source_target_pairs={{0,1},{1,0},{2,3},{3,2},{4,5},{5,4},{6,7},{7,6},{8,9},{9,8},{10,11... | collective-permute-start | bytes 270344 | tf_op jit(solution)/shard_map/ppermute | solution.py:231
  14.9 4.3 %collective-permute-done.3.refs_1_ = bf16[352,128]{1,0:T(8,128)(2,1)S(1)} collective-permute-done((bf16[352,128]{1,0:T(8,128)(2,1)S(1)}, bf16[352,128]{1,0:T(8,128)(2,1)S(1)}, u32[]{:S(2)}, u32[]{:S(2)}) %collective-permute-start.3) | collective-permute-done | bytes 90144 | tf_op jit(solution)/shard_map/ppermute | solution.py:241
  19.2 0.0 collective-permute-start.7
  19.2 0.0 collective-permute-done.4.refs_2_
  19.2 0.5 %collective-permute-start.8 = (bf16[352,128]{1,0:T(8,128)(2,1)S(1)}, bf16[352,128]{1,0:T(8,128)(2,1)S(1)}, u32[]{:S(2)}, u32[]{:S(2)}) collective-permute-start(bf16[352,128]{1,0:T(8,128)(2,1)S(1)} %collective-permute-done.4.refs_2_), channel_id=1, source_target_pairs={{0,1},{1,0},{2,3},{3,2},{4,5},{5,4},{6,7},{7,6},{8,9},{9,8},{10,11... | collective-permute-start | bytes 270344 | tf_op jit(solution)/shard_map/ppermute | solution.py:231
  19.7 0.0 collective-permute-done.5.refs_3_
  19.7 0.1 collective-permute-start.9
  19.8 0.0 collective-permute-done.6.refs_4_
  19.8 0.7 %collective-permute-done.7.refs_5_ = bf16[352,128]{1,0:T(8,128)(2,1)S(1)} collective-permute-done((bf16[352,128]{1,0:T(8,128)(2,1)S(1)}, bf16[352,128]{1,0:T(8,128)(2,1)S(1)}, u32[]{:S(2)}, u32[]{:S(2)}) %collective-permute-start.7) | collective-permute-done | bytes 90144 | tf_op jit(solution)/shard_map/ppermute | solution.py:231
  20.5 0.2 collective-permute-done.8.refs_6_
  20.6 0.4 collective-permute-done.9.refs_7_
  21.0 3.1 %convolve.1 = (bf16[304,128]{1,0:T(8,128)(2,1)S(1)}, bf16[304,128]{1,0:T(8,128)(2,1)S(1)}, bf16[304,128]{1,0:T(8,128)(2,1)S(1)}, bf16[304,128]{1,0:T(8,128)(2,1)S(1)}) custom-call(s32[9]{0:T(128)} %offsets.1, f32[16,128]{1,0:T(8,128)S(1)} %get-tuple-element.21.filters, bf16[128,128]{1,0:T(8,128)(2,1)S(1)} %get-tuple-element.22.mix, ...), custom_call_target="tpu_custom_call" | custom-call | tf_op jit(solution)/shard_map/convolve/pallas_call | solution.py:218
  24.1 2.5 %collective-permute-start.10 = (bf16[304,128]{1,0:T(8,128)(2,1)S(1)}, bf16[304,128]{1,0:T(8,128)(2,1)S(1)}, u32[]{:S(2)}, u32[]{:S(2)}) collective-permute-start(bf16[304,128]{1,0:T(8,128)(2,1)S(1)} %get-tuple-element.29), channel_id=1, source_target_pairs={{0,12},{1,15},{2,14},{3,13},{4,8},{5,11},{6,10},{7,9},{8,4},{9,7},... | collective-permute-start | bytes 233480 | tf_op jit(solution)/shard_map/ppermute | solution.py:241
  26.7 0.0 collective-permute-start.11
  26.7 1.9 %collective-permute-start.12 = (bf16[304,128]{1,0:T(8,128)(2,1)S(1)}, bf16[304,128]{1,0:T(8,128)(2,1)S(1)}, u32[]{:S(2)}, u32[]{:S(2)}) collective-permute-start(bf16[304,128]{1,0:T(8,128)(2,1)S(1)} %get-tuple-element.31), channel_id=1, source_target_pairs={{0,4},{1,7},{2,6},{3,5},{4,0},{5,3},{6,2},{7,1},{8,12},{9,15},{10,... | collective-permute-start | bytes 233480 | tf_op jit(solution)/shard_map/ppermute | solution.py:241
  28.6 0.7 %collective-permute-start.13 = (bf16[304,128]{1,0:T(8,128)(2,1)S(1)}, bf16[304,128]{1,0:T(8,128)(2,1)S(1)}, u32[]{:S(2)}, u32[]{:S(2)}) collective-permute-start(bf16[304,128]{1,0:T(8,128)(2,1)S(1)} %get-tuple-element.32), channel_id=1, source_target_pairs={{0,0},{1,3},{2,2},{3,1},{4,4},{5,7},{6,6},{7,5},{8,8},{9,11},{10,1... | collective-permute-start | bytes 233480 | tf_op jit(solution)/shard_map/ppermute | solution.py:241
  29.2 2.0 %collective-permute-done.10.refs_0_ = bf16[304,128]{1,0:T(8,128)(2,1)S(1)} collective-permute-done((bf16[304,128]{1,0:T(8,128)(2,1)S(1)}, bf16[304,128]{1,0:T(8,128)(2,1)S(1)}, u32[]{:S(2)}, u32[]{:S(2)}) %collective-permute-start.10) | collective-permute-done | bytes 77856 | tf_op jit(solution)/shard_map/ppermute | solution.py:241
  31.2 0.7 %collective-permute-start.14 = (bf16[304,128]{1,0:T(8,128)(2,1)S(1)}, bf16[304,128]{1,0:T(8,128)(2,1)S(1)}, u32[]{:S(2)}, u32[]{:S(2)}) collective-permute-start(bf16[304,128]{1,0:T(8,128)(2,1)S(1)} %collective-permute-done.10.refs_0_), channel_id=1, source_target_pairs={{0,1},{1,0},{2,3},{3,2},{4,5},{5,4},{6,7},{7,6},{8,9},{9,8},{10,11... | collective-permute-start | bytes 233480 | tf_op jit(solution)/shard_map/ppermute | solution.py:231
  32.0 2.4 %collective-permute-done.11.refs_1_ = bf16[304,128]{1,0:T(8,128)(2,1)S(1)} collective-permute-done((bf16[304,128]{1,0:T(8,128)(2,1)S(1)}, bf16[304,128]{1,0:T(8,128)(2,1)S(1)}, u32[]{:S(2)}, u32[]{:S(2)}) %collective-permute-start.11) | collective-permute-done | bytes 77856 | tf_op jit(solution)/shard_map/ppermute | solution.py:241
  34.3 0.1 collective-permute-start.15
  34.5 0.0 collective-permute-done.12.refs_2_
  34.5 0.4 %collective-permute-start.16 = (bf16[304,128]{1,0:T(8,128)(2,1)S(1)}, bf16[304,128]{1,0:T(8,128)(2,1)S(1)}, u32[]{:S(2)}, u32[]{:S(2)}) collective-permute-start(bf16[304,128]{1,0:T(8,128)(2,1)S(1)} %collective-permute-done.12.refs_2_), channel_id=1, source_target_pairs={{0,1},{1,0},{2,3},{3,2},{4,5},{5,4},{6,7},{7,6},{8,9},{9,8},{10,11... | collective-permute-start | bytes 233480 | tf_op jit(solution)/shard_map/ppermute | solution.py:231
  34.9 0.0 collective-permute-done.13.refs_3_
  34.9 0.1 collective-permute-start.17
  35.0 0.0 collective-permute-done.14.refs_4_
  35.0 0.6 %collective-permute-done.15.refs_5_ = bf16[304,128]{1,0:T(8,128)(2,1)S(1)} collective-permute-done((bf16[304,128]{1,0:T(8,128)(2,1)S(1)}, bf16[304,128]{1,0:T(8,128)(2,1)S(1)}, u32[]{:S(2)}, u32[]{:S(2)}) %collective-permute-start.15) | collective-permute-done | bytes 77856 | tf_op jit(solution)/shard_map/ppermute | solution.py:231
  35.6 0.2 collective-permute-done.16.refs_6_
  35.8 0.4 collective-permute-done.17.refs_7_
  36.1 0.0 copy-done.1
  36.1 0.0 copy-done.3
  36.1 1.1 %finish.1 = (bf16[8,64,128]{2,1,0:T(8,128)(2,1)}, bf16[8,64,128]{2,1,0:T(8,128)(2,1)}, f32[9,64]{1,0:T(8,128)}, f32[7,64]{1,0:T(8,128)}, f32[64,64]{1,0:T(8,128)}) custom-call(bf16[8,64,128]{2,1,0:T(8,128)(2,1)S(1)} %copy-done.1, bf16[8,64,128]{2,1,0:T(8,128)(2,1)S(1)} %copy-done.3, f32[16,128]{1,0:T(8,128)S(1)} %get-tuple-element.21.filters, ...), custom_call_target="tpu_custom_call" | custom-call | tf_op jit(solution)/shard_map/finish/pallas_call | solution.py:218
Async XLA Ops:
  0.6 2.8 %collective-permute-start = (bf16[8,64,128]{2,1,0:T(8,128)(2,1)}, bf16[8,64,128]{2,1,0:T(8,128)(2,1)S(1)}, u32[]{:S(2)}, u32[]{:S(2)}) collective-permute-start(bf16[8,64,128]{2,1,0:T(8,128)(2,1)} %field.1), channel_id=1, source_target_pairs={{0,1},{1,0},{2,3},{3,2},{4,5},{5,4},{6,7},{7,6},{8,9},{9,8},{10,11... | collective-permute-start | bytes 393224 | tf_op jit(solution)/shard_map/ppermute | solution.py:231
  1.1 2.3 %collective-permute-start.1 = (bf16[8,64,128]{2,1,0:T(8,128)(2,1)}, bf16[8,64,128]{2,1,0:T(8,128)(2,1)S(1)}, u32[]{:S(2)}, u32[]{:S(2)}) collective-permute-start(bf16[8,64,128]{2,1,0:T(8,128)(2,1)} %cot.1), channel_id=1, source_target_pairs={{0,1},{1,0},{2,3},{3,2},{4,5},{5,4},{6,7},{7,6},{8,9},{9,8},{10,11... | collective-permute-start | bytes 393224 | tf_op jit(solution)/shard_map/ppermute | solution.py:231
  1.2 0.7 %copy-start.4 = (bf16[64,64]{1,0:T(8,128)(2,1)S(1)}, bf16[64,64]{1,0:T(8,128)(2,1)}, u32[]{:S(2)}) copy-start(bf16[64,64]{1,0:T(8,128)(2,1)} %mixing_ref.1) | copy-start | bytes 24580
  1.9 0.7 %copy-start.5 = (f32[9,64]{1,0:T(8,128)S(1)}, f32[9,64]{1,0:T(8,128)}, u32[]{:S(2)}) copy-start(f32[9,64]{1,0:T(8,128)} %azimuth_ref.1) | copy-start | bytes 6916
  2.6 0.7 %copy-start.6 = (f32[7,64]{1,0:T(8,128)S(1)}, f32[7,64]{1,0:T(8,128)}, u32[]{:S(2)}) copy-start(f32[7,64]{1,0:T(8,128)} %radial_ref.1) | copy-start | bytes 5380
  3.4 0.9 %copy-start = (bf16[8,64,128]{2,1,0:T(8,128)(2,1)S(1)}, bf16[8,64,128]{2,1,0:T(8,128)(2,1)}, u32[]{:S(2)}) copy-start(bf16[8,64,128]{2,1,0:T(8,128)(2,1)} %field.1) | copy-start | bytes 393220
  4.3 0.9 %copy-start.2 = (bf16[8,64,128]{2,1,0:T(8,128)(2,1)S(1)}, bf16[8,64,128]{2,1,0:T(8,128)(2,1)}, u32[]{:S(2)}) copy-start(bf16[8,64,128]{2,1,0:T(8,128)(2,1)} %cot.1) | copy-start | bytes 393220
  5.4 8.4 %collective-permute-start.2 = (bf16[352,128]{1,0:T(8,128)(2,1)S(1)}, bf16[352,128]{1,0:T(8,128)(2,1)S(1)}, u32[]{:S(2)}, u32[]{:S(2)}) collective-permute-start(bf16[352,128]{1,0:T(8,128)(2,1)S(1)} %get-tuple-element.25), channel_id=1, source_target_pairs={{0,12},{1,15},{2,14},{3,13},{4,8},{5,11},{6,10},{7,9},{8,4},{9,7},... | collective-permute-start | bytes 270344 | tf_op jit(solution)/shard_map/ppermute | solution.py:241
  10.5 8.7 %collective-permute-start.3 = (bf16[352,128]{1,0:T(8,128)(2,1)S(1)}, bf16[352,128]{1,0:T(8,128)(2,1)S(1)}, u32[]{:S(2)}, u32[]{:S(2)}) collective-permute-start(bf16[352,128]{1,0:T(8,128)(2,1)S(1)} %get-tuple-element.26), channel_id=1, source_target_pairs={{0,8},{1,11},{2,10},{3,9},{4,12},{5,15},{6,14},{7,13},{8,0},{9,3},... | collective-permute-start | bytes 270344 | tf_op jit(solution)/shard_map/ppermute | solution.py:241
  10.5 8.7 %collective-permute-start.4 = (bf16[352,128]{1,0:T(8,128)(2,1)S(1)}, bf16[352,128]{1,0:T(8,128)(2,1)S(1)}, u32[]{:S(2)}, u32[]{:S(2)}) collective-permute-start(bf16[352,128]{1,0:T(8,128)(2,1)S(1)} %get-tuple-element.27), channel_id=1, source_target_pairs={{0,4},{1,7},{2,6},{3,5},{4,0},{5,3},{6,2},{7,1},{8,12},{9,15},{10,... | collective-permute-start | bytes 270344 | tf_op jit(solution)/shard_map/ppermute | solution.py:241
  11.1 25.0 %copy-start.1 = (bf16[8,64,128]{2,1,0:T(8,128)(2,1)S(1)}, bf16[8,64,128]{2,1,0:T(8,128)(2,1)}, u32[]{:S(2)}) copy-start(bf16[8,64,128]{2,1,0:T(8,128)(2,1)} %field.1) | copy-start | bytes 393220
  11.2 25.0 %copy-start.3 = (bf16[8,64,128]{2,1,0:T(8,128)(2,1)S(1)}, bf16[8,64,128]{2,1,0:T(8,128)(2,1)}, u32[]{:S(2)}) copy-start(bf16[8,64,128]{2,1,0:T(8,128)(2,1)} %cot.1) | copy-start | bytes 393220
  11.2 8.5 %collective-permute-start.5 = (bf16[352,128]{1,0:T(8,128)(2,1)S(1)}, bf16[352,128]{1,0:T(8,128)(2,1)S(1)}, u32[]{:S(2)}, u32[]{:S(2)}) collective-permute-start(bf16[352,128]{1,0:T(8,128)(2,1)S(1)} %get-tuple-element.28), channel_id=1, source_target_pairs={{0,0},{1,3},{2,2},{3,1},{4,4},{5,7},{6,6},{7,5},{8,8},{9,11},{10,1... | collective-permute-start | bytes 270344 | tf_op jit(solution)/shard_map/ppermute | solution.py:241
  13.8 5.9 %collective-permute-start.6 = (bf16[352,128]{1,0:T(8,128)(2,1)S(1)}, bf16[352,128]{1,0:T(8,128)(2,1)S(1)}, u32[]{:S(2)}, u32[]{:S(2)}) collective-permute-start(bf16[352,128]{1,0:T(8,128)(2,1)S(1)} %collective-permute-done.2.refs_0_), channel_id=1, source_target_pairs={{0,1},{1,0},{2,3},{3,2},{4,5},{5,4},{6,7},{7,6},{8,9},{9,8},{10,11... | collective-permute-start | bytes 270344 | tf_op jit(solution)/shard_map/ppermute | solution.py:231
  19.2 1.3 %collective-permute-start.7 = (bf16[352,128]{1,0:T(8,128)(2,1)S(1)}, bf16[352,128]{1,0:T(8,128)(2,1)S(1)}, u32[]{:S(2)}, u32[]{:S(2)}) collective-permute-start(bf16[352,128]{1,0:T(8,128)(2,1)S(1)} %collective-permute-done.3.refs_1_), channel_id=1, source_target_pairs={{0,1},{1,0},{2,3},{3,2},{4,5},{5,4},{6,7},{7,6},{8,9},{9,8},{10,11... | collective-permute-start | bytes 270344 | tf_op jit(solution)/shard_map/ppermute | solution.py:231
  19.2 1.4 %collective-permute-start.8 = (bf16[352,128]{1,0:T(8,128)(2,1)S(1)}, bf16[352,128]{1,0:T(8,128)(2,1)S(1)}, u32[]{:S(2)}, u32[]{:S(2)}) collective-permute-start(bf16[352,128]{1,0:T(8,128)(2,1)S(1)} %collective-permute-done.4.refs_2_), channel_id=1, source_target_pairs={{0,1},{1,0},{2,3},{3,2},{4,5},{5,4},{6,7},{7,6},{8,9},{9,8},{10,11... | collective-permute-start | bytes 270344 | tf_op jit(solution)/shard_map/ppermute | solution.py:231
  19.7 1.3 %collective-permute-start.9 = (bf16[352,128]{1,0:T(8,128)(2,1)S(1)}, bf16[352,128]{1,0:T(8,128)(2,1)S(1)}, u32[]{:S(2)}, u32[]{:S(2)}) collective-permute-start(bf16[352,128]{1,0:T(8,128)(2,1)S(1)} %collective-permute-done.5.refs_3_), channel_id=1, source_target_pairs={{0,1},{1,0},{2,3},{3,2},{4,5},{5,4},{6,7},{7,6},{8,9},{9,8},{10,11... | collective-permute-start | bytes 270344 | tf_op jit(solution)/shard_map/ppermute | solution.py:231
  24.1 7.1 %collective-permute-start.10 = (bf16[304,128]{1,0:T(8,128)(2,1)S(1)}, bf16[304,128]{1,0:T(8,128)(2,1)S(1)}, u32[]{:S(2)}, u32[]{:S(2)}) collective-permute-start(bf16[304,128]{1,0:T(8,128)(2,1)S(1)} %get-tuple-element.29), channel_id=1, source_target_pairs={{0,12},{1,15},{2,14},{3,13},{4,8},{5,11},{6,10},{7,9},{8,4},{9,7},... | collective-permute-start | bytes 233480 | tf_op jit(solution)/shard_map/ppermute | solution.py:241
  26.7 7.7 %collective-permute-start.11 = (bf16[304,128]{1,0:T(8,128)(2,1)S(1)}, bf16[304,128]{1,0:T(8,128)(2,1)S(1)}, u32[]{:S(2)}, u32[]{:S(2)}) collective-permute-start(bf16[304,128]{1,0:T(8,128)(2,1)S(1)} %get-tuple-element.30), channel_id=1, source_target_pairs={{0,8},{1,11},{2,10},{3,9},{4,12},{5,15},{6,14},{7,13},{8,0},{9,3},... | collective-permute-start | bytes 233480 | tf_op jit(solution)/shard_map/ppermute | solution.py:241
  26.7 7.8 %collective-permute-start.12 = (bf16[304,128]{1,0:T(8,128)(2,1)S(1)}, bf16[304,128]{1,0:T(8,128)(2,1)S(1)}, u32[]{:S(2)}, u32[]{:S(2)}) collective-permute-start(bf16[304,128]{1,0:T(8,128)(2,1)S(1)} %get-tuple-element.31), channel_id=1, source_target_pairs={{0,4},{1,7},{2,6},{3,5},{4,0},{5,3},{6,2},{7,1},{8,12},{9,15},{10,... | collective-permute-start | bytes 233480 | tf_op jit(solution)/shard_map/ppermute | solution.py:241
  28.6 6.3 %collective-permute-start.13 = (bf16[304,128]{1,0:T(8,128)(2,1)S(1)}, bf16[304,128]{1,0:T(8,128)(2,1)S(1)}, u32[]{:S(2)}, u32[]{:S(2)}) collective-permute-start(bf16[304,128]{1,0:T(8,128)(2,1)S(1)} %get-tuple-element.32), channel_id=1, source_target_pairs={{0,0},{1,3},{2,2},{3,1},{4,4},{5,7},{6,6},{7,5},{8,8},{9,11},{10,1... | collective-permute-start | bytes 233480 | tf_op jit(solution)/shard_map/ppermute | solution.py:241
  31.2 3.7 %collective-permute-start.14 = (bf16[304,128]{1,0:T(8,128)(2,1)S(1)}, bf16[304,128]{1,0:T(8,128)(2,1)S(1)}, u32[]{:S(2)}, u32[]{:S(2)}) collective-permute-start(bf16[304,128]{1,0:T(8,128)(2,1)S(1)} %collective-permute-done.10.refs_0_), channel_id=1, source_target_pairs={{0,1},{1,0},{2,3},{3,2},{4,5},{5,4},{6,7},{7,6},{8,9},{9,8},{10,11... | collective-permute-start | bytes 233480 | tf_op jit(solution)/shard_map/ppermute | solution.py:231
  34.3 1.3 %collective-permute-start.15 = (bf16[304,128]{1,0:T(8,128)(2,1)S(1)}, bf16[304,128]{1,0:T(8,128)(2,1)S(1)}, u32[]{:S(2)}, u32[]{:S(2)}) collective-permute-start(bf16[304,128]{1,0:T(8,128)(2,1)S(1)} %collective-permute-done.11.refs_1_), channel_id=1, source_target_pairs={{0,1},{1,0},{2,3},{3,2},{4,5},{5,4},{6,7},{7,6},{8,9},{9,8},{10,11... | collective-permute-start | bytes 233480 | tf_op jit(solution)/shard_map/ppermute | solution.py:231
  34.5 1.3 %collective-permute-start.16 = (bf16[304,128]{1,0:T(8,128)(2,1)S(1)}, bf16[304,128]{1,0:T(8,128)(2,1)S(1)}, u32[]{:S(2)}, u32[]{:S(2)}) collective-permute-start(bf16[304,128]{1,0:T(8,128)(2,1)S(1)} %collective-permute-done.12.refs_2_), channel_id=1, source_target_pairs={{0,1},{1,0},{2,3},{3,2},{4,5},{5,4},{6,7},{7,6},{8,9},{9,8},{10,11... | collective-permute-start | bytes 233480 | tf_op jit(solution)/shard_map/ppermute | solution.py:231
  34.9 1.3 %collective-permute-start.17 = (bf16[304,128]{1,0:T(8,128)(2,1)S(1)}, bf16[304,128]{1,0:T(8,128)(2,1)S(1)}, u32[]{:S(2)}, u32[]{:S(2)}) collective-permute-start(bf16[304,128]{1,0:T(8,128)(2,1)S(1)} %collective-permute-done.13.refs_3_), channel_id=1, source_target_pairs={{0,1},{1,0},{2,3},{3,2},{4,5},{5,4},{6,7},{7,6},{8,9},{9,8},{10,11... | collective-permute-start | bytes 233480 | tf_op jit(solution)/shard_map/ppermute | solution.py:231

commit v2 on v1

--- a/solution.py
+++ b/solution.py
@@ -22,17 +22,32 @@
     return at // 2, at % 2
 
 
-def widen(azimuth_ref, radial_ref, mixing_ref, filters_ref, mix_ref):
-    taps, channels = azimuth_ref.shape
-    rtaps = radial_ref.shape[0]
-    feat = mix_ref.shape[0]
-    filters_ref[...] = jnp.zeros(filters_ref.shape, F32)
-    mix_ref[...] = jnp.zeros(mix_ref.shape, BF16)
+def gather(field, cot, azimuth, radial, mixing, offsets, *refs):
+    own_f, own_g, filters, mix, own_offsets, azimuth_in, radial_in, mixing_in, sems = refs
+    pairs = (
+        (azimuth, azimuth_in),
+        (radial, radial_in),
+        (mixing, mixing_in),
+        (offsets, own_offsets),
+        (field, own_f),
+        (cot, own_g),
+    )
+    copies = [pltpu.make_async_copy(*pair, sems.at[i]) for i, pair in enumerate(pairs)]
+    for copy in copies:
+        copy.start()
+    filters[...] = jnp.zeros(filters.shape, F32)
+    mix[...] = jnp.zeros(mix.shape, BF16)
+    for copy in copies[:3]:
+        copy.wait()
+    taps, channels = azimuth_in.shape
+    rtaps, feat = radial_in.shape[0], mix.shape[0]
     for low in range(0, feat, channels):
         cell = slice(low, low + channels)
-        filters_ref[0:taps, cell] = azimuth_ref[...]
-        filters_ref[taps : taps + rtaps, cell] = radial_ref[...]
-        mix_ref[cell, cell] = mixing_ref[...]
+        filters[0:taps, cell] = azimuth_in[...]
+        filters[taps : taps + rtaps, cell] = radial_in[...]
+        mix[cell, cell] = mixing_in[...]
+    for copy in copies[3:]:
+        copy.wait()
 
 
 def visit(refs, stage, step, fill=False):
@@ -214,7 +229,9 @@
 
 
 def call(kernel, ins, outs, scratch, keep=False, name=None):
-    ins = [pltpu.with_memory_space_constraint(x, pltpu.VMEM) if x.ndim > 1 else x for x in ins]
+    ins = [
+        pltpu.with_memory_space_constraint(x, pltpu.VMEM if x.ndim > 1 else pltpu.SMEM) for x in ins
+    ]
     return pl.pallas_call(
         kernel,
         in_specs=[VMEM if x.ndim > 1 else SMEM for x in ins],
@@ -250,15 +267,31 @@
     taps, rtaps, channels = tap_offsets.shape[0], radial_filter.shape[0], mixing.shape[0]
     many = rounds > 8
     other_f, other_g = swap(fields), swap(cotangent)
-    filters, mix = call(
-        widen,
-        (azimuth_filter, radial_filter, mixing),
-        [((taps + rtaps, feat), F32), ((feat, feat), BF16)],
-        [],
-        keep=True,
-        name="widen",
-    )
-    other_f, other_g, filters, mix = lax.optimization_barrier((other_f, other_g, filters, mix))
+    arguments = (fields, cotangent, azimuth_filter, radial_filter, mixing, tap_offsets)
+    kept = [
+        pltpu.VMEM(fields.shape, BF16),
+        pltpu.VMEM(fields.shape, BF16),
+        pltpu.VMEM((taps + rtaps, feat), F32),
+        pltpu.VMEM((feat, feat), BF16),
+        pltpu.SMEM((taps,), jnp.int32),
+    ]
+    fields, cotangent, filters, mix, tap_offsets = pl.pallas_call(
+        gather,
+        in_specs=[pl.BlockSpec(memory_space=pltpu.HBM)] * len(arguments),
+        out_specs=[VMEM] * 4 + [SMEM],
+        out_shape=kept,
+        scratch_shapes=[
+            pltpu.VMEM(azimuth_filter.shape, F32),
+            pltpu.VMEM(radial_filter.shape, F32),
+            pltpu.VMEM(mixing.shape, BF16),
+            pltpu.SemaphoreType.DMA((len(arguments),)),
+        ],
+        compiler_params=PARAMS,
+        name="gather",
+    )(*(pltpu.with_memory_space_constraint(x, pltpu.HBM) for x in arguments))
+    other_f, other_g, fields, cotangent = lax.optimization_barrier(
+        (other_f, other_g, fields, cotangent)
+    )
     body = 2 * near * ROWS
     length = 2 * body + 2 * HALO * 2 * near
     message = ((length, feat), BF16)

time: 37.6 us -> 34 us (0.904)
  local copies, waits for them, and re-layouts: 3.91 us -> 0 us
  Pallas kernels: 4.45 us -> 4.87 us
    unnamed x14 -> x0, local copies, waits for them, and re-layouts: 3.91 us -> none
    pallas_call x0 -> x1, Pallas kernels: none -> 1.07 us  [local(): pl.pallas_call(gather, in_specs=[pl.BlockSpec(memory_space=pltpu.HBM)] *...]
    pallas_call x4 -> x3, Pallas kernels: 4.45 us -> 3.8 us  [call(): pl.pallas_call(kernel, in_specs=[VMEM if x.ndim > 1 else SMEM for x in in...]
    ppermute x10, waiting for transfers between devices: 2.38 us -> 2.82 us  [swap(): return lax.ppermute(x, 'az', [(i, i ^ 1) for i in range(size)])]
  transfers between devices with their start and end apart: 18 -> 18, of which waited for: 10 -> 11; matrix products, arithmetic and copies ran while one was open for 0% -> 0% of each run, Pallas kernels for 0% -> 3%
where the time goes in v2:
time: 34 us; the launch traced here: 33.8 us
  starting transfers between devices  15 us (44%)
  waiting for transfers between devices  13.2 us (39%)
  Pallas kernels  4.87 us (14%)
  between operations  0.68 us (2%)
    ppermute x8, starting transfers between devices, exchange(): got.append(lax.ppermute(message, 'az', pairs))  11.2 us
    ppermute x8, waiting for transfers between devices, exchange(): got.append(lax.ppermute(message, 'az', pairs))  10.4 us
    pallas_call x3, Pallas kernels, call(): pl.pallas_call(kernel, in_specs=[VMEM if x.ndim > 1 else SMEM for x in in...  3.8 us
    ppermute x10, starting transfers between devices, swap(): return lax.ppermute(x, 'az', [(i, i ^ 1) for i in range(size)])  3.78 us
    ppermute x10, waiting for transfers between devices, swap(): return lax.ppermute(x, 'az', [(i, i ^ 1) for i in range(size)])  2.82 us
    pallas_call x1, Pallas kernels, local(): pl.pallas_call(gather, in_specs=[pl.BlockSpec(memory_space=pltpu.HBM)] *...  1.07 us
  transfers between devices with their start and end apart: 18, of which 11 were waited for; matrix products, arithmetic and copies ran while one was open for 0% of the time, Pallas kernels for 3%

profile of v2, /device:TPU:0, one launch (start us, length us, event | category | flops | bytes accessed | tf_op | source)
XLA Modules:
  0.0 33.8 jit_solution(728849105294932689)
XLA Ops:
  0.6 0.5 %collective-permute-start = (bf16[8,64,128]{2,1,0:T(8,128)(2,1)}, bf16[8,64,128]{2,1,0:T(8,128)(2,1)S(1)}, u32[]{:S(2)}, u32[]{:S(2)}) collective-permute-start(bf16[8,64,128]{2,1,0:T(8,128)(2,1)} %field.1), channel_id=1, source_target_pairs={{0,1},{1,0},{2,3},{3,2},{4,5},{5,4},{6,7},{7,6},{8,9},{9,8},{10,11... | collective-permute-start | bytes 393224 | tf_op jit(solution)/shard_map/ppermute | solution.py:248
  1.2 0.1 collective-permute-start.1
  1.2 1.1 %gather.1 = (bf16[8,64,128]{2,1,0:T(8,128)(2,1)S(1)}, bf16[8,64,128]{2,1,0:T(8,128)(2,1)S(1)}, f32[16,128]{1,0:T(8,128)S(1)}, bf16[128,128]{1,0:T(8,128)(2,1)S(1)}, s32[9]{0:T(128)S(4)}) custom-call(bf16[8,64,128]{2,1,0:T(8,128)(2,1)} %field.1, bf16[8,64,128]{2,1,0:T(8,128)(2,1)} %cot.1, f32[9,64]{1,0:T(8,128)} %azimuth.1, f32[7,64]{1,0:T(8,128)} %radial.1, ...), custom_call_target="tpu_custom_call" | custom-call | tf_op jit(solution)/shard_map/gather/pallas_call | solution.py:278
  2.3 0.0 collective-permute-done.other_f
  2.3 0.4 %collective-permute-done.1.other_g = bf16[8,64,128]{2,1,0:T(8,128)(2,1)S(1)} collective-permute-done((bf16[8,64,128]{2,1,0:T(8,128)(2,1)}, bf16[8,64,128]{2,1,0:T(8,128)(2,1)S(1)}, u32[]{:S(2)}, u32[]{:S(2)}) %collective-permute-start.1) | collective-permute-done | bytes 131104 | tf_op jit(solution)/shard_map/ppermute | solution.py:248
  2.7 0.2 pack.1
  2.9 4.8 %collective-permute-start.2 = (bf16[352,128]{1,0:T(8,128)(2,1)S(1)}, bf16[352,128]{1,0:T(8,128)(2,1)S(1)}, u32[]{:S(2)}, u32[]{:S(2)}) collective-permute-start(bf16[352,128]{1,0:T(8,128)(2,1)S(1)} %get-tuple-element.31), channel_id=1, source_target_pairs={{0,12},{1,15},{2,14},{3,13},{4,8},{5,11},{6,10},{7,9},{8,4},{9,7},... | collective-permute-start | bytes 270344 | tf_op jit(solution)/shard_map/ppermute | solution.py:258
  7.7 0.0 collective-permute-start.3
  7.7 0.6 %collective-permute-start.4 = (bf16[352,128]{1,0:T(8,128)(2,1)S(1)}, bf16[352,128]{1,0:T(8,128)(2,1)S(1)}, u32[]{:S(2)}, u32[]{:S(2)}) collective-permute-start(bf16[352,128]{1,0:T(8,128)(2,1)S(1)} %get-tuple-element.33), channel_id=1, source_target_pairs={{0,4},{1,7},{2,6},{3,5},{4,0},{5,3},{6,2},{7,1},{8,12},{9,15},{10,... | collective-permute-start | bytes 270344 | tf_op jit(solution)/shard_map/ppermute | solution.py:258
  8.4 0.7 %collective-permute-start.5 = (bf16[352,128]{1,0:T(8,128)(2,1)S(1)}, bf16[352,128]{1,0:T(8,128)(2,1)S(1)}, u32[]{:S(2)}, u32[]{:S(2)}) collective-permute-start(bf16[352,128]{1,0:T(8,128)(2,1)S(1)} %get-tuple-element.34), channel_id=1, source_target_pairs={{0,0},{1,3},{2,2},{3,1},{4,4},{5,7},{6,6},{7,5},{8,8},{9,11},{10,1... | collective-permute-start | bytes 270344 | tf_op jit(solution)/shard_map/ppermute | solution.py:258
  9.0 1.8 %collective-permute-done.2.refs_0_ = bf16[352,128]{1,0:T(8,128)(2,1)S(1)} collective-permute-done((bf16[352,128]{1,0:T(8,128)(2,1)S(1)}, bf16[352,128]{1,0:T(8,128)(2,1)S(1)}, u32[]{:S(2)}, u32[]{:S(2)}) %collective-permute-start.2) | collective-permute-done | bytes 90144 | tf_op jit(solution)/shard_map/ppermute | solution.py:258
  10.9 1.3 %collective-permute-start.6 = (bf16[352,128]{1,0:T(8,128)(2,1)S(1)}, bf16[352,128]{1,0:T(8,128)(2,1)S(1)}, u32[]{:S(2)}, u32[]{:S(2)}) collective-permute-start(bf16[352,128]{1,0:T(8,128)(2,1)S(1)} %collective-permute-done.2.refs_0_), channel_id=1, source_target_pairs={{0,1},{1,0},{2,3},{3,2},{4,5},{5,4},{6,7},{7,6},{8,9},{9,8},{10,11... | collective-permute-start | bytes 270344 | tf_op jit(solution)/shard_map/ppermute | solution.py:248
  12.2 3.9 %collective-permute-done.3.refs_1_ = bf16[352,128]{1,0:T(8,128)(2,1)S(1)} collective-permute-done((bf16[352,128]{1,0:T(8,128)(2,1)S(1)}, bf16[352,128]{1,0:T(8,128)(2,1)S(1)}, u32[]{:S(2)}, u32[]{:S(2)}) %collective-permute-start.3) | collective-permute-done | bytes 90144 | tf_op jit(solution)/shard_map/ppermute | solution.py:258
  16.1 0.0 collective-permute-start.7
  16.2 0.0 collective-permute-done.4.refs_2_
  16.2 0.5 %collective-permute-start.8 = (bf16[352,128]{1,0:T(8,128)(2,1)S(1)}, bf16[352,128]{1,0:T(8,128)(2,1)S(1)}, u32[]{:S(2)}, u32[]{:S(2)}) collective-permute-start(bf16[352,128]{1,0:T(8,128)(2,1)S(1)} %collective-permute-done.4.refs_2_), channel_id=1, source_target_pairs={{0,1},{1,0},{2,3},{3,2},{4,5},{5,4},{6,7},{7,6},{8,9},{9,8},{10,11... | collective-permute-start | bytes 270344 | tf_op jit(solution)/shard_map/ppermute | solution.py:248
  16.7 0.0 collective-permute-done.5.refs_3_
  16.7 0.1 collective-permute-start.9
  16.7 0.0 collective-permute-done.6.refs_4_
  16.7 0.7 %collective-permute-done.7.refs_5_ = bf16[352,128]{1,0:T(8,128)(2,1)S(1)} collective-permute-done((bf16[352,128]{1,0:T(8,128)(2,1)S(1)}, bf16[352,128]{1,0:T(8,128)(2,1)S(1)}, u32[]{:S(2)}, u32[]{:S(2)}) %collective-permute-start.7) | collective-permute-done | bytes 90144 | tf_op jit(solution)/shard_map/ppermute | solution.py:248
  17.4 0.2 collective-permute-done.8.refs_6_
  17.6 0.4 %collective-permute-done.9.refs_7_ = bf16[352,128]{1,0:T(8,128)(2,1)S(1)} collective-permute-done((bf16[352,128]{1,0:T(8,128)(2,1)S(1)}, bf16[352,128]{1,0:T(8,128)(2,1)S(1)}, u32[]{:S(2)}, u32[]{:S(2)}) %collective-permute-start.9) | collective-permute-done | bytes 90144 | tf_op jit(solution)/shard_map/ppermute | solution.py:248
  18.0 2.6 %convolve.1 = (bf16[304,128]{1,0:T(8,128)(2,1)S(1)}, bf16[304,128]{1,0:T(8,128)(2,1)S(1)}, bf16[304,128]{1,0:T(8,128)(2,1)S(1)}, bf16[304,128]{1,0:T(8,128)(2,1)S(1)}) custom-call(s32[9]{0:T(128)S(4)} %get-tuple-element.28.offsets, f32[16,128]{1,0:T(8,128)S(1)} %get-tuple-element.26.filters, bf16[128,128]{1,0:T(8,128)(2,1)S(1)} %get-tuple-element.27.mix, ...), custom_call_target="tpu_custom_call" | custom-call | tf_op jit(solution)/shard_map/convolve/pallas_call | solution.py:235
  20.5 2.5 %collective-permute-start.10 = (bf16[304,128]{1,0:T(8,128)(2,1)S(1)}, bf16[304,128]{1,0:T(8,128)(2,1)S(1)}, u32[]{:S(2)}, u32[]{:S(2)}) collective-permute-start(bf16[304,128]{1,0:T(8,128)(2,1)S(1)} %get-tuple-element.35), channel_id=1, source_target_pairs={{0,12},{1,15},{2,14},{3,13},{4,8},{5,11},{6,10},{7,9},{8,4},{9,7},... | collective-permute-start | bytes 233480 | tf_op jit(solution)/shard_map/ppermute | solution.py:258
  23.1 0.0 collective-permute-start.11
  23.1 1.9 %collective-permute-start.12 = (bf16[304,128]{1,0:T(8,128)(2,1)S(1)}, bf16[304,128]{1,0:T(8,128)(2,1)S(1)}, u32[]{:S(2)}, u32[]{:S(2)}) collective-permute-start(bf16[304,128]{1,0:T(8,128)(2,1)S(1)} %get-tuple-element.37), channel_id=1, source_target_pairs={{0,4},{1,7},{2,6},{3,5},{4,0},{5,3},{6,2},{7,1},{8,12},{9,15},{10,... | collective-permute-start | bytes 233480 | tf_op jit(solution)/shard_map/ppermute | solution.py:258
  25.0 0.7 %collective-permute-start.13 = (bf16[304,128]{1,0:T(8,128)(2,1)S(1)}, bf16[304,128]{1,0:T(8,128)(2,1)S(1)}, u32[]{:S(2)}, u32[]{:S(2)}) collective-permute-start(bf16[304,128]{1,0:T(8,128)(2,1)S(1)} %get-tuple-element.38), channel_id=1, source_target_pairs={{0,0},{1,3},{2,2},{3,1},{4,4},{5,7},{6,6},{7,5},{8,8},{9,11},{10,1... | collective-permute-start | bytes 233480 | tf_op jit(solution)/shard_map/ppermute | solution.py:258
  25.7 2.0 %collective-permute-done.10.refs_0_ = bf16[304,128]{1,0:T(8,128)(2,1)S(1)} collective-permute-done((bf16[304,128]{1,0:T(8,128)(2,1)S(1)}, bf16[304,128]{1,0:T(8,128)(2,1)S(1)}, u32[]{:S(2)}, u32[]{:S(2)}) %collective-permute-start.10) | collective-permute-done | bytes 77856 | tf_op jit(solution)/shard_map/ppermute | solution.py:258
  27.7 0.7 %collective-permute-start.14 = (bf16[304,128]{1,0:T(8,128)(2,1)S(1)}, bf16[304,128]{1,0:T(8,128)(2,1)S(1)}, u32[]{:S(2)}, u32[]{:S(2)}) collective-permute-start(bf16[304,128]{1,0:T(8,128)(2,1)S(1)} %collective-permute-done.10.refs_0_), channel_id=1, source_target_pairs={{0,1},{1,0},{2,3},{3,2},{4,5},{5,4},{6,7},{7,6},{8,9},{9,8},{10,11... | collective-permute-start | bytes 233480 | tf_op jit(solution)/shard_map/ppermute | solution.py:248
  28.4 2.6 %collective-permute-done.11.refs_1_ = bf16[304,128]{1,0:T(8,128)(2,1)S(1)} collective-permute-done((bf16[304,128]{1,0:T(8,128)(2,1)S(1)}, bf16[304,128]{1,0:T(8,128)(2,1)S(1)}, u32[]{:S(2)}, u32[]{:S(2)}) %collective-permute-start.11) | collective-permute-done | bytes 77856 | tf_op jit(solution)/shard_map/ppermute | solution.py:258
  31.0 0.0 collective-permute-start.15
  31.0 0.0 collective-permute-done.12.refs_2_
  31.0 0.5 %collective-permute-start.16 = (bf16[304,128]{1,0:T(8,128)(2,1)S(1)}, bf16[304,128]{1,0:T(8,128)(2,1)S(1)}, u32[]{:S(2)}, u32[]{:S(2)}) collective-permute-start(bf16[304,128]{1,0:T(8,128)(2,1)S(1)} %collective-permute-done.12.refs_2_), channel_id=1, source_target_pairs={{0,1},{1,0},{2,3},{3,2},{4,5},{5,4},{6,7},{7,6},{8,9},{9,8},{10,11... | collective-permute-start | bytes 233480 | tf_op jit(solution)/shard_map/ppermute | solution.py:248
  31.5 0.0 collective-permute-done.13.refs_3_
  31.5 0.1 collective-permute-start.17
  31.5 0.0 collective-permute-done.14.refs_4_
  31.6 0.7 %collective-permute-done.15.refs_5_ = bf16[304,128]{1,0:T(8,128)(2,1)S(1)} collective-permute-done((bf16[304,128]{1,0:T(8,128)(2,1)S(1)}, bf16[304,128]{1,0:T(8,128)(2,1)S(1)}, u32[]{:S(2)}, u32[]{:S(2)}) %collective-permute-start.15) | collective-permute-done | bytes 77856 | tf_op jit(solution)/shard_map/ppermute | solution.py:248
  32.2 0.2 collective-permute-done.16.refs_6_
  32.4 0.4 %collective-permute-done.17.refs_7_ = bf16[304,128]{1,0:T(8,128)(2,1)S(1)} collective-permute-done((bf16[304,128]{1,0:T(8,128)(2,1)S(1)}, bf16[304,128]{1,0:T(8,128)(2,1)S(1)}, u32[]{:S(2)}, u32[]{:S(2)}) %collective-permute-start.17) | collective-permute-done | bytes 77856 | tf_op jit(solution)/shard_map/ppermute | solution.py:248
  32.8 1.1 %finish.1 = (bf16[8,64,128]{2,1,0:T(8,128)(2,1)}, bf16[8,64,128]{2,1,0:T(8,128)(2,1)}, f32[9,64]{1,0:T(8,128)}, f32[7,64]{1,0:T(8,128)}, f32[64,64]{1,0:T(8,128)}) custom-call(bf16[8,64,128]{2,1,0:T(8,128)(2,1)S(1)} %get-tuple-element.24.own_f.field, bf16[8,64,128]{2,1,0:T(8,128)(2,1)S(1)} %get-tuple-element.25.own_g.cot, ...), custom_call_target="tpu_custom_call" | custom-call | tf_op jit(solution)/shard_map/finish/pallas_call | solution.py:235
Async XLA Ops:
  0.6 1.7 %collective-permute-start = (bf16[8,64,128]{2,1,0:T(8,128)(2,1)}, bf16[8,64,128]{2,1,0:T(8,128)(2,1)S(1)}, u32[]{:S(2)}, u32[]{:S(2)}) collective-permute-start(bf16[8,64,128]{2,1,0:T(8,128)(2,1)} %field.1), channel_id=1, source_target_pairs={{0,1},{1,0},{2,3},{3,2},{4,5},{5,4},{6,7},{7,6},{8,9},{9,8},{10,11... | collective-permute-start | bytes 393224 | tf_op jit(solution)/shard_map/ppermute | solution.py:248
  1.2 1.6 %collective-permute-start.1 = (bf16[8,64,128]{2,1,0:T(8,128)(2,1)}, bf16[8,64,128]{2,1,0:T(8,128)(2,1)S(1)}, u32[]{:S(2)}, u32[]{:S(2)}) collective-permute-start(bf16[8,64,128]{2,1,0:T(8,128)(2,1)} %cot.1), channel_id=1, source_target_pairs={{0,1},{1,0},{2,3},{3,2},{4,5},{5,4},{6,7},{7,6},{8,9},{9,8},{10,11... | collective-permute-start | bytes 393224 | tf_op jit(solution)/shard_map/ppermute | solution.py:248
  2.9 8.0 %collective-permute-start.2 = (bf16[352,128]{1,0:T(8,128)(2,1)S(1)}, bf16[352,128]{1,0:T(8,128)(2,1)S(1)}, u32[]{:S(2)}, u32[]{:S(2)}) collective-permute-start(bf16[352,128]{1,0:T(8,128)(2,1)S(1)} %get-tuple-element.31), channel_id=1, source_target_pairs={{0,12},{1,15},{2,14},{3,13},{4,8},{5,11},{6,10},{7,9},{8,4},{9,7},... | collective-permute-start | bytes 270344 | tf_op jit(solution)/shard_map/ppermute | solution.py:258
  7.7 8.4 %collective-permute-start.3 = (bf16[352,128]{1,0:T(8,128)(2,1)S(1)}, bf16[352,128]{1,0:T(8,128)(2,1)S(1)}, u32[]{:S(2)}, u32[]{:S(2)}) collective-permute-start(bf16[352,128]{1,0:T(8,128)(2,1)S(1)} %get-tuple-element.32), channel_id=1, source_target_pairs={{0,8},{1,11},{2,10},{3,9},{4,12},{5,15},{6,14},{7,13},{8,0},{9,3},... | collective-permute-start | bytes 270344 | tf_op jit(solution)/shard_map/ppermute | solution.py:258
  7.7 8.4 %collective-permute-start.4 = (bf16[352,128]{1,0:T(8,128)(2,1)S(1)}, bf16[352,128]{1,0:T(8,128)(2,1)S(1)}, u32[]{:S(2)}, u32[]{:S(2)}) collective-permute-start(bf16[352,128]{1,0:T(8,128)(2,1)S(1)} %get-tuple-element.33), channel_id=1, source_target_pairs={{0,4},{1,7},{2,6},{3,5},{4,0},{5,3},{6,2},{7,1},{8,12},{9,15},{10,... | collective-permute-start | bytes 270344 | tf_op jit(solution)/shard_map/ppermute | solution.py:258
  8.4 8.3 %collective-permute-start.5 = (bf16[352,128]{1,0:T(8,128)(2,1)S(1)}, bf16[352,128]{1,0:T(8,128)(2,1)S(1)}, u32[]{:S(2)}, u32[]{:S(2)}) collective-permute-start(bf16[352,128]{1,0:T(8,128)(2,1)S(1)} %get-tuple-element.34), channel_id=1, source_target_pairs={{0,0},{1,3},{2,2},{3,1},{4,4},{5,7},{6,6},{7,5},{8,8},{9,11},{10,1... | collective-permute-start | bytes 270344 | tf_op jit(solution)/shard_map/ppermute | solution.py:258
  10.9 5.9 %collective-permute-start.6 = (bf16[352,128]{1,0:T(8,128)(2,1)S(1)}, bf16[352,128]{1,0:T(8,128)(2,1)S(1)}, u32[]{:S(2)}, u32[]{:S(2)}) collective-permute-start(bf16[352,128]{1,0:T(8,128)(2,1)S(1)} %collective-permute-done.2.refs_0_), channel_id=1, source_target_pairs={{0,1},{1,0},{2,3},{3,2},{4,5},{5,4},{6,7},{7,6},{8,9},{9,8},{10,11... | collective-permute-start | bytes 270344 | tf_op jit(solution)/shard_map/ppermute | solution.py:248
  16.1 1.3 %collective-permute-start.7 = (bf16[352,128]{1,0:T(8,128)(2,1)S(1)}, bf16[352,128]{1,0:T(8,128)(2,1)S(1)}, u32[]{:S(2)}, u32[]{:S(2)}) collective-permute-start(bf16[352,128]{1,0:T(8,128)(2,1)S(1)} %collective-permute-done.3.refs_1_), channel_id=1, source_target_pairs={{0,1},{1,0},{2,3},{3,2},{4,5},{5,4},{6,7},{7,6},{8,9},{9,8},{10,11... | collective-permute-start | bytes 270344 | tf_op jit(solution)/shard_map/ppermute | solution.py:248
  16.2 1.4 %collective-permute-start.8 = (bf16[352,128]{1,0:T(8,128)(2,1)S(1)}, bf16[352,128]{1,0:T(8,128)(2,1)S(1)}, u32[]{:S(2)}, u32[]{:S(2)}) collective-permute-start(bf16[352,128]{1,0:T(8,128)(2,1)S(1)} %collective-permute-done.4.refs_2_), channel_id=1, source_target_pairs={{0,1},{1,0},{2,3},{3,2},{4,5},{5,4},{6,7},{7,6},{8,9},{9,8},{10,11... | collective-permute-start | bytes 270344 | tf_op jit(solution)/shard_map/ppermute | solution.py:248
  16.7 1.3 %collective-permute-start.9 = (bf16[352,128]{1,0:T(8,128)(2,1)S(1)}, bf16[352,128]{1,0:T(8,128)(2,1)S(1)}, u32[]{:S(2)}, u32[]{:S(2)}) collective-permute-start(bf16[352,128]{1,0:T(8,128)(2,1)S(1)} %collective-permute-done.5.refs_3_), channel_id=1, source_target_pairs={{0,1},{1,0},{2,3},{3,2},{4,5},{5,4},{6,7},{7,6},{8,9},{9,8},{10,11... | collective-permute-start | bytes 270344 | tf_op jit(solution)/shard_map/ppermute | solution.py:248
  20.5 7.2 %collective-permute-start.10 = (bf16[304,128]{1,0:T(8,128)(2,1)S(1)}, bf16[304,128]{1,0:T(8,128)(2,1)S(1)}, u32[]{:S(2)}, u32[]{:S(2)}) collective-permute-start(bf16[304,128]{1,0:T(8,128)(2,1)S(1)} %get-tuple-element.35), channel_id=1, source_target_pairs={{0,12},{1,15},{2,14},{3,13},{4,8},{5,11},{6,10},{7,9},{8,4},{9,7},... | collective-permute-start | bytes 233480 | tf_op jit(solution)/shard_map/ppermute | solution.py:258
  23.1 7.9 %collective-permute-start.11 = (bf16[304,128]{1,0:T(8,128)(2,1)S(1)}, bf16[304,128]{1,0:T(8,128)(2,1)S(1)}, u32[]{:S(2)}, u32[]{:S(2)}) collective-permute-start(bf16[304,128]{1,0:T(8,128)(2,1)S(1)} %get-tuple-element.36), channel_id=1, source_target_pairs={{0,8},{1,11},{2,10},{3,9},{4,12},{5,15},{6,14},{7,13},{8,0},{9,3},... | collective-permute-start | bytes 233480 | tf_op jit(solution)/shard_map/ppermute | solution.py:258
  23.1 7.9 %collective-permute-start.12 = (bf16[304,128]{1,0:T(8,128)(2,1)S(1)}, bf16[304,128]{1,0:T(8,128)(2,1)S(1)}, u32[]{:S(2)}, u32[]{:S(2)}) collective-permute-start(bf16[304,128]{1,0:T(8,128)(2,1)S(1)} %get-tuple-element.37), channel_id=1, source_target_pairs={{0,4},{1,7},{2,6},{3,5},{4,0},{5,3},{6,2},{7,1},{8,12},{9,15},{10,... | collective-permute-start | bytes 233480 | tf_op jit(solution)/shard_map/ppermute | solution.py:258
  25.0 6.5 %collective-permute-start.13 = (bf16[304,128]{1,0:T(8,128)(2,1)S(1)}, bf16[304,128]{1,0:T(8,128)(2,1)S(1)}, u32[]{:S(2)}, u32[]{:S(2)}) collective-permute-start(bf16[304,128]{1,0:T(8,128)(2,1)S(1)} %get-tuple-element.38), channel_id=1, source_target_pairs={{0,0},{1,3},{2,2},{3,1},{4,4},{5,7},{6,6},{7,5},{8,8},{9,11},{10,1... | collective-permute-start | bytes 233480 | tf_op jit(solution)/shard_map/ppermute | solution.py:258
  27.7 3.9 %collective-permute-start.14 = (bf16[304,128]{1,0:T(8,128)(2,1)S(1)}, bf16[304,128]{1,0:T(8,128)(2,1)S(1)}, u32[]{:S(2)}, u32[]{:S(2)}) collective-permute-start(bf16[304,128]{1,0:T(8,128)(2,1)S(1)} %collective-permute-done.10.refs_0_), channel_id=1, source_target_pairs={{0,1},{1,0},{2,3},{3,2},{4,5},{5,4},{6,7},{7,6},{8,9},{9,8},{10,11... | collective-permute-start | bytes 233480 | tf_op jit(solution)/shard_map/ppermute | solution.py:248
  31.0 1.3 %collective-permute-start.15 = (bf16[304,128]{1,0:T(8,128)(2,1)S(1)}, bf16[304,128]{1,0:T(8,128)(2,1)S(1)}, u32[]{:S(2)}, u32[]{:S(2)}) collective-permute-start(bf16[304,128]{1,0:T(8,128)(2,1)S(1)} %collective-permute-done.11.refs_1_), channel_id=1, source_target_pairs={{0,1},{1,0},{2,3},{3,2},{4,5},{5,4},{6,7},{7,6},{8,9},{9,8},{10,11... | collective-permute-start | bytes 233480 | tf_op jit(solution)/shard_map/ppermute | solution.py:248
  31.0 1.4 %collective-permute-start.16 = (bf16[304,128]{1,0:T(8,128)(2,1)S(1)}, bf16[304,128]{1,0:T(8,128)(2,1)S(1)}, u32[]{:S(2)}, u32[]{:S(2)}) collective-permute-start(bf16[304,128]{1,0:T(8,128)(2,1)S(1)} %collective-permute-done.12.refs_2_), channel_id=1, source_target_pairs={{0,1},{1,0},{2,3},{3,2},{4,5},{5,4},{6,7},{7,6},{8,9},{9,8},{10,11... | collective-permute-start | bytes 233480 | tf_op jit(solution)/shard_map/ppermute | solution.py:248
  31.5 1.3 %collective-permute-start.17 = (bf16[304,128]{1,0:T(8,128)(2,1)S(1)}, bf16[304,128]{1,0:T(8,128)(2,1)S(1)}, u32[]{:S(2)}, u32[]{:S(2)}) collective-permute-start(bf16[304,128]{1,0:T(8,128)(2,1)S(1)} %collective-permute-done.13.refs_3_), channel_id=1, source_target_pairs={{0,1},{1,0},{2,3},{3,2},{4,5},{5,4},{6,7},{7,6},{8,9},{9,8},{10,11... | collective-permute-start | bytes 233480 | tf_op jit(solution)/shard_map/ppermute | solution.py:248

commit v3 on v2

--- a/solution.py
+++ b/solution.py
@@ -69,8 +69,28 @@
             ref[...] = stage[i]
 
 
-def partner(rounds, i, side):
-    return 2 * (rounds - 1 - i) + side
+def unpack(tags, refs, stage, core, take):
+    if stage is None:
+        for (at, swapped), ref in zip(tags, refs):
+            take(at, core ^ swapped, ref)
+        return
+    half = len(refs) // 2
+    for swapped in range(2):
+        visit(
+            refs[swapped * half : (swapped + 1) * half],
+            stage,
+            lambda i, ref, side=core ^ swapped: take(half - 1 - i, side, ref),
+        )
+
+
+def partner(rounds, at, side):
+    return 2 * at + (side ^ (at == rounds - 1) ^ (at == 1))
+
+
+def arrivals(rounds):
+    if rounds == 4:
+        return [[(3, 0), (1, 0)], [(2, 0), (0, 0), (3, 1), (1, 1)], [(2, 1), (0, 1)]]
+    return [[(at, swapped) for swapped in range(2) for at in reversed(range(rounds))]]
 
 
 def pack(rounds, own_f, own_g, other_f, other_g, *refs):
@@ -87,7 +107,7 @@
         cots[pl.ds(side * near, near)] = g[...].astype(F32)
     body = 2 * near * ROWS
 
-    def step_(i, out):
+    def fill(i, out):
         to = chip ^ partner(rounds, i, core)
         first = pl.multiple_of(to * ROWS, ROWS)
         center = wide[:, pl.ds(pl.multiple_of(first + ROWS, ROWS), ROWS), :]
@@ -99,46 +119,63 @@
         at = body + 2 * HALO * 2 * near
         out[at : at + body, :] = cots[:, pl.ds(first, ROWS), :].reshape(body, feat).astype(BF16)
 
-    visit(outs, stage[0] if stage else None, step_, fill=True)
-
-
-def convolve(rounds, taps, rtaps, channels, offsets, filters, mix, *refs):
-    blocks, outs = refs[: 2 * rounds], refs[2 * rounds : 3 * rounds]
-    fields, radial, grads, cots, hidden, spread, *stage = refs[3 * rounds :]
+    visit(outs, stage[0] if stage else None, fill, fill=True)
+
+
+def receive(tags, rounds, taps, rtaps, filters, mix, blocks, state, stage):
+    fields, radial, grads, cots = state
     chip, core = place()
-    azim = radial.shape[0] // 2
-    feat = mix.shape[0]
+    azim, feat = radial.shape[0] // 2, mix.shape[0]
     step = 2 * ROWS
     wide = fields.reshape(azim, step, feat)
     near = azim // (2 * rounds)
     body = near * ROWS
-    weight = [jnp.broadcast_to(filters[k : k + 1, :], (ROWS, feat)) for k in range(taps + rtaps)]
-    def take(side, i, block):
-        source = chip ^ partner(rounds, i, side)
-        first = source * near
+    weight = [jnp.broadcast_to(filters[taps + j : taps + j + 1, :], (ROWS, feat)) for j in range(rtaps)]
+
+    def take(at, side, block):
+        first = (chip ^ partner(rounds, at, side)) * near
         wide[pl.ds(first, near), HALO : HALO + ROWS, :] = (
             block[0:body, :].astype(F32).reshape(near, ROWS, feat)
         )
         for h in range(2 * HALO):
             row = h if h < HALO else ROWS + h
-            at = body + h * near
+            start = body + h * near
             fields[pl.ds(first * step + row, near, stride=step), :] = block[
-                at : at + near, :
+                start : start + near, :
             ].astype(F32)
-        at = body + 2 * HALO * near
-        cot = block[at : at + body, :]
+        start = body + 2 * HALO * near
+        cot = block[start : start + body, :]
         cots[pl.ds(pl.multiple_of(first * ROWS, body), body), :] = cot
         back = lax.dot_general(cot, mix[...], (((1,), (1,)), ((), ())), preferred_element_type=F32)
         back = back.astype(BF16).astype(F32).reshape(near, ROWS, feat)
         grads[pl.ds(first, near)] = back
         grads[pl.ds(azim + first, near)] = back
-        total = weight[taps] * wide[pl.ds(first, near), 0:ROWS, :]
+        total = weight[0] * wide[pl.ds(first, near), 0:ROWS, :]
         for j in range(1, rtaps):
-            total = total + weight[taps + j] * wide[pl.ds(first, near), j : j + ROWS, :]
+            total = total + weight[j] * wide[pl.ds(first, near), j : j + ROWS, :]
         radial[pl.ds(first, near)] = total
         radial[pl.ds(azim + first, near)] = total
-    for side, group in ((core, blocks[:rounds]), (1 - core, blocks[rounds:])):
-        visit(group, stage[0] if stage else None, functools.partial(take, side))
+
+    unpack(tags, blocks, stage[0] if stage else None, core, take)
+
+
+def receive_some(tags, rounds, taps, rtaps, old, filters, mix, *refs):
+    receive(tags, rounds, taps, rtaps, filters, mix, refs[: len(tags)], refs[len(tags) + old :], ())
+
+
+def convolve(tags, rounds, taps, rtaps, channels, old, offsets, filters, mix, *refs):
+    blocks, state = refs[: len(tags)], refs[len(tags) : len(tags) + old]
+    outs, rest = refs[len(tags) + old :][:rounds], refs[len(tags) + old + rounds :]
+    if not old:
+        state, rest = rest[:4], rest[4:]
+    hidden, spread, *stage = rest
+    fields, radial, grads, cots = state
+    receive(tags, rounds, taps, rtaps, filters, mix, blocks, state, stage)
+    chip, core = place()
+    azim, feat = radial.shape[0] // 2, mix.shape[0]
+    wide = fields.reshape(azim, 2 * ROWS, feat)
+    body = azim // (2 * rounds) * ROWS
+    weight = [jnp.broadcast_to(filters[k : k + 1, :], (ROWS, feat)) for k in range(taps)]
     ahead = [lax.rem(offsets[k] + azim, azim) for k in range(taps)]
     behind = [lax.rem(azim - offsets[k], azim) for k in range(taps)]
 
@@ -163,7 +200,7 @@
         return tuple(sums)
 
     zero = jnp.zeros((ROWS, feat), F32)
-    sums = lax.fori_loop(0, azim // SLAB, slab, (zero,) * (taps + rtaps))
+    sums = lax.fori_loop(0, azim // SLAB, slab, (zero,) * (taps + rtaps), unroll=2)
     product = lax.dot_general(
         hidden[...], cots[...], (((0,), (0,)), ((), ())), preferred_element_type=F32
     )
@@ -185,40 +222,67 @@
         out[2 * body : 2 * body + part.shape[0], :] = part
 
 
-def finish(rounds, taps, rtaps, scale, field, cot, filters, mix, *refs):
-    blocks = refs[: 2 * rounds]
-    out, grad, azimuth_out, radial_out, mixing_out, hidden, spread, summed, *stage = refs[2 * rounds :]
+def collect(tags, rounds, blocks, state, stage):
+    hidden, spread, summed = state
     chip, core = place()
+    near, feat = hidden.shape[0], hidden.shape[2]
+    body = near * ROWS
+    mine = pl.multiple_of(core * body, body)
+
+    def take(at, side, block):
+        first = pl.multiple_of((chip ^ partner(rounds, at, side)) * ROWS, ROWS)
+        hidden[:, pl.ds(first, ROWS), :] = (
+            block[pl.ds(mine, body), :].astype(F32).reshape(near, ROWS, feat)
+        )
+        spread[:, pl.ds(pl.multiple_of(first + ROWS, ROWS), ROWS), :] = (
+            block[pl.ds(2 * body + mine, body), :].astype(F32).reshape(near, ROWS, feat)
+        )
+        summed[...] += block[4 * body : 4 * body + summed.shape[0], :].astype(F32)
+
+    unpack(tags, blocks, stage[0] if stage else None, core, take)
+
+
+def clear(state):
+    hidden, spread, summed = state
+    near, rad, feat = hidden.shape
+    spread[:, 0:ROWS, :] = jnp.zeros((near, ROWS, feat), F32)
+    spread[:, ROWS + rad :, :] = jnp.zeros((near, ROWS, feat), F32)
+    summed[...] = jnp.zeros(summed.shape, F32)
+
+
+def collect_some(tags, rounds, old, *refs):
+    state = refs[len(tags) + old :]
+    if not old:
+        clear(state)
+    collect(tags, rounds, refs[: len(tags)], state, ())
+
+
+def finish(tags, rounds, taps, rtaps, scale, old, field, cot, filters, mix, *refs):
+    blocks, state = refs[: len(tags)], refs[len(tags) : len(tags) + old]
+    targets, rest = refs[len(tags) + old :][:5], refs[len(tags) + old + 5 :]
+    if not old:
+        state, rest = rest[:3], rest[3:]
+        clear(state)
+    hidden, spread, summed = state
+    out, grad, azimuth_out, radial_out, mixing_out, sems, *stage = rest
+    collect(tags, rounds, blocks, state, stage)
     near, rad, feat = field.shape
     channels = azimuth_out.shape[1]
-    body = near * ROWS
-    spread[:, 0:ROWS, :] = jnp.zeros((near, ROWS, feat), F32)
-    spread[:, ROWS + rad :, :] = jnp.zeros((near, ROWS, feat), F32)
+    sources = (out, grad, azimuth_out, radial_out, mixing_out)
+    copies = [pltpu.make_async_copy(*pair, sems.at[i]) for i, pair in enumerate(zip(sources, targets))]
     few, half = (taps + rtaps) // 2, channels // 2
-    mine = pl.multiple_of(core * body, body)
-    summed[...] = jnp.zeros(summed.shape, F32)
-
-    def take(side, i, block):
-        first = pl.multiple_of((chip ^ partner(rounds, i, side)) * ROWS, ROWS)
-        hidden[:, pl.ds(first, ROWS), :] = (
-            block[pl.ds(mine, body), :].astype(F32).reshape(near, ROWS, feat)
-        )
-        spread[:, pl.ds(pl.multiple_of(first + ROWS, ROWS), ROWS), :] = (
-            block[pl.ds(2 * body + mine, body), :].astype(F32).reshape(near, ROWS, feat)
-        )
-        summed[...] += block[4 * body : 4 * body + summed.shape[0], :].astype(F32)
-
-    for side, group in ((core, blocks[:rounds]), (1 - core, blocks[rounds:])):
-        visit(group, stage[0] if stage else None, functools.partial(take, side))
     part = summed[0 : few + half, :] * scale
     azimuth_out[0:few, :] = part[0:few, 0:channels]
     azimuth_out[few:taps, :] = part[0 : taps - few, channels:feat]
     radial_out[...] = part[taps - few : few, channels:feat]
     mixing_out[0:half, :] = part[few : few + half, 0:channels]
     mixing_out[half:channels, :] = part[few : few + half, channels:feat]
+    for copy in copies[2:]:
+        copy.start()
     flat = hidden[...].reshape(near * rad, feat).astype(BF16)
     mixed = jnp.dot(flat, mix[...], preferred_element_type=F32).reshape(near, rad, feat)
     out[...] = (field[...].astype(F32) + mixed).astype(BF16)
+    copies[0].start()
     total = jnp.zeros((near, rad, feat), F32)
     for j in range(rtaps):
         weight = jnp.broadcast_to(filters[taps + j : taps + j + 1, :], (rad, feat))
@@ -226,9 +290,12 @@
         total = total + weight * spread[:, first : first + rad, :]
     branch = total.astype(BF16).astype(F32)
     grad[...] = (cot[...].astype(F32) + branch).astype(BF16)
-
-
-def call(kernel, ins, outs, scratch, keep=False, name=None):
+    copies[1].start()
+    for copy in copies:
+        copy.wait()
+
+
+def call(kernel, ins, outs, scratch, old=0, name=None):
     ins = [
         pltpu.with_memory_space_constraint(x, pltpu.VMEM if x.ndim > 1 else pltpu.SMEM) for x in ins
     ]
@@ -236,8 +303,9 @@
         kernel,
         in_specs=[VMEM if x.ndim > 1 else SMEM for x in ins],
         out_specs=[VMEM] * len(outs),
-        out_shape=[(pltpu.VMEM if keep else jax.ShapeDtypeStruct)(*out) for out in outs],
+        out_shape=[pltpu.VMEM(*out) for out in outs],
         scratch_shapes=[pltpu.VMEM(*out) for out in scratch],
+        input_output_aliases={len(ins) - old + i: i for i in range(old)},
         compiler_params=PARAMS,
         name=name,
     )(*ins)
@@ -248,15 +316,24 @@
     return lax.ppermute(x, "az", [(i, i ^ 1) for i in range(size)])
 
 
-def exchange(messages):
-    chips = lax.axis_size("az") // 2
-    got = []
-    for i, message in enumerate(messages):
-        pairs = [
-            (2 * c + k, 2 * (c ^ partner(len(messages), i, k)) + k) for c in range(chips) for k in range(2)
-        ]
-        got.append(lax.ppermute(message, "az", pairs))
-    return got + [swap(x) for x in got]
+def exchange(messages, unpacked, empty):
+    rounds, chips = len(messages), lax.axis_size("az") // 2
+    blocks = {}
+    for at in reversed(range(rounds)):
+        pairs = [(2 * c + k, 2 * (c ^ partner(rounds, at, k)) + k) for c in range(chips) for k in range(2)]
+        blocks[at, 0] = lax.ppermute(messages[at], "az", pairs)
+    groups, state = arrivals(rounds), []
+    for group in groups:
+        fresh = [tag for tag in group if not tag[1]]
+        if state:
+            tied = lax.optimization_barrier(([blocks[tag] for tag in fresh], state))
+            state = list(tied[1])
+            blocks.update(zip(fresh, tied[0]))
+        for at, _ in fresh:
+            blocks[at, 1] = swap(blocks[at, 0])
+        if group is not groups[-1]:
+            state = list(unpacked(group, [blocks[tag] for tag in group], state, empty))
+    return groups[-1], [blocks[tag] for tag in groups[-1]], state
 
 
 def local(fields, cotangent, azimuth_filter, radial_filter, mixing, tap_offsets):
@@ -294,46 +371,72 @@
     )
     body = 2 * near * ROWS
     length = 2 * body + 2 * HALO * 2 * near
-    message = ((length, feat), BF16)
     messages = call(
         functools.partial(pack, rounds),
         (fields, cotangent, other_f, other_g),
-        [message] * rounds,
+        [((length, feat), BF16)] * rounds,
         [((2 * near * (rad + 2 * ROWS), feat), F32), ((2 * near, rad, feat), F32)]
         + [((rounds, length, feat), BF16)] * many,
-        keep=True,
         name="pack",
     )
-    blocks = exchange(messages)
+
+    def receiver(tags, blocks, state, empty):
+        return call(
+            functools.partial(receive_some, tags, rounds, taps, rtaps, len(state)),
+            (filters, mix, *blocks, *state),
+            empty,
+            [],
+            old=len(state),
+            name="receive",
+        )
+
+    flat = ((azim * ROWS, feat), BF16)
+    twice = ((2 * azim, ROWS, feat), F32)
+    empty = [((azim * 2 * ROWS, feat), F32), twice, twice, flat]
+    tags, blocks, state = exchange(messages, receiver, empty)
     sums = (taps + rtaps + channels) // 2 + 8
-    flat = ((azim * ROWS, feat), BF16)
     messages = call(
-        functools.partial(convolve, rounds, taps, rtaps, channels),
-        (tap_offsets, filters, mix, *blocks),
+        functools.partial(convolve, tags, rounds, taps, rtaps, channels, len(state)),
+        (tap_offsets, filters, mix, *blocks, *state),
         [((2 * body + sums, feat), BF16)] * rounds,
-        [((azim * 2 * ROWS, feat), F32)]
-        + [((2 * azim, ROWS, feat), F32)] * 2
-        + [flat] * 3
+        ([] if state else empty)
+        + [flat, flat]
         + [((rounds, length, feat), BF16)] * many,
-        keep=True,
         name="convolve",
     )
-    blocks = exchange(messages)
+
+    def collector(tags, blocks, state, empty):
+        return call(
+            functools.partial(collect_some, tags, rounds, len(state)),
+            (*blocks, *state),
+            empty,
+            [],
+            old=len(state),
+            name="collect",
+        )
+
+    empty = [((near, rad, feat), F32), ((near, rad + 2 * ROWS, feat), F32), ((sums, feat), F32)]
+    tags, blocks, state = exchange(messages, collector, empty)
     scale = 1.0 / math.sqrt(azim * rad * (feat // channels))
-    return call(
-        functools.partial(finish, rounds, taps, rtaps, scale),
-        (fields, cotangent, filters, mix, *blocks),
-        [
-            (fields.shape, BF16),
-            (fields.shape, BF16),
-            ((taps, channels), F32),
-            ((rtaps, channels), F32),
-            ((channels, channels), F32),
-        ],
-        [((near, rad, feat), F32), ((near, rad + 2 * ROWS, feat), F32), ((sums, feat), F32)]
-        + [((rounds, 2 * body + sums, feat), BF16)] * many,
+    ins = (fields, cotangent, filters, mix, *blocks, *state)
+    outs = [
+        (fields.shape, BF16),
+        (fields.shape, BF16),
+        ((taps, channels), F32),
+        ((rtaps, channels), F32),
+        ((channels, channels), F32),
+    ]
+    return pl.pallas_call(
+        functools.partial(finish, tags, rounds, taps, rtaps, scale, len(state)),
+        in_specs=[VMEM] * len(ins),
+        out_specs=[pl.BlockSpec(memory_space=pltpu.HBM)] * len(outs),
+        out_shape=[jax.ShapeDtypeStruct(*out) for out in outs],
+        scratch_shapes=[pltpu.VMEM(*out) for out in ([] if state else empty) + outs]
+        + [pltpu.SemaphoreType.DMA((len(outs),))]
+        + [pltpu.VMEM((rounds, 2 * body + sums, feat), BF16)] * many,
+        compiler_params=PARAMS,
         name="finish",
-    )
+    )(*(pltpu.with_memory_space_constraint(x, pltpu.VMEM) for x in ins))
 
 
 def solution(mesh):

time: 34 us -> 32.2 us (0.947)
  waiting for transfers between devices: 13.2 us -> 11.5 us
    ppermute x10, starting transfers between devices: 3.78 us -> 1.63 us  [swap(): return lax.ppermute(x, 'az', [(i, i ^ 1) for i in range(size)])]
    ppermute x8, starting transfers between devices: 11.2 us -> 13.1 us  [exchange(): blocks[at, 0] = lax.ppermute(messages[at], 'az', pairs)]
    pallas_call x0 -> x1, Pallas kernels: none -> 1.08 us  [local(): pl.pallas_call(functools.partial(finish, tags, rounds, taps, rtaps, scale...]
    ppermute x8, waiting for transfers between devices: 10.4 us -> 9.46 us  [exchange(): blocks[at, 0] = lax.ppermute(messages[at], 'az', pairs)]
    pallas_call x3 -> x6, Pallas kernels: 3.8 us -> 2.92 us  [call(): pl.pallas_call(kernel, in_specs=[VMEM if x.ndim > 1 else SMEM for x in in...]
    ppermute x10, waiting for transfers between devices: 2.82 us -> 2 us  [swap(): return lax.ppermute(x, 'az', [(i, i ^ 1) for i in range(size)])]
  transfers between devices with their start and end apart: 18 -> 18, of which waited for: 11 -> 12; matrix products, arithmetic and copies ran while one was open for 0% -> 0% of each run, Pallas kernels for 3% -> 5%
where the time goes in v3:
time: 32.2 us; the launch traced here: 32 us
  starting transfers between devices  14.7 us (46%)
  waiting for transfers between devices  11.5 us (36%)
  Pallas kernels  5.07 us (16%)
  between operations  0.72 us (2%)
    ppermute x8, starting transfers between devices, exchange(): blocks[at, 0] = lax.ppermute(messages[at], 'az', pairs)  13.1 us
    ppermute x8, waiting for transfers between devices, exchange(): blocks[at, 0] = lax.ppermute(messages[at], 'az', pairs)  9.46 us
    pallas_call x6, Pallas kernels, call(): pl.pallas_call(kernel, in_specs=[VMEM if x.ndim > 1 else SMEM for x in in...  2.92 us
    ppermute x10, waiting for transfers between devices, swap(): return lax.ppermute(x, 'az', [(i, i ^ 1) for i in range(size)])  2 us
    ppermute x10, starting transfers between devices, swap(): return lax.ppermute(x, 'az', [(i, i ^ 1) for i in range(size)])  1.63 us
    pallas_call x1, Pallas kernels, local(): pl.pallas_call(functools.partial(finish, tags, rounds, taps, rtaps, scale...  1.08 us
    pallas_call x1, Pallas kernels, local(): pl.pallas_call(gather, in_specs=[pl.BlockSpec(memory_space=pltpu.HBM)] *...  1.07 us
  transfers between devices with their start and end apart: 18, of which 12 were waited for; matrix products, arithmetic and copies ran while one was open for 0% of the time, Pallas kernels for 5%

profile of v3, /device:TPU:0, one launch (start us, length us, event | category | flops | bytes accessed | tf_op | source)
XLA Modules:
  0.0 32.0 jit_solution(18044221280895311049)
XLA Ops:
  0.6 0.5 %collective-permute-start = (bf16[8,64,128]{2,1,0:T(8,128)(2,1)}, bf16[8,64,128]{2,1,0:T(8,128)(2,1)S(1)}, u32[]{:S(2)}, u32[]{:S(2)}) collective-permute-start(bf16[8,64,128]{2,1,0:T(8,128)(2,1)} %field.1), channel_id=1, source_target_pairs={{0,1},{1,0},{2,3},{3,2},{4,5},{5,4},{6,7},{7,6},{8,9},{9,8},{10,11... | collective-permute-start | bytes 393224 | tf_op jit(solution)/shard_map/ppermute | solution.py:316
  1.2 0.1 collective-permute-start.1
  1.2 1.1 %gather.1 = (bf16[8,64,128]{2,1,0:T(8,128)(2,1)S(1)}, bf16[8,64,128]{2,1,0:T(8,128)(2,1)S(1)}, f32[16,128]{1,0:T(8,128)S(1)}, bf16[128,128]{1,0:T(8,128)(2,1)S(1)}, s32[9]{0:T(128)S(4)}) custom-call(bf16[8,64,128]{2,1,0:T(8,128)(2,1)} %field.1, bf16[8,64,128]{2,1,0:T(8,128)(2,1)} %cot.1, f32[9,64]{1,0:T(8,128)} %azimuth.1, f32[7,64]{1,0:T(8,128)} %radial.1, ...), custom_call_target="tpu_custom_call" | custom-call | tf_op jit(solution)/shard_map/gather/pallas_call | solution.py:355
  2.3 0.0 collective-permute-done.other_f
  2.3 0.4 %collective-permute-done.1.other_g = bf16[8,64,128]{2,1,0:T(8,128)(2,1)S(1)} collective-permute-done((bf16[8,64,128]{2,1,0:T(8,128)(2,1)}, bf16[8,64,128]{2,1,0:T(8,128)(2,1)S(1)}, u32[]{:S(2)}, u32[]{:S(2)}) %collective-permute-start.1) | collective-permute-done | bytes 131104 | tf_op jit(solution)/shard_map/ppermute | solution.py:316
  2.7 0.2 pack.1
  2.9 5.8 %collective-permute-start.4 = (bf16[352,128]{1,0:T(8,128)(2,1)S(1)}, bf16[352,128]{1,0:T(8,128)(2,1)S(1)}, u32[]{:S(2)}, u32[]{:S(2)}) collective-permute-start(bf16[352,128]{1,0:T(8,128)(2,1)S(1)} %get-tuple-element.58), channel_id=1, source_target_pairs={{0,14},{1,13},{2,12},{3,15},{4,10},{5,9},{6,8},{7,11},{8,6},{9,5},... | collective-permute-start | bytes 270344 | tf_op jit(solution)/shard_map/ppermute | solution.py:324
  8.7 0.0 collective-permute-start.5
  8.7 0.6 %collective-permute-start.2 = (bf16[352,128]{1,0:T(8,128)(2,1)S(1)}, bf16[352,128]{1,0:T(8,128)(2,1)S(1)}, u32[]{:S(2)}, u32[]{:S(2)}) collective-permute-start(bf16[352,128]{1,0:T(8,128)(2,1)S(1)} %get-tuple-element.56), channel_id=1, source_target_pairs={{0,8},{1,11},{2,10},{3,9},{4,12},{5,15},{6,14},{7,13},{8,0},{9,3},... | collective-permute-start | bytes 270344 | tf_op jit(solution)/shard_map/ppermute | solution.py:324
  9.3 0.7 %collective-permute-start.3 = (bf16[352,128]{1,0:T(8,128)(2,1)S(1)}, bf16[352,128]{1,0:T(8,128)(2,1)S(1)}, u32[]{:S(2)}, u32[]{:S(2)}) collective-permute-start(bf16[352,128]{1,0:T(8,128)(2,1)S(1)} %get-tuple-element.57), channel_id=1, source_target_pairs={{0,0},{1,3},{2,2},{3,1},{4,4},{5,7},{6,6},{7,5},{8,8},{9,11},{10,1... | collective-permute-start | bytes 270344 | tf_op jit(solution)/shard_map/ppermute | solution.py:324
  10.0 2.1 %collective-permute-done.4.refs_0_ = bf16[352,128]{1,0:T(8,128)(2,1)S(1)} collective-permute-done((bf16[352,128]{1,0:T(8,128)(2,1)S(1)}, bf16[352,128]{1,0:T(8,128)(2,1)S(1)}, u32[]{:S(2)}, u32[]{:S(2)}) %collective-permute-start.4) | collective-permute-done | bytes 90144 | tf_op jit(solution)/shard_map/ppermute | solution.py:324
  12.1 0.0 collective-permute-start.8
  12.1 2.8 %collective-permute-done.5.refs_1_ = bf16[352,128]{1,0:T(8,128)(2,1)S(1)} collective-permute-done((bf16[352,128]{1,0:T(8,128)(2,1)S(1)}, bf16[352,128]{1,0:T(8,128)(2,1)S(1)}, u32[]{:S(2)}, u32[]{:S(2)}) %collective-permute-start.5) | collective-permute-done | bytes 90144 | tf_op jit(solution)/shard_map/ppermute | solution.py:324
  14.9 0.0 collective-permute-start.9
  14.9 0.2 receive.2
  15.1 1.0 %collective-permute-done.2.refs_0_ = bf16[352,128]{1,0:T(8,128)(2,1)S(1)} collective-permute-done((bf16[352,128]{1,0:T(8,128)(2,1)S(1)}, bf16[352,128]{1,0:T(8,128)(2,1)S(1)}, u32[]{:S(2)}, u32[]{:S(2)}) %collective-permute-start.2) | collective-permute-done | bytes 90144 | tf_op jit(solution)/shard_map/ppermute | solution.py:324
  16.1 0.0 collective-permute-done.3.refs_1_
  16.1 0.0 collective-permute-start.6
  16.1 0.5 %collective-permute-start.7 = (bf16[352,128]{1,0:T(8,128)(2,1)S(1)}, bf16[352,128]{1,0:T(8,128)(2,1)S(1)}, u32[]{:S(2)}, u32[]{:S(2)}) collective-permute-start(bf16[352,128]{1,0:T(8,128)(2,1)S(1)} %collective-permute-done.3.refs_1_), channel_id=1, source_target_pairs={{0,1},{1,0},{2,3},{3,2},{4,5},{5,4},{6,7},{7,6},{8,9},{9,8},{10,11... | collective-permute-start | bytes 270344 | tf_op jit(solution)/shard_map/ppermute | solution.py:316
  16.6 0.0 collective-permute-done.8.refs_2_
  16.6 0.0 collective-permute-done.9.refs_3_
  16.6 0.4 %receive.3 = (f32[2048,128]{1,0:T(8,128)S(1)}, f32[256,8,128]{2,1,0:T(8,128)S(1)}, f32[256,8,128]{2,1,0:T(8,128)S(1)}, bf16[1024,128]{1,0:T(8,128)(2,1)S(1)}) custom-call(f32[16,128]{1,0:T(8,128)S(1)} %get-tuple-element.51.filters, ...), custom_call_target="tpu_custom_call", output_to_operand_aliasing={{0}: (6, {}), {1}: (7, {}), {2}: (8, {}), {3}: (9, {})} | custom-call | tf_op jit(solution)/shard_map/receive/pallas_call | solution.py:302
  17.0 0.4 %collective-permute-done.6.refs_0_ = bf16[352,128]{1,0:T(8,128)(2,1)S(1)} collective-permute-done((bf16[352,128]{1,0:T(8,128)(2,1)S(1)}, bf16[352,128]{1,0:T(8,128)(2,1)S(1)}, u32[]{:S(2)}, u32[]{:S(2)}) %collective-permute-start.6) | collective-permute-done | bytes 90144 | tf_op jit(solution)/shard_map/ppermute | solution.py:316
  17.4 0.2 collective-permute-done.7.refs_1_
  17.5 2.0 %convolve.1 = (bf16[304,128]{1,0:T(8,128)(2,1)S(1)}, bf16[304,128]{1,0:T(8,128)(2,1)S(1)}, bf16[304,128]{1,0:T(8,128)(2,1)S(1)}, bf16[304,128]{1,0:T(8,128)(2,1)S(1)}) custom-call(s32[9]{0:T(128)S(4)} %get-tuple-element.53.offsets, f32[16,128]{1,0:T(8,128)S(1)} %get-tuple-element.51.filters, bf16[128,128]{1,0:T(8,128)(2,1)S(1)} %get-tuple-element.52.mix, ...), custom_call_target="tpu_custom_call" | custom-call | tf_op jit(solution)/shard_map/convolve/pallas_call | solution.py:302
  19.6 2.1 %collective-permute-start.12 = (bf16[304,128]{1,0:T(8,128)(2,1)S(1)}, bf16[304,128]{1,0:T(8,128)(2,1)S(1)}, u32[]{:S(2)}, u32[]{:S(2)}) collective-permute-start(bf16[304,128]{1,0:T(8,128)(2,1)S(1)} %get-tuple-element.76), channel_id=1, source_target_pairs={{0,14},{1,13},{2,12},{3,15},{4,10},{5,9},{6,8},{7,11},{8,6},{9,5},... | collective-permute-start | bytes 233480 | tf_op jit(solution)/shard_map/ppermute | solution.py:324
  21.7 0.9 %collective-permute-start.13 = (bf16[304,128]{1,0:T(8,128)(2,1)S(1)}, bf16[304,128]{1,0:T(8,128)(2,1)S(1)}, u32[]{:S(2)}, u32[]{:S(2)}) collective-permute-start(bf16[304,128]{1,0:T(8,128)(2,1)S(1)} %get-tuple-element.77), channel_id=1, source_target_pairs={{0,6},{1,5},{2,4},{3,7},{4,2},{5,1},{6,0},{7,3},{8,14},{9,13},{10,... | collective-permute-start | bytes 233480 | tf_op jit(solution)/shard_map/ppermute | solution.py:324
  22.5 2.4 %collective-permute-start.10 = (bf16[304,128]{1,0:T(8,128)(2,1)S(1)}, bf16[304,128]{1,0:T(8,128)(2,1)S(1)}, u32[]{:S(2)}, u32[]{:S(2)}) collective-permute-start(bf16[304,128]{1,0:T(8,128)(2,1)S(1)} %get-tuple-element.74), channel_id=1, source_target_pairs={{0,8},{1,11},{2,10},{3,9},{4,12},{5,15},{6,14},{7,13},{8,0},{9,3},... | collective-permute-start | bytes 233480 | tf_op jit(solution)/shard_map/ppermute | solution.py:324
  24.9 0.7 %collective-permute-start.11 = (bf16[304,128]{1,0:T(8,128)(2,1)S(1)}, bf16[304,128]{1,0:T(8,128)(2,1)S(1)}, u32[]{:S(2)}, u32[]{:S(2)}) collective-permute-start(bf16[304,128]{1,0:T(8,128)(2,1)S(1)} %get-tuple-element.75), channel_id=1, source_target_pairs={{0,0},{1,3},{2,2},{3,1},{4,4},{5,7},{6,6},{7,5},{8,8},{9,11},{10,1... | collective-permute-start | bytes 233480 | tf_op jit(solution)/shard_map/ppermute | solution.py:324
  25.6 2.0 %collective-permute-done.12.refs_0_ = bf16[304,128]{1,0:T(8,128)(2,1)S(1)} collective-permute-done((bf16[304,128]{1,0:T(8,128)(2,1)S(1)}, bf16[304,128]{1,0:T(8,128)(2,1)S(1)}, u32[]{:S(2)}, u32[]{:S(2)}) %collective-permute-start.12) | collective-permute-done | bytes 77856 | tf_op jit(solution)/shard_map/ppermute | solution.py:324
  27.6 0.0 collective-permute-start.16
  27.6 1.3 %collective-permute-done.13.refs_1_ = bf16[304,128]{1,0:T(8,128)(2,1)S(1)} collective-permute-done((bf16[304,128]{1,0:T(8,128)(2,1)S(1)}, bf16[304,128]{1,0:T(8,128)(2,1)S(1)}, u32[]{:S(2)}, u32[]{:S(2)}) %collective-permute-start.13) | collective-permute-done | bytes 77856 | tf_op jit(solution)/shard_map/ppermute | solution.py:324
  29.0 0.0 collective-permute-start.17
  29.0 0.2 collective-permute-done.10.refs_0_
  29.2 0.0 collective-permute-done.11.refs_1_
  29.2 0.4 %collective-permute-start.14 = (bf16[304,128]{1,0:T(8,128)(2,1)S(1)}, bf16[304,128]{1,0:T(8,128)(2,1)S(1)}, u32[]{:S(2)}, u32[]{:S(2)}) collective-permute-start(bf16[304,128]{1,0:T(8,128)(2,1)S(1)} %collective-permute-done.10.refs_0_), channel_id=1, source_target_pairs={{0,1},{1,0},{2,3},{3,2},{4,5},{5,4},{6,7},{7,6},{8,9},{9,8},{10,11... | collective-permute-start | bytes 233480 | tf_op jit(solution)/shard_map/ppermute | solution.py:316
  29.6 0.2 collective-permute-start.15
  29.8 0.0 collective-permute-done.16.refs_2_
  29.8 0.5 %collective-permute-done.17.refs_3_ = bf16[304,128]{1,0:T(8,128)(2,1)S(1)} collective-permute-done((bf16[304,128]{1,0:T(8,128)(2,1)S(1)}, bf16[304,128]{1,0:T(8,128)(2,1)S(1)}, u32[]{:S(2)}, u32[]{:S(2)}) %collective-permute-start.17) | collective-permute-done | bytes 77856 | tf_op jit(solution)/shard_map/ppermute | solution.py:316
  30.3 0.2 collective-permute-done.14.refs_0_
  30.5 0.4 %collective-permute-done.15.refs_1_ = bf16[304,128]{1,0:T(8,128)(2,1)S(1)} collective-permute-done((bf16[304,128]{1,0:T(8,128)(2,1)S(1)}, bf16[304,128]{1,0:T(8,128)(2,1)S(1)}, u32[]{:S(2)}, u32[]{:S(2)}) %collective-permute-start.15) | collective-permute-done | bytes 77856 | tf_op jit(solution)/shard_map/ppermute | solution.py:316
  30.9 1.1 %finish.1 = (bf16[8,64,128]{2,1,0:T(8,128)(2,1)}, bf16[8,64,128]{2,1,0:T(8,128)(2,1)}, f32[9,64]{1,0:T(8,128)}, f32[7,64]{1,0:T(8,128)}, f32[64,64]{1,0:T(8,128)}) custom-call(bf16[8,64,128]{2,1,0:T(8,128)(2,1)S(1)} %get-tuple-element.49.own_f.field, bf16[8,64,128]{2,1,0:T(8,128)(2,1)S(1)} %get-tuple-element.50.own_g.cot, ...), custom_call_target="tpu_custom_call" | custom-call | tf_op jit(solution)/shard_map/finish/pallas_call | solution.py:429
  (2 shorter events, 0.1 us)
Async XLA Ops:
  0.6 1.7 %collective-permute-start = (bf16[8,64,128]{2,1,0:T(8,128)(2,1)}, bf16[8,64,128]{2,1,0:T(8,128)(2,1)S(1)}, u32[]{:S(2)}, u32[]{:S(2)}) collective-permute-start(bf16[8,64,128]{2,1,0:T(8,128)(2,1)} %field.1), channel_id=1, source_target_pairs={{0,1},{1,0},{2,3},{3,2},{4,5},{5,4},{6,7},{7,6},{8,9},{9,8},{10,11... | collective-permute-start | bytes 393224 | tf_op jit(solution)/shard_map/ppermute | solution.py:316
  1.2 1.6 %collective-permute-start.1 = (bf16[8,64,128]{2,1,0:T(8,128)(2,1)}, bf16[8,64,128]{2,1,0:T(8,128)(2,1)S(1)}, u32[]{:S(2)}, u32[]{:S(2)}) collective-permute-start(bf16[8,64,128]{2,1,0:T(8,128)(2,1)} %cot.1), channel_id=1, source_target_pairs={{0,1},{1,0},{2,3},{3,2},{4,5},{5,4},{6,7},{7,6},{8,9},{9,8},{10,11... | collective-permute-start | bytes 393224 | tf_op jit(solution)/shard_map/ppermute | solution.py:316
  2.9 9.2 %collective-permute-start.4 = (bf16[352,128]{1,0:T(8,128)(2,1)S(1)}, bf16[352,128]{1,0:T(8,128)(2,1)S(1)}, u32[]{:S(2)}, u32[]{:S(2)}) collective-permute-start(bf16[352,128]{1,0:T(8,128)(2,1)S(1)} %get-tuple-element.58), channel_id=1, source_target_pairs={{0,14},{1,13},{2,12},{3,15},{4,10},{5,9},{6,8},{7,11},{8,6},{9,5},... | collective-permute-start | bytes 270344 | tf_op jit(solution)/shard_map/ppermute | solution.py:324
  8.7 6.2 %collective-permute-start.5 = (bf16[352,128]{1,0:T(8,128)(2,1)S(1)}, bf16[352,128]{1,0:T(8,128)(2,1)S(1)}, u32[]{:S(2)}, u32[]{:S(2)}) collective-permute-start(bf16[352,128]{1,0:T(8,128)(2,1)S(1)} %get-tuple-element.59), channel_id=1, source_target_pairs={{0,6},{1,5},{2,4},{3,7},{4,2},{5,1},{6,0},{7,3},{8,14},{9,13},{10,... | collective-permute-start | bytes 270344 | tf_op jit(solution)/shard_map/ppermute | solution.py:324
  8.7 7.4 %collective-permute-start.2 = (bf16[352,128]{1,0:T(8,128)(2,1)S(1)}, bf16[352,128]{1,0:T(8,128)(2,1)S(1)}, u32[]{:S(2)}, u32[]{:S(2)}) collective-permute-start(bf16[352,128]{1,0:T(8,128)(2,1)S(1)} %get-tuple-element.56), channel_id=1, source_target_pairs={{0,8},{1,11},{2,10},{3,9},{4,12},{5,15},{6,14},{7,13},{8,0},{9,3},... | collective-permute-start | bytes 270344 | tf_op jit(solution)/shard_map/ppermute | solution.py:324
  9.3 6.8 %collective-permute-start.3 = (bf16[352,128]{1,0:T(8,128)(2,1)S(1)}, bf16[352,128]{1,0:T(8,128)(2,1)S(1)}, u32[]{:S(2)}, u32[]{:S(2)}) collective-permute-start(bf16[352,128]{1,0:T(8,128)(2,1)S(1)} %get-tuple-element.57), channel_id=1, source_target_pairs={{0,0},{1,3},{2,2},{3,1},{4,4},{5,7},{6,6},{7,5},{8,8},{9,11},{10,1... | collective-permute-start | bytes 270344 | tf_op jit(solution)/shard_map/ppermute | solution.py:324
  12.1 4.5 %collective-permute-start.8 = (bf16[352,128]{1,0:T(8,128)(2,1)S(1)}, bf16[352,128]{1,0:T(8,128)(2,1)S(1)}, u32[]{:S(2)}, u32[]{:S(2)}) collective-permute-start(bf16[352,128]{1,0:T(8,128)(2,1)S(1)} %collective-permute-done.4.refs_0_), channel_id=1, source_target_pairs={{0,1},{1,0},{2,3},{3,2},{4,5},{5,4},{6,7},{7,6},{8,9},{9,8},{10,11... | collective-permute-start | bytes 270344 | tf_op jit(solution)/shard_map/ppermute | solution.py:316
  14.9 1.7 %collective-permute-start.9 = (bf16[352,128]{1,0:T(8,128)(2,1)S(1)}, bf16[352,128]{1,0:T(8,128)(2,1)S(1)}, u32[]{:S(2)}, u32[]{:S(2)}) collective-permute-start(bf16[352,128]{1,0:T(8,128)(2,1)S(1)} %collective-permute-done.5.refs_1_), channel_id=1, source_target_pairs={{0,1},{1,0},{2,3},{3,2},{4,5},{5,4},{6,7},{7,6},{8,9},{9,8},{10,11... | collective-permute-start | bytes 270344 | tf_op jit(solution)/shard_map/ppermute | solution.py:316
  16.1 1.3 %collective-permute-start.6 = (bf16[352,128]{1,0:T(8,128)(2,1)S(1)}, bf16[352,128]{1,0:T(8,128)(2,1)S(1)}, u32[]{:S(2)}, u32[]{:S(2)}) collective-permute-start(bf16[352,128]{1,0:T(8,128)(2,1)S(1)} %collective-permute-done.2.refs_0_), channel_id=1, source_target_pairs={{0,1},{1,0},{2,3},{3,2},{4,5},{5,4},{6,7},{7,6},{8,9},{9,8},{10,11... | collective-permute-start | bytes 270344 | tf_op jit(solution)/shard_map/ppermute | solution.py:316
  16.1 1.4 %collective-permute-start.7 = (bf16[352,128]{1,0:T(8,128)(2,1)S(1)}, bf16[352,128]{1,0:T(8,128)(2,1)S(1)}, u32[]{:S(2)}, u32[]{:S(2)}) collective-permute-start(bf16[352,128]{1,0:T(8,128)(2,1)S(1)} %collective-permute-done.3.refs_1_), channel_id=1, source_target_pairs={{0,1},{1,0},{2,3},{3,2},{4,5},{5,4},{6,7},{7,6},{8,9},{9,8},{10,11... | collective-permute-start | bytes 270344 | tf_op jit(solution)/shard_map/ppermute | solution.py:316
  19.6 8.1 %collective-permute-start.12 = (bf16[304,128]{1,0:T(8,128)(2,1)S(1)}, bf16[304,128]{1,0:T(8,128)(2,1)S(1)}, u32[]{:S(2)}, u32[]{:S(2)}) collective-permute-start(bf16[304,128]{1,0:T(8,128)(2,1)S(1)} %get-tuple-element.76), channel_id=1, source_target_pairs={{0,14},{1,13},{2,12},{3,15},{4,10},{5,9},{6,8},{7,11},{8,6},{9,5},... | collective-permute-start | bytes 233480 | tf_op jit(solution)/shard_map/ppermute | solution.py:324
  21.7 7.3 %collective-permute-start.13 = (bf16[304,128]{1,0:T(8,128)(2,1)S(1)}, bf16[304,128]{1,0:T(8,128)(2,1)S(1)}, u32[]{:S(2)}, u32[]{:S(2)}) collective-permute-start(bf16[304,128]{1,0:T(8,128)(2,1)S(1)} %get-tuple-element.77), channel_id=1, source_target_pairs={{0,6},{1,5},{2,4},{3,7},{4,2},{5,1},{6,0},{7,3},{8,14},{9,13},{10,... | collective-permute-start | bytes 233480 | tf_op jit(solution)/shard_map/ppermute | solution.py:324
  22.5 6.7 %collective-permute-start.10 = (bf16[304,128]{1,0:T(8,128)(2,1)S(1)}, bf16[304,128]{1,0:T(8,128)(2,1)S(1)}, u32[]{:S(2)}, u32[]{:S(2)}) collective-permute-start(bf16[304,128]{1,0:T(8,128)(2,1)S(1)} %get-tuple-element.74), channel_id=1, source_target_pairs={{0,8},{1,11},{2,10},{3,9},{4,12},{5,15},{6,14},{7,13},{8,0},{9,3},... | collective-permute-start | bytes 233480 | tf_op jit(solution)/shard_map/ppermute | solution.py:324
  24.9 4.3 %collective-permute-start.11 = (bf16[304,128]{1,0:T(8,128)(2,1)S(1)}, bf16[304,128]{1,0:T(8,128)(2,1)S(1)}, u32[]{:S(2)}, u32[]{:S(2)}) collective-permute-start(bf16[304,128]{1,0:T(8,128)(2,1)S(1)} %get-tuple-element.75), channel_id=1, source_target_pairs={{0,0},{1,3},{2,2},{3,1},{4,4},{5,7},{6,6},{7,5},{8,8},{9,11},{10,1... | collective-permute-start | bytes 233480 | tf_op jit(solution)/shard_map/ppermute | solution.py:324
  27.6 2.1 %collective-permute-start.16 = (bf16[304,128]{1,0:T(8,128)(2,1)S(1)}, bf16[304,128]{1,0:T(8,128)(2,1)S(1)}, u32[]{:S(2)}, u32[]{:S(2)}) collective-permute-start(bf16[304,128]{1,0:T(8,128)(2,1)S(1)} %collective-permute-done.12.refs_0_), channel_id=1, source_target_pairs={{0,1},{1,0},{2,3},{3,2},{4,5},{5,4},{6,7},{7,6},{8,9},{9,8},{10,11... | collective-permute-start | bytes 233480 | tf_op jit(solution)/shard_map/ppermute | solution.py:316
  29.0 1.3 %collective-permute-start.17 = (bf16[304,128]{1,0:T(8,128)(2,1)S(1)}, bf16[304,128]{1,0:T(8,128)(2,1)S(1)}, u32[]{:S(2)}, u32[]{:S(2)}) collective-permute-start(bf16[304,128]{1,0:T(8,128)(2,1)S(1)} %collective-permute-done.13.refs_1_), channel_id=1, source_target_pairs={{0,1},{1,0},{2,3},{3,2},{4,5},{5,4},{6,7},{7,6},{8,9},{9,8},{10,11... | collective-permute-start | bytes 233480 | tf_op jit(solution)/shard_map/ppermute | solution.py:316
  29.2 1.3 %collective-permute-start.14 = (bf16[304,128]{1,0:T(8,128)(2,1)S(1)}, bf16[304,128]{1,0:T(8,128)(2,1)S(1)}, u32[]{:S(2)}, u32[]{:S(2)}) collective-permute-start(bf16[304,128]{1,0:T(8,128)(2,1)S(1)} %collective-permute-done.10.refs_0_), channel_id=1, source_target_pairs={{0,1},{1,0},{2,3},{3,2},{4,5},{5,4},{6,7},{7,6},{8,9},{9,8},{10,11... | collective-permute-start | bytes 233480 | tf_op jit(solution)/shard_map/ppermute | solution.py:316
  29.6 1.3 %collective-permute-start.15 = (bf16[304,128]{1,0:T(8,128)(2,1)S(1)}, bf16[304,128]{1,0:T(8,128)(2,1)S(1)}, u32[]{:S(2)}, u32[]{:S(2)}) collective-permute-start(bf16[304,128]{1,0:T(8,128)(2,1)S(1)} %collective-permute-done.11.refs_1_), channel_id=1, source_target_pairs={{0,1},{1,0},{2,3},{3,2},{4,5},{5,4},{6,7},{7,6},{8,9},{9,8},{10,11... | collective-permute-start | bytes 233480 | tf_op jit(solution)/shard_map/ppermute | solution.py:316

commit v4 on v3

--- a/solution.py
+++ b/solution.py
@@ -83,17 +83,31 @@
         )
 
 
-def partner(rounds, at, side):
-    return 2 * at + (side ^ (at == rounds - 1) ^ (at == 1))
-
-
-def arrivals(rounds):
+def plan(rounds):
     if rounds == 4:
-        return [[(3, 0), (1, 0)], [(2, 0), (0, 0), (3, 1), (1, 1)], [(2, 1), (0, 1)]]
-    return [[(at, swapped) for swapped in range(2) for at in reversed(range(rounds))]]
-
-
-def pack(rounds, own_f, own_g, other_f, other_g, *refs):
+        return ((3, 1, 2, 0), (3,)), ((3, 1, 2, 0), (3, 1))
+    descending = tuple(reversed(range(rounds)))
+    return (descending, ()), (descending, ())
+
+
+def partner(route, at, side):
+    return 2 * at + (side ^ (at in route[1]) if isinstance(at, int) else side)
+
+
+def arrivals(route):
+    order = route[0]
+    if len(order) != 4:
+        return [[(at, swapped) for swapped in range(2) for at in order]]
+    first, second = order[:2], order[2:]
+    return [
+        [(at, 0) for at in first],
+        [(at, 0) for at in second] + [(at, 1) for at in first],
+        [(at, 1) for at in second],
+    ]
+
+
+def pack(route, own_f, own_g, other_f, other_g, *refs):
+    rounds = len(route[0])
     outs, (fields, cots, *stage) = refs[:rounds], refs[rounds:]
     chip, core = place()
     near, rad, feat = own_f.shape
@@ -107,24 +121,43 @@
         cots[pl.ds(side * near, near)] = g[...].astype(F32)
     body = 2 * near * ROWS
 
+    half = feat // 2
+
+    def beside(moved, kept, cell):
+        lane = lax.broadcasted_iota(jnp.int32, moved.shape, 1)
+        return jnp.where((lane < half) == (cell == 1), pltpu.roll(moved, half, 1), kept).astype(BF16)
+
     def fill(i, out):
-        to = chip ^ partner(rounds, i, core)
-        first = pl.multiple_of(to * ROWS, ROWS)
-        center = wide[:, pl.ds(pl.multiple_of(first + ROWS, ROWS), ROWS), :]
-        out[0:body, :] = center.reshape(body, feat).astype(BF16)
-        for h in range(2 * HALO):
-            row = first + ROWS + (h - HALO if h < HALO else ROWS + h - HALO)
+        to = chip ^ partner(route, rounds - 1 - i, core)
+        cell = to % 2
+        first = to // 2 * (2 * ROWS)
+
+        def rows(ref, start, second):
+            start = pl.multiple_of(start + ROWS * second, ROWS)
+            return ref[:, pl.ds(start, ROWS), :].reshape(body, feat)
+
+        def pair(ref, start):
+            return beside(rows(ref, start, 1 - cell), rows(ref, start, cell), cell)
+
+        out[0:body, :] = pair(wide, first + ROWS)
+        for h in range(HALO):
             at = body + h * 2 * near
-            out[at : at + 2 * near, :] = fields[pl.ds(row, 2 * near, stride=step), :].astype(BF16)
-        at = body + 2 * HALO * 2 * near
-        out[at : at + body, :] = cots[:, pl.ds(first, ROWS), :].reshape(body, feat).astype(BF16)
+            above, between = first + ROWS - HALO + h, HALO + 2 * ROWS
+            out[at : at + 2 * near, :] = beside(
+                fields[pl.ds(above + between * (1 - cell), 2 * near, stride=step), :],
+                fields[pl.ds(above + between * cell, 2 * near, stride=step), :],
+                cell,
+            )
+        at = body + HALO * 2 * near
+        out[at : at + body, :] = pair(cots, first)
 
     visit(outs, stage[0] if stage else None, fill, fill=True)
 
 
-def receive(tags, rounds, taps, rtaps, filters, mix, blocks, state, stage):
+def receive(tags, route, taps, rtaps, filters, mix, blocks, state, stage):
     fields, radial, grads, cots = state
     chip, core = place()
+    rounds = len(route[0])
     azim, feat = radial.shape[0] // 2, mix.shape[0]
     step = 2 * ROWS
     wide = fields.reshape(azim, step, feat)
@@ -133,17 +166,23 @@
     weight = [jnp.broadcast_to(filters[taps + j : taps + j + 1, :], (ROWS, feat)) for j in range(rtaps)]
 
     def take(at, side, block):
-        first = (chip ^ partner(rounds, at, side)) * near
+        first = (chip ^ partner(route, at, side)) * near
         wide[pl.ds(first, near), HALO : HALO + ROWS, :] = (
             block[0:body, :].astype(F32).reshape(near, ROWS, feat)
         )
-        for h in range(2 * HALO):
-            row = h if h < HALO else ROWS + h
+        lane = lax.broadcasted_iota(jnp.int32, (near, feat), 1)
+        for h in range(HALO):
             start = body + h * near
-            fields[pl.ds(first * step + row, near, stride=step), :] = block[
-                start : start + near, :
-            ].astype(F32)
-        start = body + 2 * HALO * near
+            edge = block[start : start + near, :].astype(F32)
+
+            def row(r):
+                return pl.ds(first * step + r, near, stride=step)
+
+            lower = pltpu.roll(fields[row(ROWS + h), :], feat // 2, 1)
+            upper = pltpu.roll(fields[row(HALO + h), :], feat // 2, 1)
+            fields[row(h), :] = jnp.where(lane < feat // 2, edge, lower)
+            fields[row(HALO + ROWS + h), :] = jnp.where(lane < feat // 2, upper, edge)
+        start = body + HALO * near
         cot = block[start : start + body, :]
         cots[pl.ds(pl.multiple_of(first * ROWS, body), body), :] = cot
         back = lax.dot_general(cot, mix[...], (((1,), (1,)), ((), ())), preferred_element_type=F32)
@@ -159,18 +198,19 @@
     unpack(tags, blocks, stage[0] if stage else None, core, take)
 
 
-def receive_some(tags, rounds, taps, rtaps, old, filters, mix, *refs):
-    receive(tags, rounds, taps, rtaps, filters, mix, refs[: len(tags)], refs[len(tags) + old :], ())
-
-
-def convolve(tags, rounds, taps, rtaps, channels, old, offsets, filters, mix, *refs):
+def receive_some(tags, route, taps, rtaps, old, filters, mix, *refs):
+    receive(tags, route, taps, rtaps, filters, mix, refs[: len(tags)], refs[len(tags) + old :], ())
+
+
+def convolve(tags, route_in, route, taps, rtaps, channels, old, offsets, filters, mix, *refs):
+    rounds = len(route[0])
     blocks, state = refs[: len(tags)], refs[len(tags) : len(tags) + old]
     outs, rest = refs[len(tags) + old :][:rounds], refs[len(tags) + old + rounds :]
     if not old:
         state, rest = rest[:4], rest[4:]
     hidden, spread, *stage = rest
     fields, radial, grads, cots = state
-    receive(tags, rounds, taps, rtaps, filters, mix, blocks, state, stage)
+    receive(tags, route_in, taps, rtaps, filters, mix, blocks, state, stage)
     chip, core = place()
     azim, feat = radial.shape[0] // 2, mix.shape[0]
     wide = fields.reshape(azim, 2 * ROWS, feat)
@@ -215,28 +255,36 @@
     part = jnp.where(lane < channels, low, high)
     part = jnp.concatenate([part, jnp.zeros((8, feat), F32)], axis=0).astype(BF16)
     for i, out in enumerate(outs):
-        to = chip ^ partner(rounds, i, core)
+        to = chip ^ partner(route, rounds - 1 - i, core)
         rows = pl.ds(pl.multiple_of(to * body, body), body)
         out[0:body, :] = hidden[rows, :]
         out[body : 2 * body, :] = spread[rows, :]
         out[2 * body : 2 * body + part.shape[0], :] = part
 
 
-def collect(tags, rounds, blocks, state, stage):
+def collect(tags, route, blocks, state, stage):
     hidden, spread, summed = state
     chip, core = place()
     near, feat = hidden.shape[0], hidden.shape[2]
     body = near * ROWS
     mine = pl.multiple_of(core * body, body)
 
+    half = feat // 2
+    lane = lax.broadcasted_iota(jnp.int32, (body, feat), 1)
+
+    def put(ref, start, value, cell):
+        start = pl.multiple_of(start, ROWS)
+        old = ref[:, pl.ds(start, ROWS), :].reshape(body, feat)
+        new = jnp.where((lane >= half) == (cell == 1), value, old)
+        ref[:, pl.ds(start, ROWS), :] = new.reshape(near, ROWS, feat)
+
     def take(at, side, block):
-        first = pl.multiple_of((chip ^ partner(rounds, at, side)) * ROWS, ROWS)
-        hidden[:, pl.ds(first, ROWS), :] = (
-            block[pl.ds(mine, body), :].astype(F32).reshape(near, ROWS, feat)
-        )
-        spread[:, pl.ds(pl.multiple_of(first + ROWS, ROWS), ROWS), :] = (
-            block[pl.ds(2 * body + mine, body), :].astype(F32).reshape(near, ROWS, feat)
-        )
+        source = chip ^ partner(route, at, side)
+        first, cell = source // 2 * (2 * ROWS), source % 2
+        for ref, start, edge in ((hidden, mine, 0), (spread, 2 * body + mine, ROWS)):
+            value = block[pl.ds(start, body), :].astype(F32)
+            put(ref, first + edge + ROWS * cell, value, cell)
+            put(ref, first + edge + ROWS * (1 - cell), pltpu.roll(value, half, 1), cell)
         summed[...] += block[4 * body : 4 * body + summed.shape[0], :].astype(F32)
 
     unpack(tags, blocks, stage[0] if stage else None, core, take)
@@ -250,14 +298,14 @@
     summed[...] = jnp.zeros(summed.shape, F32)
 
 
-def collect_some(tags, rounds, old, *refs):
+def collect_some(tags, route, old, *refs):
     state = refs[len(tags) + old :]
     if not old:
         clear(state)
-    collect(tags, rounds, refs[: len(tags)], state, ())
-
-
-def finish(tags, rounds, taps, rtaps, scale, old, field, cot, filters, mix, *refs):
+    collect(tags, route, refs[: len(tags)], state, ())
+
+
+def finish(tags, route, taps, rtaps, scale, old, field, cot, filters, mix, *refs):
     blocks, state = refs[: len(tags)], refs[len(tags) : len(tags) + old]
     targets, rest = refs[len(tags) + old :][:5], refs[len(tags) + old + 5 :]
     if not old:
@@ -265,7 +313,7 @@
         clear(state)
     hidden, spread, summed = state
     out, grad, azimuth_out, radial_out, mixing_out, sems, *stage = rest
-    collect(tags, rounds, blocks, state, stage)
+    collect(tags, route, blocks, state, stage)
     near, rad, feat = field.shape
     channels = azimuth_out.shape[1]
     sources = (out, grad, azimuth_out, radial_out, mixing_out)
@@ -316,13 +364,13 @@
     return lax.ppermute(x, "az", [(i, i ^ 1) for i in range(size)])
 
 
-def exchange(messages, unpacked, empty):
+def exchange(messages, route, unpacked, empty):
     rounds, chips = len(messages), lax.axis_size("az") // 2
     blocks = {}
-    for at in reversed(range(rounds)):
-        pairs = [(2 * c + k, 2 * (c ^ partner(rounds, at, k)) + k) for c in range(chips) for k in range(2)]
-        blocks[at, 0] = lax.ppermute(messages[at], "az", pairs)
-    groups, state = arrivals(rounds), []
+    for at in route[0]:
+        pairs = [(2 * c + k, 2 * (c ^ partner(route, at, k)) + k) for c in range(chips) for k in range(2)]
+        blocks[at, 0] = lax.ppermute(messages[rounds - 1 - at], "az", pairs)
+    groups, state = arrivals(route), []
     for group in groups:
         fresh = [tag for tag in group if not tag[1]]
         if state:
@@ -343,6 +391,7 @@
     azim = near * size
     taps, rtaps, channels = tap_offsets.shape[0], radial_filter.shape[0], mixing.shape[0]
     many = rounds > 8
+    first, second = plan(rounds)
     other_f, other_g = swap(fields), swap(cotangent)
     arguments = (fields, cotangent, azimuth_filter, radial_filter, mixing, tap_offsets)
     kept = [
@@ -370,9 +419,9 @@
         (other_f, other_g, fields, cotangent)
     )
     body = 2 * near * ROWS
-    length = 2 * body + 2 * HALO * 2 * near
+    length = 2 * body + HALO * 2 * near
     messages = call(
-        functools.partial(pack, rounds),
+        functools.partial(pack, first),
         (fields, cotangent, other_f, other_g),
         [((length, feat), BF16)] * rounds,
         [((2 * near * (rad + 2 * ROWS), feat), F32), ((2 * near, rad, feat), F32)]
@@ -382,7 +431,7 @@
 
     def receiver(tags, blocks, state, empty):
         return call(
-            functools.partial(receive_some, tags, rounds, taps, rtaps, len(state)),
+            functools.partial(receive_some, tags, first, taps, rtaps, len(state)),
             (filters, mix, *blocks, *state),
             empty,
             [],
@@ -393,10 +442,10 @@
     flat = ((azim * ROWS, feat), BF16)
     twice = ((2 * azim, ROWS, feat), F32)
     empty = [((azim * 2 * ROWS, feat), F32), twice, twice, flat]
-    tags, blocks, state = exchange(messages, receiver, empty)
+    tags, blocks, state = exchange(messages, first, receiver, empty)
     sums = (taps + rtaps + channels) // 2 + 8
     messages = call(
-        functools.partial(convolve, tags, rounds, taps, rtaps, channels, len(state)),
+        functools.partial(convolve, tags, first, second, taps, rtaps, channels, len(state)),
         (tap_offsets, filters, mix, *blocks, *state),
         [((2 * body + sums, feat), BF16)] * rounds,
         ([] if state else empty)
@@ -407,7 +456,7 @@
 
     def collector(tags, blocks, state, empty):
         return call(
-            functools.partial(collect_some, tags, rounds, len(state)),
+            functools.partial(collect_some, tags, second, len(state)),
             (*blocks, *state),
             empty,
             [],
@@ -416,7 +465,7 @@
         )
 
     empty = [((near, rad, feat), F32), ((near, rad + 2 * ROWS, feat), F32), ((sums, feat), F32)]
-    tags, blocks, state = exchange(messages, collector, empty)
+    tags, blocks, state = exchange(messages, second, collector, empty)
     scale = 1.0 / math.sqrt(azim * rad * (feat // channels))
     ins = (fields, cotangent, filters, mix, *blocks, *state)
     outs = [
@@ -427,7 +476,7 @@
         ((channels, channels), F32),
     ]
     return pl.pallas_call(
-        functools.partial(finish, tags, rounds, taps, rtaps, scale, len(state)),
+        functools.partial(finish, tags, second, taps, rtaps, scale, len(state)),
         in_specs=[VMEM] * len(ins),
         out_specs=[pl.BlockSpec(memory_space=pltpu.HBM)] * len(outs),
         out_shape=[jax.ShapeDtypeStruct(*out) for out in outs],

time: 32.2 us -> 31.6 us (0.981)
  waiting for transfers between devices: 11.5 us -> 9.51 us
  starting transfers between devices: 14.7 us -> 15.6 us
  Pallas kernels: 5.07 us -> 5.55 us
    ppermute x8, waiting for transfers between devices: 9.46 us -> 7.94 us  [exchange(): blocks[at, 0] = lax.ppermute(messages[rounds - 1 - at], 'az', pairs)]
    ppermute x10, starting transfers between devices: 1.63 us -> 2.4 us  [swap(): return lax.ppermute(x, 'az', [(i, i ^ 1) for i in range(size)])]
    ppermute x10, waiting for transfers between devices: 2 us -> 1.58 us  [swap(): return lax.ppermute(x, 'az', [(i, i ^ 1) for i in range(size)])]
    pallas_call x6, Pallas kernels: 2.92 us -> 3.33 us  [call(): pl.pallas_call(kernel, in_specs=[VMEM if x.ndim > 1 else SMEM for x in in...]
  transfers between devices with their start and end apart: 18 -> 18, of which waited for: 12 -> 11; matrix products, arithmetic and copies ran while one was open for 0% -> 0% of each run, Pallas kernels for 5% -> 7%
where the time goes in v4:
time: 31.6 us; the launch traced here: 31.4 us
  starting transfers between devices  15.6 us (49%)
  waiting for transfers between devices  9.51 us (30%)
  Pallas kernels  5.55 us (18%)
  between operations  0.72 us (2%)
    ppermute x8, starting transfers between devices, exchange(): blocks[at, 0] = lax.ppermute(messages[rounds - 1 - at], 'az', pairs)  13.2 us
    ppermute x8, waiting for transfers between devices, exchange(): blocks[at, 0] = lax.ppermute(messages[rounds - 1 - at], 'az', pairs)  7.94 us
    pallas_call x6, Pallas kernels, call(): pl.pallas_call(kernel, in_specs=[VMEM if x.ndim > 1 else SMEM for x in in...  3.33 us
    ppermute x10, starting transfers between devices, swap(): return lax.ppermute(x, 'az', [(i, i ^ 1) for i in range(size)])  2.4 us
    ppermute x10, waiting for transfers between devices, swap(): return lax.ppermute(x, 'az', [(i, i ^ 1) for i in range(size)])  1.58 us
    pallas_call x1, Pallas kernels, local(): pl.pallas_call(functools.partial(finish, tags, second, taps, rtaps, scale...  1.15 us
    pallas_call x1, Pallas kernels, local(): pl.pallas_call(gather, in_specs=[pl.BlockSpec(memory_space=pltpu.HBM)] *...  1.07 us
  transfers between devices with their start and end apart: 18, of which 11 were waited for; matrix products, arithmetic and copies ran while one was open for 0% of the time, Pallas kernels for 7%

profile of v4, /device:TPU:0, one launch (start us, length us, event | category | flops | bytes accessed | tf_op | source)
XLA Modules:
  0.0 31.4 jit_solution(17763675031671307185)
XLA Ops:
  0.6 0.5 %collective-permute-start = (bf16[8,64,128]{2,1,0:T(8,128)(2,1)}, bf16[8,64,128]{2,1,0:T(8,128)(2,1)S(1)}, u32[]{:S(2)}, u32[]{:S(2)}) collective-permute-start(bf16[8,64,128]{2,1,0:T(8,128)(2,1)} %field.1), channel_id=1, source_target_pairs={{0,1},{1,0},{2,3},{3,2},{4,5},{5,4},{6,7},{7,6},{8,9},{9,8},{10,11... | collective-permute-start | bytes 393224 | tf_op jit(solution)/shard_map/ppermute | solution.py:364
  1.2 0.1 collective-permute-start.1
  1.2 1.1 %gather.1 = (bf16[8,64,128]{2,1,0:T(8,128)(2,1)S(1)}, bf16[8,64,128]{2,1,0:T(8,128)(2,1)S(1)}, f32[16,128]{1,0:T(8,128)S(1)}, bf16[128,128]{1,0:T(8,128)(2,1)S(1)}, s32[9]{0:T(128)S(4)}) custom-call(bf16[8,64,128]{2,1,0:T(8,128)(2,1)} %field.1, bf16[8,64,128]{2,1,0:T(8,128)(2,1)} %cot.1, f32[9,64]{1,0:T(8,128)} %azimuth.1, f32[7,64]{1,0:T(8,128)} %radial.1, ...), custom_call_target="tpu_custom_call" | custom-call | tf_op jit(solution)/shard_map/gather/pallas_call | solution.py:404
  2.3 0.0 collective-permute-done.other_f
  2.3 0.4 %collective-permute-done.1.other_g = bf16[8,64,128]{2,1,0:T(8,128)(2,1)S(1)} collective-permute-done((bf16[8,64,128]{2,1,0:T(8,128)(2,1)}, bf16[8,64,128]{2,1,0:T(8,128)(2,1)S(1)}, u32[]{:S(2)}, u32[]{:S(2)}) %collective-permute-start.1) | collective-permute-done | bytes 131104 | tf_op jit(solution)/shard_map/ppermute | solution.py:364
  2.7 0.2 pack.1
  3.0 5.8 %collective-permute-start.4 = (bf16[304,128]{1,0:T(8,128)(2,1)S(1)}, bf16[304,128]{1,0:T(8,128)(2,1)S(1)}, u32[]{:S(2)}, u32[]{:S(2)}) collective-permute-start(bf16[304,128]{1,0:T(8,128)(2,1)S(1)} %get-tuple-element.58), channel_id=1, source_target_pairs={{0,14},{1,13},{2,12},{3,15},{4,10},{5,9},{6,8},{7,11},{8,6},{9,5},... | collective-permute-start | bytes 233480 | tf_op jit(solution)/shard_map/ppermute | solution.py:372
  8.7 0.0 collective-permute-start.5
  8.7 0.8 %collective-permute-start.2 = (bf16[304,128]{1,0:T(8,128)(2,1)S(1)}, bf16[304,128]{1,0:T(8,128)(2,1)S(1)}, u32[]{:S(2)}, u32[]{:S(2)}) collective-permute-start(bf16[304,128]{1,0:T(8,128)(2,1)S(1)} %get-tuple-element.56), channel_id=1, source_target_pairs={{0,8},{1,11},{2,10},{3,9},{4,12},{5,15},{6,14},{7,13},{8,0},{9,3},... | collective-permute-start | bytes 233480 | tf_op jit(solution)/shard_map/ppermute | solution.py:372
  9.5 0.7 %collective-permute-start.3 = (bf16[304,128]{1,0:T(8,128)(2,1)S(1)}, bf16[304,128]{1,0:T(8,128)(2,1)S(1)}, u32[]{:S(2)}, u32[]{:S(2)}) collective-permute-start(bf16[304,128]{1,0:T(8,128)(2,1)S(1)} %get-tuple-element.57), channel_id=1, source_target_pairs={{0,0},{1,3},{2,2},{3,1},{4,4},{5,7},{6,6},{7,5},{8,8},{9,11},{10,1... | collective-permute-start | bytes 233480 | tf_op jit(solution)/shard_map/ppermute | solution.py:372
  10.2 1.7 %collective-permute-done.4.refs_0_ = bf16[304,128]{1,0:T(8,128)(2,1)S(1)} collective-permute-done((bf16[304,128]{1,0:T(8,128)(2,1)S(1)}, bf16[304,128]{1,0:T(8,128)(2,1)S(1)}, u32[]{:S(2)}, u32[]{:S(2)}) %collective-permute-start.4) | collective-permute-done | bytes 77856 | tf_op jit(solution)/shard_map/ppermute | solution.py:372
  11.9 0.4 %collective-permute-start.8 = (bf16[304,128]{1,0:T(8,128)(2,1)S(1)}, bf16[304,128]{1,0:T(8,128)(2,1)S(1)}, u32[]{:S(2)}, u32[]{:S(2)}) collective-permute-start(bf16[304,128]{1,0:T(8,128)(2,1)S(1)} %collective-permute-done.4.refs_0_), channel_id=1, source_target_pairs={{0,1},{1,0},{2,3},{3,2},{4,5},{5,4},{6,7},{7,6},{8,9},{9,8},{10,11... | collective-permute-start | bytes 233480 | tf_op jit(solution)/shard_map/ppermute | solution.py:364
  12.3 2.6 %collective-permute-done.5.refs_1_ = bf16[304,128]{1,0:T(8,128)(2,1)S(1)} collective-permute-done((bf16[304,128]{1,0:T(8,128)(2,1)S(1)}, bf16[304,128]{1,0:T(8,128)(2,1)S(1)}, u32[]{:S(2)}, u32[]{:S(2)}) %collective-permute-start.5) | collective-permute-done | bytes 77856 | tf_op jit(solution)/shard_map/ppermute | solution.py:372
  14.9 0.0 collective-permute-start.9
  14.9 0.3 receive.2
  15.2 0.5 %collective-permute-done.2.refs_0_ = bf16[304,128]{1,0:T(8,128)(2,1)S(1)} collective-permute-done((bf16[304,128]{1,0:T(8,128)(2,1)S(1)}, bf16[304,128]{1,0:T(8,128)(2,1)S(1)}, u32[]{:S(2)}, u32[]{:S(2)}) %collective-permute-start.2) | collective-permute-done | bytes 77856 | tf_op jit(solution)/shard_map/ppermute | solution.py:372
  15.7 0.0 collective-permute-done.3.refs_1_
  15.7 0.1 collective-permute-start.6
  15.8 0.4 %collective-permute-start.7 = (bf16[304,128]{1,0:T(8,128)(2,1)S(1)}, bf16[304,128]{1,0:T(8,128)(2,1)S(1)}, u32[]{:S(2)}, u32[]{:S(2)}) collective-permute-start(bf16[304,128]{1,0:T(8,128)(2,1)S(1)} %collective-permute-done.3.refs_1_), channel_id=1, source_target_pairs={{0,1},{1,0},{2,3},{3,2},{4,5},{5,4},{6,7},{7,6},{8,9},{9,8},{10,11... | collective-permute-start | bytes 233480 | tf_op jit(solution)/shard_map/ppermute | solution.py:364
  16.2 0.0 collective-permute-done.8.refs_2_
  16.2 0.0 collective-permute-done.9.refs_3_
  16.2 0.5 %receive.3 = (f32[2048,128]{1,0:T(8,128)S(1)}, f32[256,8,128]{2,1,0:T(8,128)S(1)}, f32[256,8,128]{2,1,0:T(8,128)S(1)}, bf16[1024,128]{1,0:T(8,128)(2,1)S(1)}) custom-call(f32[16,128]{1,0:T(8,128)S(1)} %get-tuple-element.51.filters, ...), custom_call_target="tpu_custom_call", output_to_operand_aliasing={{0}: (6, {}), {1}: (7, {}), {2}: (8, {}), {3}: (9, {})} | custom-call | tf_op jit(solution)/shard_map/receive/pallas_call | solution.py:350
  16.8 0.2 collective-permute-done.6.refs_0_
  17.0 0.2 collective-permute-done.7.refs_1_
  17.1 2.0 %convolve.1 = (bf16[304,128]{1,0:T(8,128)(2,1)S(1)}, bf16[304,128]{1,0:T(8,128)(2,1)S(1)}, bf16[304,128]{1,0:T(8,128)(2,1)S(1)}, bf16[304,128]{1,0:T(8,128)(2,1)S(1)}) custom-call(s32[9]{0:T(128)S(4)} %get-tuple-element.53.offsets, f32[16,128]{1,0:T(8,128)S(1)} %get-tuple-element.51.filters, bf16[128,128]{1,0:T(8,128)(2,1)S(1)} %get-tuple-element.52.mix, ...), custom_call_target="tpu_custom_call" | custom-call | tf_op jit(solution)/shard_map/convolve/pallas_call | solution.py:350
  19.2 2.8 %collective-permute-start.12 = (bf16[304,128]{1,0:T(8,128)(2,1)S(1)}, bf16[304,128]{1,0:T(8,128)(2,1)S(1)}, u32[]{:S(2)}, u32[]{:S(2)}) collective-permute-start(bf16[304,128]{1,0:T(8,128)(2,1)S(1)} %get-tuple-element.76), channel_id=1, source_target_pairs={{0,14},{1,13},{2,12},{3,15},{4,10},{5,9},{6,8},{7,11},{8,6},{9,5},... | collective-permute-start | bytes 233480 | tf_op jit(solution)/shard_map/ppermute | solution.py:372
  22.0 0.0 collective-permute-start.13
  22.0 2.5 %collective-permute-start.10 = (bf16[304,128]{1,0:T(8,128)(2,1)S(1)}, bf16[304,128]{1,0:T(8,128)(2,1)S(1)}, u32[]{:S(2)}, u32[]{:S(2)}) collective-permute-start(bf16[304,128]{1,0:T(8,128)(2,1)S(1)} %get-tuple-element.74), channel_id=1, source_target_pairs={{0,8},{1,11},{2,10},{3,9},{4,12},{5,15},{6,14},{7,13},{8,0},{9,3},... | collective-permute-start | bytes 233480 | tf_op jit(solution)/shard_map/ppermute | solution.py:372
  24.5 0.7 %collective-permute-start.11 = (bf16[304,128]{1,0:T(8,128)(2,1)S(1)}, bf16[304,128]{1,0:T(8,128)(2,1)S(1)}, u32[]{:S(2)}, u32[]{:S(2)}) collective-permute-start(bf16[304,128]{1,0:T(8,128)(2,1)S(1)} %get-tuple-element.75), channel_id=1, source_target_pairs={{0,0},{1,3},{2,2},{3,1},{4,4},{5,7},{6,6},{7,5},{8,8},{9,11},{10,1... | collective-permute-start | bytes 233480 | tf_op jit(solution)/shard_map/ppermute | solution.py:372
  25.2 1.3 %collective-permute-done.12.refs_0_ = bf16[304,128]{1,0:T(8,128)(2,1)S(1)} collective-permute-done((bf16[304,128]{1,0:T(8,128)(2,1)S(1)}, bf16[304,128]{1,0:T(8,128)(2,1)S(1)}, u32[]{:S(2)}, u32[]{:S(2)}) %collective-permute-start.12) | collective-permute-done | bytes 77856 | tf_op jit(solution)/shard_map/ppermute | solution.py:372
  26.4 0.0 collective-permute-start.16
  26.4 1.8 %collective-permute-done.13.refs_1_ = bf16[304,128]{1,0:T(8,128)(2,1)S(1)} collective-permute-done((bf16[304,128]{1,0:T(8,128)(2,1)S(1)}, bf16[304,128]{1,0:T(8,128)(2,1)S(1)}, u32[]{:S(2)}, u32[]{:S(2)}) %collective-permute-start.13) | collective-permute-done | bytes 77856 | tf_op jit(solution)/shard_map/ppermute | solution.py:372
  28.3 0.3 collective-permute-start.17
  28.6 0.1 collect.2
  28.7 0.0 collective-permute-done.10.refs_0_
  28.7 0.0 collective-permute-done.11.refs_1_
  28.7 0.3 collective-permute-start.14
  29.0 0.3 collective-permute-start.15
  29.3 0.0 collective-permute-done.16.refs_2_
  29.3 0.3 collective-permute-done.17.refs_3_
  29.6 0.2 collect.3
  29.7 0.3 %collective-permute-done.14.refs_0_ = bf16[304,128]{1,0:T(8,128)(2,1)S(1)} collective-permute-done((bf16[304,128]{1,0:T(8,128)(2,1)S(1)}, bf16[304,128]{1,0:T(8,128)(2,1)S(1)}, u32[]{:S(2)}, u32[]{:S(2)}) %collective-permute-start.14) | collective-permute-done | bytes 77856 | tf_op jit(solution)/shard_map/ppermute | solution.py:364
  30.1 0.2 collective-permute-done.15.refs_1_
  30.3 1.2 %finish.1 = (bf16[8,64,128]{2,1,0:T(8,128)(2,1)}, bf16[8,64,128]{2,1,0:T(8,128)(2,1)}, f32[9,64]{1,0:T(8,128)}, f32[7,64]{1,0:T(8,128)}, f32[64,64]{1,0:T(8,128)}) custom-call(bf16[8,64,128]{2,1,0:T(8,128)(2,1)S(1)} %get-tuple-element.49.own_f.field, bf16[8,64,128]{2,1,0:T(8,128)(2,1)S(1)} %get-tuple-element.50.own_g.cot, ...), custom_call_target="tpu_custom_call" | custom-call | tf_op jit(solution)/shard_map/finish/pallas_call | solution.py:478
Async XLA Ops:
  0.6 1.7 %collective-permute-start = (bf16[8,64,128]{2,1,0:T(8,128)(2,1)}, bf16[8,64,128]{2,1,0:T(8,128)(2,1)S(1)}, u32[]{:S(2)}, u32[]{:S(2)}) collective-permute-start(bf16[8,64,128]{2,1,0:T(8,128)(2,1)} %field.1), channel_id=1, source_target_pairs={{0,1},{1,0},{2,3},{3,2},{4,5},{5,4},{6,7},{7,6},{8,9},{9,8},{10,11... | collective-permute-start | bytes 393224 | tf_op jit(solution)/shard_map/ppermute | solution.py:364
  1.2 1.6 %collective-permute-start.1 = (bf16[8,64,128]{2,1,0:T(8,128)(2,1)}, bf16[8,64,128]{2,1,0:T(8,128)(2,1)S(1)}, u32[]{:S(2)}, u32[]{:S(2)}) collective-permute-start(bf16[8,64,128]{2,1,0:T(8,128)(2,1)} %cot.1), channel_id=1, source_target_pairs={{0,1},{1,0},{2,3},{3,2},{4,5},{5,4},{6,7},{7,6},{8,9},{9,8},{10,11... | collective-permute-start | bytes 393224 | tf_op jit(solution)/shard_map/ppermute | solution.py:364
  3.0 8.9 %collective-permute-start.4 = (bf16[304,128]{1,0:T(8,128)(2,1)S(1)}, bf16[304,128]{1,0:T(8,128)(2,1)S(1)}, u32[]{:S(2)}, u32[]{:S(2)}) collective-permute-start(bf16[304,128]{1,0:T(8,128)(2,1)S(1)} %get-tuple-element.58), channel_id=1, source_target_pairs={{0,14},{1,13},{2,12},{3,15},{4,10},{5,9},{6,8},{7,11},{8,6},{9,5},... | collective-permute-start | bytes 233480 | tf_op jit(solution)/shard_map/ppermute | solution.py:372
  8.7 6.2 %collective-permute-start.5 = (bf16[304,128]{1,0:T(8,128)(2,1)S(1)}, bf16[304,128]{1,0:T(8,128)(2,1)S(1)}, u32[]{:S(2)}, u32[]{:S(2)}) collective-permute-start(bf16[304,128]{1,0:T(8,128)(2,1)S(1)} %get-tuple-element.59), channel_id=1, source_target_pairs={{0,4},{1,7},{2,6},{3,5},{4,0},{5,3},{6,2},{7,1},{8,12},{9,15},{10,... | collective-permute-start | bytes 233480 | tf_op jit(solution)/shard_map/ppermute | solution.py:372
  8.7 7.0 %collective-permute-start.2 = (bf16[304,128]{1,0:T(8,128)(2,1)S(1)}, bf16[304,128]{1,0:T(8,128)(2,1)S(1)}, u32[]{:S(2)}, u32[]{:S(2)}) collective-permute-start(bf16[304,128]{1,0:T(8,128)(2,1)S(1)} %get-tuple-element.56), channel_id=1, source_target_pairs={{0,8},{1,11},{2,10},{3,9},{4,12},{5,15},{6,14},{7,13},{8,0},{9,3},... | collective-permute-start | bytes 233480 | tf_op jit(solution)/shard_map/ppermute | solution.py:372
  9.5 6.2 %collective-permute-start.3 = (bf16[304,128]{1,0:T(8,128)(2,1)S(1)}, bf16[304,128]{1,0:T(8,128)(2,1)S(1)}, u32[]{:S(2)}, u32[]{:S(2)}) collective-permute-start(bf16[304,128]{1,0:T(8,128)(2,1)S(1)} %get-tuple-element.57), channel_id=1, source_target_pairs={{0,0},{1,3},{2,2},{3,1},{4,4},{5,7},{6,6},{7,5},{8,8},{9,11},{10,1... | collective-permute-start | bytes 233480 | tf_op jit(solution)/shard_map/ppermute | solution.py:372
  11.9 4.3 %collective-permute-start.8 = (bf16[304,128]{1,0:T(8,128)(2,1)S(1)}, bf16[304,128]{1,0:T(8,128)(2,1)S(1)}, u32[]{:S(2)}, u32[]{:S(2)}) collective-permute-start(bf16[304,128]{1,0:T(8,128)(2,1)S(1)} %collective-permute-done.4.refs_0_), channel_id=1, source_target_pairs={{0,1},{1,0},{2,3},{3,2},{4,5},{5,4},{6,7},{7,6},{8,9},{9,8},{10,11... | collective-permute-start | bytes 233480 | tf_op jit(solution)/shard_map/ppermute | solution.py:364
  14.9 1.3 %collective-permute-start.9 = (bf16[304,128]{1,0:T(8,128)(2,1)S(1)}, bf16[304,128]{1,0:T(8,128)(2,1)S(1)}, u32[]{:S(2)}, u32[]{:S(2)}) collective-permute-start(bf16[304,128]{1,0:T(8,128)(2,1)S(1)} %collective-permute-done.5.refs_1_), channel_id=1, source_target_pairs={{0,1},{1,0},{2,3},{3,2},{4,5},{5,4},{6,7},{7,6},{8,9},{9,8},{10,11... | collective-permute-start | bytes 233480 | tf_op jit(solution)/shard_map/ppermute | solution.py:364
  15.7 1.3 %collective-permute-start.6 = (bf16[304,128]{1,0:T(8,128)(2,1)S(1)}, bf16[304,128]{1,0:T(8,128)(2,1)S(1)}, u32[]{:S(2)}, u32[]{:S(2)}) collective-permute-start(bf16[304,128]{1,0:T(8,128)(2,1)S(1)} %collective-permute-done.2.refs_0_), channel_id=1, source_target_pairs={{0,1},{1,0},{2,3},{3,2},{4,5},{5,4},{6,7},{7,6},{8,9},{9,8},{10,11... | collective-permute-start | bytes 233480 | tf_op jit(solution)/shard_map/ppermute | solution.py:364
  15.8 1.4 %collective-permute-start.7 = (bf16[304,128]{1,0:T(8,128)(2,1)S(1)}, bf16[304,128]{1,0:T(8,128)(2,1)S(1)}, u32[]{:S(2)}, u32[]{:S(2)}) collective-permute-start(bf16[304,128]{1,0:T(8,128)(2,1)S(1)} %collective-permute-done.3.refs_1_), channel_id=1, source_target_pairs={{0,1},{1,0},{2,3},{3,2},{4,5},{5,4},{6,7},{7,6},{8,9},{9,8},{10,11... | collective-permute-start | bytes 233480 | tf_op jit(solution)/shard_map/ppermute | solution.py:364
  19.2 7.3 %collective-permute-start.12 = (bf16[304,128]{1,0:T(8,128)(2,1)S(1)}, bf16[304,128]{1,0:T(8,128)(2,1)S(1)}, u32[]{:S(2)}, u32[]{:S(2)}) collective-permute-start(bf16[304,128]{1,0:T(8,128)(2,1)S(1)} %get-tuple-element.76), channel_id=1, source_target_pairs={{0,14},{1,13},{2,12},{3,15},{4,10},{5,9},{6,8},{7,11},{8,6},{9,5},... | collective-permute-start | bytes 233480 | tf_op jit(solution)/shard_map/ppermute | solution.py:372
  22.0 6.3 %collective-permute-start.13 = (bf16[304,128]{1,0:T(8,128)(2,1)S(1)}, bf16[304,128]{1,0:T(8,128)(2,1)S(1)}, u32[]{:S(2)}, u32[]{:S(2)}) collective-permute-start(bf16[304,128]{1,0:T(8,128)(2,1)S(1)} %get-tuple-element.77), channel_id=1, source_target_pairs={{0,6},{1,5},{2,4},{3,7},{4,2},{5,1},{6,0},{7,3},{8,14},{9,13},{10,... | collective-permute-start | bytes 233480 | tf_op jit(solution)/shard_map/ppermute | solution.py:372
  22.0 6.7 %collective-permute-start.10 = (bf16[304,128]{1,0:T(8,128)(2,1)S(1)}, bf16[304,128]{1,0:T(8,128)(2,1)S(1)}, u32[]{:S(2)}, u32[]{:S(2)}) collective-permute-start(bf16[304,128]{1,0:T(8,128)(2,1)S(1)} %get-tuple-element.74), channel_id=1, source_target_pairs={{0,8},{1,11},{2,10},{3,9},{4,12},{5,15},{6,14},{7,13},{8,0},{9,3},... | collective-permute-start | bytes 233480 | tf_op jit(solution)/shard_map/ppermute | solution.py:372
  24.5 4.2 %collective-permute-start.11 = (bf16[304,128]{1,0:T(8,128)(2,1)S(1)}, bf16[304,128]{1,0:T(8,128)(2,1)S(1)}, u32[]{:S(2)}, u32[]{:S(2)}) collective-permute-start(bf16[304,128]{1,0:T(8,128)(2,1)S(1)} %get-tuple-element.75), channel_id=1, source_target_pairs={{0,0},{1,3},{2,2},{3,1},{4,4},{5,7},{6,6},{7,5},{8,8},{9,11},{10,1... | collective-permute-start | bytes 233480 | tf_op jit(solution)/shard_map/ppermute | solution.py:372
  26.4 2.9 %collective-permute-start.16 = (bf16[304,128]{1,0:T(8,128)(2,1)S(1)}, bf16[304,128]{1,0:T(8,128)(2,1)S(1)}, u32[]{:S(2)}, u32[]{:S(2)}) collective-permute-start(bf16[304,128]{1,0:T(8,128)(2,1)S(1)} %collective-permute-done.12.refs_0_), channel_id=1, source_target_pairs={{0,1},{1,0},{2,3},{3,2},{4,5},{5,4},{6,7},{7,6},{8,9},{9,8},{10,11... | collective-permute-start | bytes 233480 | tf_op jit(solution)/shard_map/ppermute | solution.py:364
  28.3 1.3 %collective-permute-start.17 = (bf16[304,128]{1,0:T(8,128)(2,1)S(1)}, bf16[304,128]{1,0:T(8,128)(2,1)S(1)}, u32[]{:S(2)}, u32[]{:S(2)}) collective-permute-start(bf16[304,128]{1,0:T(8,128)(2,1)S(1)} %collective-permute-done.13.refs_1_), channel_id=1, source_target_pairs={{0,1},{1,0},{2,3},{3,2},{4,5},{5,4},{6,7},{7,6},{8,9},{9,8},{10,11... | collective-permute-start | bytes 233480 | tf_op jit(solution)/shard_map/ppermute | solution.py:364
  28.7 1.3 %collective-permute-start.14 = (bf16[304,128]{1,0:T(8,128)(2,1)S(1)}, bf16[304,128]{1,0:T(8,128)(2,1)S(1)}, u32[]{:S(2)}, u32[]{:S(2)}) collective-permute-start(bf16[304,128]{1,0:T(8,128)(2,1)S(1)} %collective-permute-done.10.refs_0_), channel_id=1, source_target_pairs={{0,1},{1,0},{2,3},{3,2},{4,5},{5,4},{6,7},{7,6},{8,9},{9,8},{10,11... | collective-permute-start | bytes 233480 | tf_op jit(solution)/shard_map/ppermute | solution.py:364
  29.0 1.3 %collective-permute-start.15 = (bf16[304,128]{1,0:T(8,128)(2,1)S(1)}, bf16[304,128]{1,0:T(8,128)(2,1)S(1)}, u32[]{:S(2)}, u32[]{:S(2)}) collective-permute-start(bf16[304,128]{1,0:T(8,128)(2,1)S(1)} %collective-permute-done.11.refs_1_), channel_id=1, source_target_pairs={{0,1},{1,0},{2,3},{3,2},{4,5},{5,4},{6,7},{7,6},{8,9},{9,8},{10,11... | collective-permute-start | bytes 233480 | tf_op jit(solution)/shard_map/ppermute | solution.py:364

commit v5 on v4

--- a/solution.py
+++ b/solution.py
@@ -85,9 +85,9 @@
 
 def plan(rounds):
     if rounds == 4:
-        return ((3, 1, 2, 0), (3,)), ((3, 1, 2, 0), (3, 1))
+        return ((3, 1, 2, 0), (3,), 3), ((3, 1, 2, 0), (3, 1), 2)
     descending = tuple(reversed(range(rounds)))
-    return (descending, ()), (descending, ())
+    return (descending, (), 1), (descending, (), 1)
 
 
 def partner(route, at, side):
@@ -98,12 +98,10 @@
     order = route[0]
     if len(order) != 4:
         return [[(at, swapped) for swapped in range(2) for at in order]]
-    first, second = order[:2], order[2:]
-    return [
-        [(at, 0) for at in first],
-        [(at, 0) for at in second] + [(at, 1) for at in first],
-        [(at, 1) for at in second],
-    ]
+    a, b, c, d = order
+    if route[2] == 2:
+        return [[(a, 0), (b, 0), (a, 1), (c, 0), (d, 0)], [(b, 1), (c, 1), (d, 1)]]
+    return [[(a, 0), (b, 0)], [(c, 0), (d, 0), (a, 1), (b, 1)], [(c, 1), (d, 1)]]
 
 
 def pack(route, own_f, own_g, other_f, other_g, *refs):

time: 31.6 us -> 31.4 us (level)
    pallas_call x6 -> x5, Pallas kernels: 3.33 us -> 3.23 us  [call(): pl.pallas_call(kernel, in_specs=[VMEM if x.ndim > 1 else SMEM for x in in...]
where the time goes in v5:
time: 31.4 us; the launch traced here: 31.2 us
  starting transfers between devices  15.6 us (50%)
  waiting for transfers between devices  9.5 us (30%)
  Pallas kernels  5.47 us (17%)
  between operations  0.7 us (2%)
    ppermute x8, starting transfers between devices, exchange(): blocks[at, 0] = lax.ppermute(messages[rounds - 1 - at], 'az', pairs)  13.2 us
    ppermute x8, waiting for transfers between devices, exchange(): blocks[at, 0] = lax.ppermute(messages[rounds - 1 - at], 'az', pairs)  7.94 us
    pallas_call x5, Pallas kernels, call(): pl.pallas_call(kernel, in_specs=[VMEM if x.ndim > 1 else SMEM for x in in...  3.23 us
    ppermute x10, starting transfers between devices, swap(): return lax.ppermute(x, 'az', [(i, i ^ 1) for i in range(size)])  2.34 us
    ppermute x10, waiting for transfers between devices, swap(): return lax.ppermute(x, 'az', [(i, i ^ 1) for i in range(size)])  1.56 us
    pallas_call x1, Pallas kernels, local(): pl.pallas_call(functools.partial(finish, tags, second, taps, rtaps, scale...  1.17 us
    pallas_call x1, Pallas kernels, local(): pl.pallas_call(gather, in_specs=[pl.BlockSpec(memory_space=pltpu.HBM)] *...  1.07 us
  transfers between devices with their start and end apart: 18, of which 11 were waited for; matrix products, arithmetic and copies ran while one was open for 0% of the time, Pallas kernels for 7%

profile of v5, /device:TPU:0, one launch (start us, length us, event | category | flops | bytes accessed | tf_op | source)
XLA Modules:
  0.0 31.2 jit_solution(9026382536954825803)
XLA Ops:
  0.6 0.5 %collective-permute-start = (bf16[8,64,128]{2,1,0:T(8,128)(2,1)}, bf16[8,64,128]{2,1,0:T(8,128)(2,1)S(1)}, u32[]{:S(2)}, u32[]{:S(2)}) collective-permute-start(bf16[8,64,128]{2,1,0:T(8,128)(2,1)} %field.1), channel_id=1, source_target_pairs={{0,1},{1,0},{2,3},{3,2},{4,5},{5,4},{6,7},{7,6},{8,9},{9,8},{10,11... | collective-permute-start | bytes 393224 | tf_op jit(solution)/shard_map/ppermute | solution.py:362
  1.2 0.1 collective-permute-start.1
  1.2 1.1 %gather.1 = (bf16[8,64,128]{2,1,0:T(8,128)(2,1)S(1)}, bf16[8,64,128]{2,1,0:T(8,128)(2,1)S(1)}, f32[16,128]{1,0:T(8,128)S(1)}, bf16[128,128]{1,0:T(8,128)(2,1)S(1)}, s32[9]{0:T(128)S(4)}) custom-call(bf16[8,64,128]{2,1,0:T(8,128)(2,1)} %field.1, bf16[8,64,128]{2,1,0:T(8,128)(2,1)} %cot.1, f32[9,64]{1,0:T(8,128)} %azimuth.1, f32[7,64]{1,0:T(8,128)} %radial.1, ...), custom_call_target="tpu_custom_call" | custom-call | tf_op jit(solution)/shard_map/gather/pallas_call | solution.py:402
  2.3 0.0 collective-permute-done.other_f
  2.3 0.4 %collective-permute-done.1.other_g = bf16[8,64,128]{2,1,0:T(8,128)(2,1)S(1)} collective-permute-done((bf16[8,64,128]{2,1,0:T(8,128)(2,1)}, bf16[8,64,128]{2,1,0:T(8,128)(2,1)S(1)}, u32[]{:S(2)}, u32[]{:S(2)}) %collective-permute-start.1) | collective-permute-done | bytes 131104 | tf_op jit(solution)/shard_map/ppermute | solution.py:362
  2.7 0.2 pack.1
  3.0 5.8 %collective-permute-start.4 = (bf16[304,128]{1,0:T(8,128)(2,1)S(1)}, bf16[304,128]{1,0:T(8,128)(2,1)S(1)}, u32[]{:S(2)}, u32[]{:S(2)}) collective-permute-start(bf16[304,128]{1,0:T(8,128)(2,1)S(1)} %get-tuple-element.50), channel_id=1, source_target_pairs={{0,14},{1,13},{2,12},{3,15},{4,10},{5,9},{6,8},{7,11},{8,6},{9,5},... | collective-permute-start | bytes 233480 | tf_op jit(solution)/shard_map/ppermute | solution.py:370
  8.7 0.0 collective-permute-start.5
  8.7 0.8 %collective-permute-start.2 = (bf16[304,128]{1,0:T(8,128)(2,1)S(1)}, bf16[304,128]{1,0:T(8,128)(2,1)S(1)}, u32[]{:S(2)}, u32[]{:S(2)}) collective-permute-start(bf16[304,128]{1,0:T(8,128)(2,1)S(1)} %get-tuple-element.48), channel_id=1, source_target_pairs={{0,8},{1,11},{2,10},{3,9},{4,12},{5,15},{6,14},{7,13},{8,0},{9,3},... | collective-permute-start | bytes 233480 | tf_op jit(solution)/shard_map/ppermute | solution.py:370
  9.5 0.7 %collective-permute-start.3 = (bf16[304,128]{1,0:T(8,128)(2,1)S(1)}, bf16[304,128]{1,0:T(8,128)(2,1)S(1)}, u32[]{:S(2)}, u32[]{:S(2)}) collective-permute-start(bf16[304,128]{1,0:T(8,128)(2,1)S(1)} %get-tuple-element.49), channel_id=1, source_target_pairs={{0,0},{1,3},{2,2},{3,1},{4,4},{5,7},{6,6},{7,5},{8,8},{9,11},{10,1... | collective-permute-start | bytes 233480 | tf_op jit(solution)/shard_map/ppermute | solution.py:370
  10.2 1.7 %collective-permute-done.4.refs_0_ = bf16[304,128]{1,0:T(8,128)(2,1)S(1)} collective-permute-done((bf16[304,128]{1,0:T(8,128)(2,1)S(1)}, bf16[304,128]{1,0:T(8,128)(2,1)S(1)}, u32[]{:S(2)}, u32[]{:S(2)}) %collective-permute-start.4) | collective-permute-done | bytes 77856 | tf_op jit(solution)/shard_map/ppermute | solution.py:370
  11.9 0.4 %collective-permute-start.8 = (bf16[304,128]{1,0:T(8,128)(2,1)S(1)}, bf16[304,128]{1,0:T(8,128)(2,1)S(1)}, u32[]{:S(2)}, u32[]{:S(2)}) collective-permute-start(bf16[304,128]{1,0:T(8,128)(2,1)S(1)} %collective-permute-done.4.refs_0_), channel_id=1, source_target_pairs={{0,1},{1,0},{2,3},{3,2},{4,5},{5,4},{6,7},{7,6},{8,9},{9,8},{10,11... | collective-permute-start | bytes 233480 | tf_op jit(solution)/shard_map/ppermute | solution.py:362
  12.3 2.6 %collective-permute-done.5.refs_1_ = bf16[304,128]{1,0:T(8,128)(2,1)S(1)} collective-permute-done((bf16[304,128]{1,0:T(8,128)(2,1)S(1)}, bf16[304,128]{1,0:T(8,128)(2,1)S(1)}, u32[]{:S(2)}, u32[]{:S(2)}) %collective-permute-start.5) | collective-permute-done | bytes 77856 | tf_op jit(solution)/shard_map/ppermute | solution.py:370
  14.9 0.0 collective-permute-start.9
  14.9 0.3 receive.2
  15.2 0.5 %collective-permute-done.2.refs_0_ = bf16[304,128]{1,0:T(8,128)(2,1)S(1)} collective-permute-done((bf16[304,128]{1,0:T(8,128)(2,1)S(1)}, bf16[304,128]{1,0:T(8,128)(2,1)S(1)}, u32[]{:S(2)}, u32[]{:S(2)}) %collective-permute-start.2) | collective-permute-done | bytes 77856 | tf_op jit(solution)/shard_map/ppermute | solution.py:370
  15.7 0.0 collective-permute-done.3.refs_1_
  15.7 0.1 collective-permute-start.6
  15.8 0.4 %collective-permute-start.7 = (bf16[304,128]{1,0:T(8,128)(2,1)S(1)}, bf16[304,128]{1,0:T(8,128)(2,1)S(1)}, u32[]{:S(2)}, u32[]{:S(2)}) collective-permute-start(bf16[304,128]{1,0:T(8,128)(2,1)S(1)} %collective-permute-done.3.refs_1_), channel_id=1, source_target_pairs={{0,1},{1,0},{2,3},{3,2},{4,5},{5,4},{6,7},{7,6},{8,9},{9,8},{10,11... | collective-permute-start | bytes 233480 | tf_op jit(solution)/shard_map/ppermute | solution.py:362
  16.2 0.0 collective-permute-done.8.refs_2_
  16.2 0.0 collective-permute-done.9.refs_3_
  16.2 0.5 %receive.3 = (f32[2048,128]{1,0:T(8,128)S(1)}, f32[256,8,128]{2,1,0:T(8,128)S(1)}, f32[256,8,128]{2,1,0:T(8,128)S(1)}, bf16[1024,128]{1,0:T(8,128)(2,1)S(1)}) custom-call(f32[16,128]{1,0:T(8,128)S(1)} %get-tuple-element.43.filters, ...), custom_call_target="tpu_custom_call", output_to_operand_aliasing={{0}: (6, {}), {1}: (7, {}), {2}: (8, {}), {3}: (9, {})} | custom-call | tf_op jit(solution)/shard_map/receive/pallas_call | solution.py:348
  16.8 0.2 collective-permute-done.6.refs_0_
  17.0 0.2 collective-permute-done.7.refs_1_
  17.1 2.0 %convolve.1 = (bf16[304,128]{1,0:T(8,128)(2,1)S(1)}, bf16[304,128]{1,0:T(8,128)(2,1)S(1)}, bf16[304,128]{1,0:T(8,128)(2,1)S(1)}, bf16[304,128]{1,0:T(8,128)(2,1)S(1)}) custom-call(s32[9]{0:T(128)S(4)} %get-tuple-element.45.offsets, f32[16,128]{1,0:T(8,128)S(1)} %get-tuple-element.43.filters, bf16[128,128]{1,0:T(8,128)(2,1)S(1)} %get-tuple-element.44.mix, ...), custom_call_target="tpu_custom_call" | custom-call | tf_op jit(solution)/shard_map/convolve/pallas_call | solution.py:348
  19.2 2.8 %collective-permute-start.16 = (bf16[304,128]{1,0:T(8,128)(2,1)S(1)}, bf16[304,128]{1,0:T(8,128)(2,1)S(1)}, u32[]{:S(2)}, u32[]{:S(2)}) collective-permute-start(bf16[304,128]{1,0:T(8,128)(2,1)S(1)} %get-tuple-element.69), channel_id=1, source_target_pairs={{0,14},{1,13},{2,12},{3,15},{4,10},{5,9},{6,8},{7,11},{8,6},{9,5},... | collective-permute-start | bytes 233480 | tf_op jit(solution)/shard_map/ppermute | solution.py:370
  22.0 0.0 collective-permute-start.10
  22.0 2.5 %collective-permute-start.12 = (bf16[304,128]{1,0:T(8,128)(2,1)S(1)}, bf16[304,128]{1,0:T(8,128)(2,1)S(1)}, u32[]{:S(2)}, u32[]{:S(2)}) collective-permute-start(bf16[304,128]{1,0:T(8,128)(2,1)S(1)} %get-tuple-element.67), channel_id=1, source_target_pairs={{0,8},{1,11},{2,10},{3,9},{4,12},{5,15},{6,14},{7,13},{8,0},{9,3},... | collective-permute-start | bytes 233480 | tf_op jit(solution)/shard_map/ppermute | solution.py:370
  24.5 0.7 %collective-permute-start.14 = (bf16[304,128]{1,0:T(8,128)(2,1)S(1)}, bf16[304,128]{1,0:T(8,128)(2,1)S(1)}, u32[]{:S(2)}, u32[]{:S(2)}) collective-permute-start(bf16[304,128]{1,0:T(8,128)(2,1)S(1)} %get-tuple-element.68), channel_id=1, source_target_pairs={{0,0},{1,3},{2,2},{3,1},{4,4},{5,7},{6,6},{7,5},{8,8},{9,11},{10,1... | collective-permute-start | bytes 233480 | tf_op jit(solution)/shard_map/ppermute | solution.py:370
  25.2 1.3 %collective-permute-done.16.refs_0_ = bf16[304,128]{1,0:T(8,128)(2,1)S(1)} collective-permute-done((bf16[304,128]{1,0:T(8,128)(2,1)S(1)}, bf16[304,128]{1,0:T(8,128)(2,1)S(1)}, u32[]{:S(2)}, u32[]{:S(2)}) %collective-permute-start.16) | collective-permute-done | bytes 77856 | tf_op jit(solution)/shard_map/ppermute | solution.py:370
  26.4 0.0 collective-permute-start.17
  26.4 1.8 %collective-permute-done.10.refs_1_ = bf16[304,128]{1,0:T(8,128)(2,1)S(1)} collective-permute-done((bf16[304,128]{1,0:T(8,128)(2,1)S(1)}, bf16[304,128]{1,0:T(8,128)(2,1)S(1)}, u32[]{:S(2)}, u32[]{:S(2)}) %collective-permute-start.10) | collective-permute-done | bytes 77856 | tf_op jit(solution)/shard_map/ppermute | solution.py:370
  28.3 0.3 %collective-permute-start.11 = (bf16[304,128]{1,0:T(8,128)(2,1)S(1)}, bf16[304,128]{1,0:T(8,128)(2,1)S(1)}, u32[]{:S(2)}, u32[]{:S(2)}) collective-permute-start(bf16[304,128]{1,0:T(8,128)(2,1)S(1)} %collective-permute-done.10.refs_1_), channel_id=1, source_target_pairs={{0,1},{1,0},{2,3},{3,2},{4,5},{5,4},{6,7},{7,6},{8,9},{9,8},{10,11... | collective-permute-start | bytes 233480 | tf_op jit(solution)/shard_map/ppermute | solution.py:362
  28.6 0.0 collective-permute-done.12.refs_3_
  28.6 0.2 collective-permute-start.13
  28.8 0.0 collective-permute-done.14.refs_4_
  28.8 0.3 %collective-permute-start.15 = (bf16[304,128]{1,0:T(8,128)(2,1)S(1)}, bf16[304,128]{1,0:T(8,128)(2,1)S(1)}, u32[]{:S(2)}, u32[]{:S(2)}) collective-permute-start(bf16[304,128]{1,0:T(8,128)(2,1)S(1)} %collective-permute-done.14.refs_4_), channel_id=1, source_target_pairs={{0,1},{1,0},{2,3},{3,2},{4,5},{5,4},{6,7},{7,6},{8,9},{9,8},{10,11... | collective-permute-start | bytes 233480 | tf_op jit(solution)/shard_map/ppermute | solution.py:362
  29.1 0.0 collective-permute-done.17.refs_2_
  29.1 0.2 collect.1
  29.3 0.3 collective-permute-done.11.refs_0_
  29.5 0.3 %collective-permute-done.13.refs_1_ = bf16[304,128]{1,0:T(8,128)(2,1)S(1)} collective-permute-done((bf16[304,128]{1,0:T(8,128)(2,1)S(1)}, bf16[304,128]{1,0:T(8,128)(2,1)S(1)}, u32[]{:S(2)}, u32[]{:S(2)}) %collective-permute-start.13) | collective-permute-done | bytes 77856 | tf_op jit(solution)/shard_map/ppermute | solution.py:362
  29.9 0.2 collective-permute-done.15.refs_2_
  30.1 1.2 %finish.1 = (bf16[8,64,128]{2,1,0:T(8,128)(2,1)}, bf16[8,64,128]{2,1,0:T(8,128)(2,1)}, f32[9,64]{1,0:T(8,128)}, f32[7,64]{1,0:T(8,128)}, f32[64,64]{1,0:T(8,128)}) custom-call(bf16[8,64,128]{2,1,0:T(8,128)(2,1)S(1)} %get-tuple-element.41.own_f.field, bf16[8,64,128]{2,1,0:T(8,128)(2,1)S(1)} %get-tuple-element.42.own_g.cot, ...), custom_call_target="tpu_custom_call" | custom-call | tf_op jit(solution)/shard_map/finish/pallas_call | solution.py:476
Async XLA Ops:
  0.6 1.7 %collective-permute-start = (bf16[8,64,128]{2,1,0:T(8,128)(2,1)}, bf16[8,64,128]{2,1,0:T(8,128)(2,1)S(1)}, u32[]{:S(2)}, u32[]{:S(2)}) collective-permute-start(bf16[8,64,128]{2,1,0:T(8,128)(2,1)} %field.1), channel_id=1, source_target_pairs={{0,1},{1,0},{2,3},{3,2},{4,5},{5,4},{6,7},{7,6},{8,9},{9,8},{10,11... | collective-permute-start | bytes 393224 | tf_op jit(solution)/shard_map/ppermute | solution.py:362
  1.2 1.6 %collective-permute-start.1 = (bf16[8,64,128]{2,1,0:T(8,128)(2,1)}, bf16[8,64,128]{2,1,0:T(8,128)(2,1)S(1)}, u32[]{:S(2)}, u32[]{:S(2)}) collective-permute-start(bf16[8,64,128]{2,1,0:T(8,128)(2,1)} %cot.1), channel_id=1, source_target_pairs={{0,1},{1,0},{2,3},{3,2},{4,5},{5,4},{6,7},{7,6},{8,9},{9,8},{10,11... | collective-permute-start | bytes 393224 | tf_op jit(solution)/shard_map/ppermute | solution.py:362
  3.0 8.9 %collective-permute-start.4 = (bf16[304,128]{1,0:T(8,128)(2,1)S(1)}, bf16[304,128]{1,0:T(8,128)(2,1)S(1)}, u32[]{:S(2)}, u32[]{:S(2)}) collective-permute-start(bf16[304,128]{1,0:T(8,128)(2,1)S(1)} %get-tuple-element.50), channel_id=1, source_target_pairs={{0,14},{1,13},{2,12},{3,15},{4,10},{5,9},{6,8},{7,11},{8,6},{9,5},... | collective-permute-start | bytes 233480 | tf_op jit(solution)/shard_map/ppermute | solution.py:370
  8.7 6.2 %collective-permute-start.5 = (bf16[304,128]{1,0:T(8,128)(2,1)S(1)}, bf16[304,128]{1,0:T(8,128)(2,1)S(1)}, u32[]{:S(2)}, u32[]{:S(2)}) collective-permute-start(bf16[304,128]{1,0:T(8,128)(2,1)S(1)} %get-tuple-element.51), channel_id=1, source_target_pairs={{0,4},{1,7},{2,6},{3,5},{4,0},{5,3},{6,2},{7,1},{8,12},{9,15},{10,... | collective-permute-start | bytes 233480 | tf_op jit(solution)/shard_map/ppermute | solution.py:370
  8.7 7.0 %collective-permute-start.2 = (bf16[304,128]{1,0:T(8,128)(2,1)S(1)}, bf16[304,128]{1,0:T(8,128)(2,1)S(1)}, u32[]{:S(2)}, u32[]{:S(2)}) collective-permute-start(bf16[304,128]{1,0:T(8,128)(2,1)S(1)} %get-tuple-element.48), channel_id=1, source_target_pairs={{0,8},{1,11},{2,10},{3,9},{4,12},{5,15},{6,14},{7,13},{8,0},{9,3},... | collective-permute-start | bytes 233480 | tf_op jit(solution)/shard_map/ppermute | solution.py:370
  9.5 6.2 %collective-permute-start.3 = (bf16[304,128]{1,0:T(8,128)(2,1)S(1)}, bf16[304,128]{1,0:T(8,128)(2,1)S(1)}, u32[]{:S(2)}, u32[]{:S(2)}) collective-permute-start(bf16[304,128]{1,0:T(8,128)(2,1)S(1)} %get-tuple-element.49), channel_id=1, source_target_pairs={{0,0},{1,3},{2,2},{3,1},{4,4},{5,7},{6,6},{7,5},{8,8},{9,11},{10,1... | collective-permute-start | bytes 233480 | tf_op jit(solution)/shard_map/ppermute | solution.py:370
  11.9 4.3 %collective-permute-start.8 = (bf16[304,128]{1,0:T(8,128)(2,1)S(1)}, bf16[304,128]{1,0:T(8,128)(2,1)S(1)}, u32[]{:S(2)}, u32[]{:S(2)}) collective-permute-start(bf16[304,128]{1,0:T(8,128)(2,1)S(1)} %collective-permute-done.4.refs_0_), channel_id=1, source_target_pairs={{0,1},{1,0},{2,3},{3,2},{4,5},{5,4},{6,7},{7,6},{8,9},{9,8},{10,11... | collective-permute-start | bytes 233480 | tf_op jit(solution)/shard_map/ppermute | solution.py:362
  14.9 1.3 %collective-permute-start.9 = (bf16[304,128]{1,0:T(8,128)(2,1)S(1)}, bf16[304,128]{1,0:T(8,128)(2,1)S(1)}, u32[]{:S(2)}, u32[]{:S(2)}) collective-permute-start(bf16[304,128]{1,0:T(8,128)(2,1)S(1)} %collective-permute-done.5.refs_1_), channel_id=1, source_target_pairs={{0,1},{1,0},{2,3},{3,2},{4,5},{5,4},{6,7},{7,6},{8,9},{9,8},{10,11... | collective-permute-start | bytes 233480 | tf_op jit(solution)/shard_map/ppermute | solution.py:362
  15.7 1.3 %collective-permute-start.6 = (bf16[304,128]{1,0:T(8,128)(2,1)S(1)}, bf16[304,128]{1,0:T(8,128)(2,1)S(1)}, u32[]{:S(2)}, u32[]{:S(2)}) collective-permute-start(bf16[304,128]{1,0:T(8,128)(2,1)S(1)} %collective-permute-done.2.refs_0_), channel_id=1, source_target_pairs={{0,1},{1,0},{2,3},{3,2},{4,5},{5,4},{6,7},{7,6},{8,9},{9,8},{10,11... | collective-permute-start | bytes 233480 | tf_op jit(solution)/shard_map/ppermute | solution.py:362
  15.8 1.4 %collective-permute-start.7 = (bf16[304,128]{1,0:T(8,128)(2,1)S(1)}, bf16[304,128]{1,0:T(8,128)(2,1)S(1)}, u32[]{:S(2)}, u32[]{:S(2)}) collective-permute-start(bf16[304,128]{1,0:T(8,128)(2,1)S(1)} %collective-permute-done.3.refs_1_), channel_id=1, source_target_pairs={{0,1},{1,0},{2,3},{3,2},{4,5},{5,4},{6,7},{7,6},{8,9},{9,8},{10,11... | collective-permute-start | bytes 233480 | tf_op jit(solution)/shard_map/ppermute | solution.py:362
  19.2 7.3 %collective-permute-start.16 = (bf16[304,128]{1,0:T(8,128)(2,1)S(1)}, bf16[304,128]{1,0:T(8,128)(2,1)S(1)}, u32[]{:S(2)}, u32[]{:S(2)}) collective-permute-start(bf16[304,128]{1,0:T(8,128)(2,1)S(1)} %get-tuple-element.69), channel_id=1, source_target_pairs={{0,14},{1,13},{2,12},{3,15},{4,10},{5,9},{6,8},{7,11},{8,6},{9,5},... | collective-permute-start | bytes 233480 | tf_op jit(solution)/shard_map/ppermute | solution.py:370
  22.0 6.3 %collective-permute-start.10 = (bf16[304,128]{1,0:T(8,128)(2,1)S(1)}, bf16[304,128]{1,0:T(8,128)(2,1)S(1)}, u32[]{:S(2)}, u32[]{:S(2)}) collective-permute-start(bf16[304,128]{1,0:T(8,128)(2,1)S(1)} %get-tuple-element.66), channel_id=1, source_target_pairs={{0,6},{1,5},{2,4},{3,7},{4,2},{5,1},{6,0},{7,3},{8,14},{9,13},{10,... | collective-permute-start | bytes 233480 | tf_op jit(solution)/shard_map/ppermute | solution.py:370
  22.0 6.6 %collective-permute-start.12 = (bf16[304,128]{1,0:T(8,128)(2,1)S(1)}, bf16[304,128]{1,0:T(8,128)(2,1)S(1)}, u32[]{:S(2)}, u32[]{:S(2)}) collective-permute-start(bf16[304,128]{1,0:T(8,128)(2,1)S(1)} %get-tuple-element.67), channel_id=1, source_target_pairs={{0,8},{1,11},{2,10},{3,9},{4,12},{5,15},{6,14},{7,13},{8,0},{9,3},... | collective-permute-start | bytes 233480 | tf_op jit(solution)/shard_map/ppermute | solution.py:370
  24.5 4.3 %collective-permute-start.14 = (bf16[304,128]{1,0:T(8,128)(2,1)S(1)}, bf16[304,128]{1,0:T(8,128)(2,1)S(1)}, u32[]{:S(2)}, u32[]{:S(2)}) collective-permute-start(bf16[304,128]{1,0:T(8,128)(2,1)S(1)} %get-tuple-element.68), channel_id=1, source_target_pairs={{0,0},{1,3},{2,2},{3,1},{4,4},{5,7},{6,6},{7,5},{8,8},{9,11},{10,1... | collective-permute-start | bytes 233480 | tf_op jit(solution)/shard_map/ppermute | solution.py:370
  26.4 2.7 %collective-permute-start.17 = (bf16[304,128]{1,0:T(8,128)(2,1)S(1)}, bf16[304,128]{1,0:T(8,128)(2,1)S(1)}, u32[]{:S(2)}, u32[]{:S(2)}) collective-permute-start(bf16[304,128]{1,0:T(8,128)(2,1)S(1)} %collective-permute-done.16.refs_0_), channel_id=1, source_target_pairs={{0,1},{1,0},{2,3},{3,2},{4,5},{5,4},{6,7},{7,6},{8,9},{9,8},{10,11... | collective-permute-start | bytes 233480 | tf_op jit(solution)/shard_map/ppermute | solution.py:362
  28.3 1.3 %collective-permute-start.11 = (bf16[304,128]{1,0:T(8,128)(2,1)S(1)}, bf16[304,128]{1,0:T(8,128)(2,1)S(1)}, u32[]{:S(2)}, u32[]{:S(2)}) collective-permute-start(bf16[304,128]{1,0:T(8,128)(2,1)S(1)} %collective-permute-done.10.refs_1_), channel_id=1, source_target_pairs={{0,1},{1,0},{2,3},{3,2},{4,5},{5,4},{6,7},{7,6},{8,9},{9,8},{10,11... | collective-permute-start | bytes 233480 | tf_op jit(solution)/shard_map/ppermute | solution.py:362
  28.6 1.3 %collective-permute-start.13 = (bf16[304,128]{1,0:T(8,128)(2,1)S(1)}, bf16[304,128]{1,0:T(8,128)(2,1)S(1)}, u32[]{:S(2)}, u32[]{:S(2)}) collective-permute-start(bf16[304,128]{1,0:T(8,128)(2,1)S(1)} %collective-permute-done.12.refs_3_), channel_id=1, source_target_pairs={{0,1},{1,0},{2,3},{3,2},{4,5},{5,4},{6,7},{7,6},{8,9},{9,8},{10,11... | collective-permute-start | bytes 233480 | tf_op jit(solution)/shard_map/ppermute | solution.py:362
  28.8 1.3 %collective-permute-start.15 = (bf16[304,128]{1,0:T(8,128)(2,1)S(1)}, bf16[304,128]{1,0:T(8,128)(2,1)S(1)}, u32[]{:S(2)}, u32[]{:S(2)}) collective-permute-start(bf16[304,128]{1,0:T(8,128)(2,1)S(1)} %collective-permute-done.14.refs_4_), channel_id=1, source_target_pairs={{0,1},{1,0},{2,3},{3,2},{4,5},{5,4},{6,7},{7,6},{8,9},{9,8},{10,11... | collective-permute-start | bytes 233480 | tf_op jit(solution)/shard_map/ppermute | solution.py:362

commit v6 on v5

--- a/solution.py
+++ b/solution.py
@@ -238,7 +238,7 @@
         return tuple(sums)
 
     zero = jnp.zeros((ROWS, feat), F32)
-    sums = lax.fori_loop(0, azim // SLAB, slab, (zero,) * (taps + rtaps), unroll=2)
+    sums = lax.fori_loop(0, azim // SLAB, slab, (zero,) * (taps + rtaps), unroll=4)
     product = lax.dot_general(
         hidden[...], cots[...], (((0,), (0,)), ((), ())), preferred_element_type=F32
     )
@@ -316,15 +316,6 @@
     channels = azimuth_out.shape[1]
     sources = (out, grad, azimuth_out, radial_out, mixing_out)
     copies = [pltpu.make_async_copy(*pair, sems.at[i]) for i, pair in enumerate(zip(sources, targets))]
-    few, half = (taps + rtaps) // 2, channels // 2
-    part = summed[0 : few + half, :] * scale
-    azimuth_out[0:few, :] = part[0:few, 0:channels]
-    azimuth_out[few:taps, :] = part[0 : taps - few, channels:feat]
-    radial_out[...] = part[taps - few : few, channels:feat]
-    mixing_out[0:half, :] = part[few : few + half, 0:channels]
-    mixing_out[half:channels, :] = part[few : few + half, channels:feat]
-    for copy in copies[2:]:
-        copy.start()
     flat = hidden[...].reshape(near * rad, feat).astype(BF16)
     mixed = jnp.dot(flat, mix[...], preferred_element_type=F32).reshape(near, rad, feat)
     out[...] = (field[...].astype(F32) + mixed).astype(BF16)
@@ -337,6 +328,15 @@
     branch = total.astype(BF16).astype(F32)
     grad[...] = (cot[...].astype(F32) + branch).astype(BF16)
     copies[1].start()
+    few, half = (taps + rtaps) // 2, channels // 2
+    part = summed[0 : few + half, :] * scale
+    azimuth_out[0:few, :] = part[0:few, 0:channels]
+    azimuth_out[few:taps, :] = part[0 : taps - few, channels:feat]
+    radial_out[...] = part[taps - few : few, channels:feat]
+    mixing_out[0:half, :] = part[few : few + half, 0:channels]
+    mixing_out[half:channels, :] = part[few : few + half, channels:feat]
+    for copy in copies[2:]:
+        copy.start()
     for copy in copies:
         copy.wait()
 

time: 31.4 us -> 31.3 us (level)
  no operation moved by 1% of the time
where the time goes in v6:
time: 31.3 us; the launch traced here: 31.1 us
  starting transfers between devices  15.6 us (50%)
  waiting for transfers between devices  9.51 us (30%)
  Pallas kernels  5.34 us (17%)
  between operations  0.7 us (2%)
    ppermute x8, starting transfers between devices, exchange(): blocks[at, 0] = lax.ppermute(messages[rounds - 1 - at], 'az', pairs)  13.2 us
    ppermute x8, waiting for transfers between devices, exchange(): blocks[at, 0] = lax.ppermute(messages[rounds - 1 - at], 'az', pairs)  7.94 us
    pallas_call x5, Pallas kernels, call(): pl.pallas_call(kernel, in_specs=[VMEM if x.ndim > 1 else SMEM for x in in...  3.09 us
    ppermute x10, starting transfers between devices, swap(): return lax.ppermute(x, 'az', [(i, i ^ 1) for i in range(size)])  2.33 us
    ppermute x10, waiting for transfers between devices, swap(): return lax.ppermute(x, 'az', [(i, i ^ 1) for i in range(size)])  1.57 us
    pallas_call x1, Pallas kernels, local(): pl.pallas_call(functools.partial(finish, tags, second, taps, rtaps, scale...  1.17 us
    pallas_call x1, Pallas kernels, local(): pl.pallas_call(gather, in_specs=[pl.BlockSpec(memory_space=pltpu.HBM)] *...  1.07 us
  transfers between devices with their start and end apart: 18, of which 11 were waited for; matrix products, arithmetic and copies ran while one was open for 0% of the time, Pallas kernels for 7%

profile of v6, /device:TPU:0, one launch (start us, length us, event | category | flops | bytes accessed | tf_op | source)
XLA Modules:
  0.0 31.1 jit_solution(18157203771915867536)
XLA Ops:
  0.6 0.5 %collective-permute-start = (bf16[8,64,128]{2,1,0:T(8,128)(2,1)}, bf16[8,64,128]{2,1,0:T(8,128)(2,1)S(1)}, u32[]{:S(2)}, u32[]{:S(2)}) collective-permute-start(bf16[8,64,128]{2,1,0:T(8,128)(2,1)} %field.1), channel_id=1, source_target_pairs={{0,1},{1,0},{2,3},{3,2},{4,5},{5,4},{6,7},{7,6},{8,9},{9,8},{10,11... | collective-permute-start | bytes 393224 | tf_op jit(solution)/shard_map/ppermute | solution.py:362
  1.2 0.1 collective-permute-start.1
  1.2 1.1 %gather.1 = (bf16[8,64,128]{2,1,0:T(8,128)(2,1)S(1)}, bf16[8,64,128]{2,1,0:T(8,128)(2,1)S(1)}, f32[16,128]{1,0:T(8,128)S(1)}, bf16[128,128]{1,0:T(8,128)(2,1)S(1)}, s32[9]{0:T(128)S(4)}) custom-call(bf16[8,64,128]{2,1,0:T(8,128)(2,1)} %field.1, bf16[8,64,128]{2,1,0:T(8,128)(2,1)} %cot.1, f32[9,64]{1,0:T(8,128)} %azimuth.1, f32[7,64]{1,0:T(8,128)} %radial.1, ...), custom_call_target="tpu_custom_call" | custom-call | tf_op jit(solution)/shard_map/gather/pallas_call | solution.py:402
  2.3 0.0 collective-permute-done.other_f
  2.3 0.4 %collective-permute-done.1.other_g = bf16[8,64,128]{2,1,0:T(8,128)(2,1)S(1)} collective-permute-done((bf16[8,64,128]{2,1,0:T(8,128)(2,1)}, bf16[8,64,128]{2,1,0:T(8,128)(2,1)S(1)}, u32[]{:S(2)}, u32[]{:S(2)}) %collective-permute-start.1) | collective-permute-done | bytes 131104 | tf_op jit(solution)/shard_map/ppermute | solution.py:362
  2.7 0.2 pack.1
  3.0 5.8 %collective-permute-start.4 = (bf16[304,128]{1,0:T(8,128)(2,1)S(1)}, bf16[304,128]{1,0:T(8,128)(2,1)S(1)}, u32[]{:S(2)}, u32[]{:S(2)}) collective-permute-start(bf16[304,128]{1,0:T(8,128)(2,1)S(1)} %get-tuple-element.50), channel_id=1, source_target_pairs={{0,14},{1,13},{2,12},{3,15},{4,10},{5,9},{6,8},{7,11},{8,6},{9,5},... | collective-permute-start | bytes 233480 | tf_op jit(solution)/shard_map/ppermute | solution.py:370
  8.7 0.0 collective-permute-start.5
  8.7 0.8 %collective-permute-start.2 = (bf16[304,128]{1,0:T(8,128)(2,1)S(1)}, bf16[304,128]{1,0:T(8,128)(2,1)S(1)}, u32[]{:S(2)}, u32[]{:S(2)}) collective-permute-start(bf16[304,128]{1,0:T(8,128)(2,1)S(1)} %get-tuple-element.48), channel_id=1, source_target_pairs={{0,8},{1,11},{2,10},{3,9},{4,12},{5,15},{6,14},{7,13},{8,0},{9,3},... | collective-permute-start | bytes 233480 | tf_op jit(solution)/shard_map/ppermute | solution.py:370
  9.5 0.7 %collective-permute-start.3 = (bf16[304,128]{1,0:T(8,128)(2,1)S(1)}, bf16[304,128]{1,0:T(8,128)(2,1)S(1)}, u32[]{:S(2)}, u32[]{:S(2)}) collective-permute-start(bf16[304,128]{1,0:T(8,128)(2,1)S(1)} %get-tuple-element.49), channel_id=1, source_target_pairs={{0,0},{1,3},{2,2},{3,1},{4,4},{5,7},{6,6},{7,5},{8,8},{9,11},{10,1... | collective-permute-start | bytes 233480 | tf_op jit(solution)/shard_map/ppermute | solution.py:370
  10.2 1.7 %collective-permute-done.4.refs_0_ = bf16[304,128]{1,0:T(8,128)(2,1)S(1)} collective-permute-done((bf16[304,128]{1,0:T(8,128)(2,1)S(1)}, bf16[304,128]{1,0:T(8,128)(2,1)S(1)}, u32[]{:S(2)}, u32[]{:S(2)}) %collective-permute-start.4) | collective-permute-done | bytes 77856 | tf_op jit(solution)/shard_map/ppermute | solution.py:370
  11.9 0.4 %collective-permute-start.8 = (bf16[304,128]{1,0:T(8,128)(2,1)S(1)}, bf16[304,128]{1,0:T(8,128)(2,1)S(1)}, u32[]{:S(2)}, u32[]{:S(2)}) collective-permute-start(bf16[304,128]{1,0:T(8,128)(2,1)S(1)} %collective-permute-done.4.refs_0_), channel_id=1, source_target_pairs={{0,1},{1,0},{2,3},{3,2},{4,5},{5,4},{6,7},{7,6},{8,9},{9,8},{10,11... | collective-permute-start | bytes 233480 | tf_op jit(solution)/shard_map/ppermute | solution.py:362
  12.3 2.6 %collective-permute-done.5.refs_1_ = bf16[304,128]{1,0:T(8,128)(2,1)S(1)} collective-permute-done((bf16[304,128]{1,0:T(8,128)(2,1)S(1)}, bf16[304,128]{1,0:T(8,128)(2,1)S(1)}, u32[]{:S(2)}, u32[]{:S(2)}) %collective-permute-start.5) | collective-permute-done | bytes 77856 | tf_op jit(solution)/shard_map/ppermute | solution.py:370
  14.9 0.0 collective-permute-start.9
  14.9 0.3 receive.2
  15.2 0.5 %collective-permute-done.2.refs_0_ = bf16[304,128]{1,0:T(8,128)(2,1)S(1)} collective-permute-done((bf16[304,128]{1,0:T(8,128)(2,1)S(1)}, bf16[304,128]{1,0:T(8,128)(2,1)S(1)}, u32[]{:S(2)}, u32[]{:S(2)}) %collective-permute-start.2) | collective-permute-done | bytes 77856 | tf_op jit(solution)/shard_map/ppermute | solution.py:370
  15.7 0.0 collective-permute-done.3.refs_1_
  15.7 0.1 collective-permute-start.6
  15.8 0.4 %collective-permute-start.7 = (bf16[304,128]{1,0:T(8,128)(2,1)S(1)}, bf16[304,128]{1,0:T(8,128)(2,1)S(1)}, u32[]{:S(2)}, u32[]{:S(2)}) collective-permute-start(bf16[304,128]{1,0:T(8,128)(2,1)S(1)} %collective-permute-done.3.refs_1_), channel_id=1, source_target_pairs={{0,1},{1,0},{2,3},{3,2},{4,5},{5,4},{6,7},{7,6},{8,9},{9,8},{10,11... | collective-permute-start | bytes 233480 | tf_op jit(solution)/shard_map/ppermute | solution.py:362
  16.2 0.0 collective-permute-done.8.refs_2_
  16.2 0.0 collective-permute-done.9.refs_3_
  16.2 0.5 %receive.3 = (f32[2048,128]{1,0:T(8,128)S(1)}, f32[256,8,128]{2,1,0:T(8,128)S(1)}, f32[256,8,128]{2,1,0:T(8,128)S(1)}, bf16[1024,128]{1,0:T(8,128)(2,1)S(1)}) custom-call(f32[16,128]{1,0:T(8,128)S(1)} %get-tuple-element.43.filters, ...), custom_call_target="tpu_custom_call", output_to_operand_aliasing={{0}: (6, {}), {1}: (7, {}), {2}: (8, {}), {3}: (9, {})} | custom-call | tf_op jit(solution)/shard_map/receive/pallas_call | solution.py:348
  16.8 0.2 collective-permute-done.6.refs_0_
  17.0 0.2 collective-permute-done.7.refs_1_
  17.1 1.9 %convolve.1 = (bf16[304,128]{1,0:T(8,128)(2,1)S(1)}, bf16[304,128]{1,0:T(8,128)(2,1)S(1)}, bf16[304,128]{1,0:T(8,128)(2,1)S(1)}, bf16[304,128]{1,0:T(8,128)(2,1)S(1)}) custom-call(s32[9]{0:T(128)S(4)} %get-tuple-element.45.offsets, f32[16,128]{1,0:T(8,128)S(1)} %get-tuple-element.43.filters, bf16[128,128]{1,0:T(8,128)(2,1)S(1)} %get-tuple-element.44.mix, ...), custom_call_target="tpu_custom_call" | custom-call | tf_op jit(solution)/shard_map/convolve/pallas_call | solution.py:348
  19.0 2.8 %collective-permute-start.16 = (bf16[304,128]{1,0:T(8,128)(2,1)S(1)}, bf16[304,128]{1,0:T(8,128)(2,1)S(1)}, u32[]{:S(2)}, u32[]{:S(2)}) collective-permute-start(bf16[304,128]{1,0:T(8,128)(2,1)S(1)} %get-tuple-element.69), channel_id=1, source_target_pairs={{0,14},{1,13},{2,12},{3,15},{4,10},{5,9},{6,8},{7,11},{8,6},{9,5},... | collective-permute-start | bytes 233480 | tf_op jit(solution)/shard_map/ppermute | solution.py:370
  21.9 0.0 collective-permute-start.10
  21.9 2.5 %collective-permute-start.12 = (bf16[304,128]{1,0:T(8,128)(2,1)S(1)}, bf16[304,128]{1,0:T(8,128)(2,1)S(1)}, u32[]{:S(2)}, u32[]{:S(2)}) collective-permute-start(bf16[304,128]{1,0:T(8,128)(2,1)S(1)} %get-tuple-element.67), channel_id=1, source_target_pairs={{0,8},{1,11},{2,10},{3,9},{4,12},{5,15},{6,14},{7,13},{8,0},{9,3},... | collective-permute-start | bytes 233480 | tf_op jit(solution)/shard_map/ppermute | solution.py:370
  24.4 0.7 %collective-permute-start.14 = (bf16[304,128]{1,0:T(8,128)(2,1)S(1)}, bf16[304,128]{1,0:T(8,128)(2,1)S(1)}, u32[]{:S(2)}, u32[]{:S(2)}) collective-permute-start(bf16[304,128]{1,0:T(8,128)(2,1)S(1)} %get-tuple-element.68), channel_id=1, source_target_pairs={{0,0},{1,3},{2,2},{3,1},{4,4},{5,7},{6,6},{7,5},{8,8},{9,11},{10,1... | collective-permute-start | bytes 233480 | tf_op jit(solution)/shard_map/ppermute | solution.py:370
  25.0 1.2 %collective-permute-done.16.refs_0_ = bf16[304,128]{1,0:T(8,128)(2,1)S(1)} collective-permute-done((bf16[304,128]{1,0:T(8,128)(2,1)S(1)}, bf16[304,128]{1,0:T(8,128)(2,1)S(1)}, u32[]{:S(2)}, u32[]{:S(2)}) %collective-permute-start.16) | collective-permute-done | bytes 77856 | tf_op jit(solution)/shard_map/ppermute | solution.py:370
  26.3 0.0 collective-permute-start.17
  26.3 1.8 %collective-permute-done.10.refs_1_ = bf16[304,128]{1,0:T(8,128)(2,1)S(1)} collective-permute-done((bf16[304,128]{1,0:T(8,128)(2,1)S(1)}, bf16[304,128]{1,0:T(8,128)(2,1)S(1)}, u32[]{:S(2)}, u32[]{:S(2)}) %collective-permute-start.10) | collective-permute-done | bytes 77856 | tf_op jit(solution)/shard_map/ppermute | solution.py:370
  28.1 0.3 %collective-permute-start.11 = (bf16[304,128]{1,0:T(8,128)(2,1)S(1)}, bf16[304,128]{1,0:T(8,128)(2,1)S(1)}, u32[]{:S(2)}, u32[]{:S(2)}) collective-permute-start(bf16[304,128]{1,0:T(8,128)(2,1)S(1)} %collective-permute-done.10.refs_1_), channel_id=1, source_target_pairs={{0,1},{1,0},{2,3},{3,2},{4,5},{5,4},{6,7},{7,6},{8,9},{9,8},{10,11... | collective-permute-start | bytes 233480 | tf_op jit(solution)/shard_map/ppermute | solution.py:362
  28.5 0.0 collective-permute-done.12.refs_3_
  28.5 0.2 collective-permute-start.13
  28.7 0.0 collective-permute-done.14.refs_4_
  28.7 0.3 %collective-permute-start.15 = (bf16[304,128]{1,0:T(8,128)(2,1)S(1)}, bf16[304,128]{1,0:T(8,128)(2,1)S(1)}, u32[]{:S(2)}, u32[]{:S(2)}) collective-permute-start(bf16[304,128]{1,0:T(8,128)(2,1)S(1)} %collective-permute-done.14.refs_4_), channel_id=1, source_target_pairs={{0,1},{1,0},{2,3},{3,2},{4,5},{5,4},{6,7},{7,6},{8,9},{9,8},{10,11... | collective-permute-start | bytes 233480 | tf_op jit(solution)/shard_map/ppermute | solution.py:362
  29.0 0.0 collective-permute-done.17.refs_2_
  29.0 0.2 collect.1
  29.2 0.3 collective-permute-done.11.refs_0_
  29.4 0.3 %collective-permute-done.13.refs_1_ = bf16[304,128]{1,0:T(8,128)(2,1)S(1)} collective-permute-done((bf16[304,128]{1,0:T(8,128)(2,1)S(1)}, bf16[304,128]{1,0:T(8,128)(2,1)S(1)}, u32[]{:S(2)}, u32[]{:S(2)}) %collective-permute-start.13) | collective-permute-done | bytes 77856 | tf_op jit(solution)/shard_map/ppermute | solution.py:362
  29.7 0.2 collective-permute-done.15.refs_2_
  29.9 1.2 %finish.1 = (bf16[8,64,128]{2,1,0:T(8,128)(2,1)}, bf16[8,64,128]{2,1,0:T(8,128)(2,1)}, f32[9,64]{1,0:T(8,128)}, f32[7,64]{1,0:T(8,128)}, f32[64,64]{1,0:T(8,128)}) custom-call(bf16[8,64,128]{2,1,0:T(8,128)(2,1)S(1)} %get-tuple-element.41.own_f.field, bf16[8,64,128]{2,1,0:T(8,128)(2,1)S(1)} %get-tuple-element.42.own_g.cot, ...), custom_call_target="tpu_custom_call" | custom-call | tf_op jit(solution)/shard_map/finish/pallas_call | solution.py:476
Async XLA Ops:
  0.6 1.7 %collective-permute-start = (bf16[8,64,128]{2,1,0:T(8,128)(2,1)}, bf16[8,64,128]{2,1,0:T(8,128)(2,1)S(1)}, u32[]{:S(2)}, u32[]{:S(2)}) collective-permute-start(bf16[8,64,128]{2,1,0:T(8,128)(2,1)} %field.1), channel_id=1, source_target_pairs={{0,1},{1,0},{2,3},{3,2},{4,5},{5,4},{6,7},{7,6},{8,9},{9,8},{10,11... | collective-permute-start | bytes 393224 | tf_op jit(solution)/shard_map/ppermute | solution.py:362
  1.2 1.6 %collective-permute-start.1 = (bf16[8,64,128]{2,1,0:T(8,128)(2,1)}, bf16[8,64,128]{2,1,0:T(8,128)(2,1)S(1)}, u32[]{:S(2)}, u32[]{:S(2)}) collective-permute-start(bf16[8,64,128]{2,1,0:T(8,128)(2,1)} %cot.1), channel_id=1, source_target_pairs={{0,1},{1,0},{2,3},{3,2},{4,5},{5,4},{6,7},{7,6},{8,9},{9,8},{10,11... | collective-permute-start | bytes 393224 | tf_op jit(solution)/shard_map/ppermute | solution.py:362
  3.0 8.9 %collective-permute-start.4 = (bf16[304,128]{1,0:T(8,128)(2,1)S(1)}, bf16[304,128]{1,0:T(8,128)(2,1)S(1)}, u32[]{:S(2)}, u32[]{:S(2)}) collective-permute-start(bf16[304,128]{1,0:T(8,128)(2,1)S(1)} %get-tuple-element.50), channel_id=1, source_target_pairs={{0,14},{1,13},{2,12},{3,15},{4,10},{5,9},{6,8},{7,11},{8,6},{9,5},... | collective-permute-start | bytes 233480 | tf_op jit(solution)/shard_map/ppermute | solution.py:370
  8.7 6.2 %collective-permute-start.5 = (bf16[304,128]{1,0:T(8,128)(2,1)S(1)}, bf16[304,128]{1,0:T(8,128)(2,1)S(1)}, u32[]{:S(2)}, u32[]{:S(2)}) collective-permute-start(bf16[304,128]{1,0:T(8,128)(2,1)S(1)} %get-tuple-element.51), channel_id=1, source_target_pairs={{0,4},{1,7},{2,6},{3,5},{4,0},{5,3},{6,2},{7,1},{8,12},{9,15},{10,... | collective-permute-start | bytes 233480 | tf_op jit(solution)/shard_map/ppermute | solution.py:370
  8.7 7.0 %collective-permute-start.2 = (bf16[304,128]{1,0:T(8,128)(2,1)S(1)}, bf16[304,128]{1,0:T(8,128)(2,1)S(1)}, u32[]{:S(2)}, u32[]{:S(2)}) collective-permute-start(bf16[304,128]{1,0:T(8,128)(2,1)S(1)} %get-tuple-element.48), channel_id=1, source_target_pairs={{0,8},{1,11},{2,10},{3,9},{4,12},{5,15},{6,14},{7,13},{8,0},{9,3},... | collective-permute-start | bytes 233480 | tf_op jit(solution)/shard_map/ppermute | solution.py:370
  9.5 6.2 %collective-permute-start.3 = (bf16[304,128]{1,0:T(8,128)(2,1)S(1)}, bf16[304,128]{1,0:T(8,128)(2,1)S(1)}, u32[]{:S(2)}, u32[]{:S(2)}) collective-permute-start(bf16[304,128]{1,0:T(8,128)(2,1)S(1)} %get-tuple-element.49), channel_id=1, source_target_pairs={{0,0},{1,3},{2,2},{3,1},{4,4},{5,7},{6,6},{7,5},{8,8},{9,11},{10,1... | collective-permute-start | bytes 233480 | tf_op jit(solution)/shard_map/ppermute | solution.py:370
  11.9 4.3 %collective-permute-start.8 = (bf16[304,128]{1,0:T(8,128)(2,1)S(1)}, bf16[304,128]{1,0:T(8,128)(2,1)S(1)}, u32[]{:S(2)}, u32[]{:S(2)}) collective-permute-start(bf16[304,128]{1,0:T(8,128)(2,1)S(1)} %collective-permute-done.4.refs_0_), channel_id=1, source_target_pairs={{0,1},{1,0},{2,3},{3,2},{4,5},{5,4},{6,7},{7,6},{8,9},{9,8},{10,11... | collective-permute-start | bytes 233480 | tf_op jit(solution)/shard_map/ppermute | solution.py:362
  14.9 1.3 %collective-permute-start.9 = (bf16[304,128]{1,0:T(8,128)(2,1)S(1)}, bf16[304,128]{1,0:T(8,128)(2,1)S(1)}, u32[]{:S(2)}, u32[]{:S(2)}) collective-permute-start(bf16[304,128]{1,0:T(8,128)(2,1)S(1)} %collective-permute-done.5.refs_1_), channel_id=1, source_target_pairs={{0,1},{1,0},{2,3},{3,2},{4,5},{5,4},{6,7},{7,6},{8,9},{9,8},{10,11... | collective-permute-start | bytes 233480 | tf_op jit(solution)/shard_map/ppermute | solution.py:362
  15.7 1.3 %collective-permute-start.6 = (bf16[304,128]{1,0:T(8,128)(2,1)S(1)}, bf16[304,128]{1,0:T(8,128)(2,1)S(1)}, u32[]{:S(2)}, u32[]{:S(2)}) collective-permute-start(bf16[304,128]{1,0:T(8,128)(2,1)S(1)} %collective-permute-done.2.refs_0_), channel_id=1, source_target_pairs={{0,1},{1,0},{2,3},{3,2},{4,5},{5,4},{6,7},{7,6},{8,9},{9,8},{10,11... | collective-permute-start | bytes 233480 | tf_op jit(solution)/shard_map/ppermute | solution.py:362
  15.8 1.4 %collective-permute-start.7 = (bf16[304,128]{1,0:T(8,128)(2,1)S(1)}, bf16[304,128]{1,0:T(8,128)(2,1)S(1)}, u32[]{:S(2)}, u32[]{:S(2)}) collective-permute-start(bf16[304,128]{1,0:T(8,128)(2,1)S(1)} %collective-permute-done.3.refs_1_), channel_id=1, source_target_pairs={{0,1},{1,0},{2,3},{3,2},{4,5},{5,4},{6,7},{7,6},{8,9},{9,8},{10,11... | collective-permute-start | bytes 233480 | tf_op jit(solution)/shard_map/ppermute | solution.py:362
  19.0 7.3 %collective-permute-start.16 = (bf16[304,128]{1,0:T(8,128)(2,1)S(1)}, bf16[304,128]{1,0:T(8,128)(2,1)S(1)}, u32[]{:S(2)}, u32[]{:S(2)}) collective-permute-start(bf16[304,128]{1,0:T(8,128)(2,1)S(1)} %get-tuple-element.69), channel_id=1, source_target_pairs={{0,14},{1,13},{2,12},{3,15},{4,10},{5,9},{6,8},{7,11},{8,6},{9,5},... | collective-permute-start | bytes 233480 | tf_op jit(solution)/shard_map/ppermute | solution.py:370
  21.9 6.3 %collective-permute-start.10 = (bf16[304,128]{1,0:T(8,128)(2,1)S(1)}, bf16[304,128]{1,0:T(8,128)(2,1)S(1)}, u32[]{:S(2)}, u32[]{:S(2)}) collective-permute-start(bf16[304,128]{1,0:T(8,128)(2,1)S(1)} %get-tuple-element.66), channel_id=1, source_target_pairs={{0,6},{1,5},{2,4},{3,7},{4,2},{5,1},{6,0},{7,3},{8,14},{9,13},{10,... | collective-permute-start | bytes 233480 | tf_op jit(solution)/shard_map/ppermute | solution.py:370
  21.9 6.6 %collective-permute-start.12 = (bf16[304,128]{1,0:T(8,128)(2,1)S(1)}, bf16[304,128]{1,0:T(8,128)(2,1)S(1)}, u32[]{:S(2)}, u32[]{:S(2)}) collective-permute-start(bf16[304,128]{1,0:T(8,128)(2,1)S(1)} %get-tuple-element.67), channel_id=1, source_target_pairs={{0,8},{1,11},{2,10},{3,9},{4,12},{5,15},{6,14},{7,13},{8,0},{9,3},... | collective-permute-start | bytes 233480 | tf_op jit(solution)/shard_map/ppermute | solution.py:370
  24.4 4.3 %collective-permute-start.14 = (bf16[304,128]{1,0:T(8,128)(2,1)S(1)}, bf16[304,128]{1,0:T(8,128)(2,1)S(1)}, u32[]{:S(2)}, u32[]{:S(2)}) collective-permute-start(bf16[304,128]{1,0:T(8,128)(2,1)S(1)} %get-tuple-element.68), channel_id=1, source_target_pairs={{0,0},{1,3},{2,2},{3,1},{4,4},{5,7},{6,6},{7,5},{8,8},{9,11},{10,1... | collective-permute-start | bytes 233480 | tf_op jit(solution)/shard_map/ppermute | solution.py:370
  26.3 2.7 %collective-permute-start.17 = (bf16[304,128]{1,0:T(8,128)(2,1)S(1)}, bf16[304,128]{1,0:T(8,128)(2,1)S(1)}, u32[]{:S(2)}, u32[]{:S(2)}) collective-permute-start(bf16[304,128]{1,0:T(8,128)(2,1)S(1)} %collective-permute-done.16.refs_0_), channel_id=1, source_target_pairs={{0,1},{1,0},{2,3},{3,2},{4,5},{5,4},{6,7},{7,6},{8,9},{9,8},{10,11... | collective-permute-start | bytes 233480 | tf_op jit(solution)/shard_map/ppermute | solution.py:362
  28.1 1.3 %collective-permute-start.11 = (bf16[304,128]{1,0:T(8,128)(2,1)S(1)}, bf16[304,128]{1,0:T(8,128)(2,1)S(1)}, u32[]{:S(2)}, u32[]{:S(2)}) collective-permute-start(bf16[304,128]{1,0:T(8,128)(2,1)S(1)} %collective-permute-done.10.refs_1_), channel_id=1, source_target_pairs={{0,1},{1,0},{2,3},{3,2},{4,5},{5,4},{6,7},{7,6},{8,9},{9,8},{10,11... | collective-permute-start | bytes 233480 | tf_op jit(solution)/shard_map/ppermute | solution.py:362
  28.5 1.3 %collective-permute-start.13 = (bf16[304,128]{1,0:T(8,128)(2,1)S(1)}, bf16[304,128]{1,0:T(8,128)(2,1)S(1)}, u32[]{:S(2)}, u32[]{:S(2)}) collective-permute-start(bf16[304,128]{1,0:T(8,128)(2,1)S(1)} %collective-permute-done.12.refs_3_), channel_id=1, source_target_pairs={{0,1},{1,0},{2,3},{3,2},{4,5},{5,4},{6,7},{7,6},{8,9},{9,8},{10,11... | collective-permute-start | bytes 233480 | tf_op jit(solution)/shard_map/ppermute | solution.py:362
  28.7 1.3 %collective-permute-start.15 = (bf16[304,128]{1,0:T(8,128)(2,1)S(1)}, bf16[304,128]{1,0:T(8,128)(2,1)S(1)}, u32[]{:S(2)}, u32[]{:S(2)}) collective-permute-start(bf16[304,128]{1,0:T(8,128)(2,1)S(1)} %collective-permute-done.14.refs_4_), channel_id=1, source_target_pairs={{0,1},{1,0},{2,3},{3,2},{4,5},{5,4},{6,7},{7,6},{8,9},{9,8},{10,11... | collective-permute-start | bytes 233480 | tf_op jit(solution)/shard_map/ppermute | solution.py:362
